TPU v7x, 768 devices: a whole 4x8x12 slice. The times are simulated.
768 devices in a mesh: mesh: 48 (over z, y_lo, core), state: 16 (over x, y_hi).
Axes of the slice: x: 4, y: 8 (y_hi: 4, y_lo: 2; y = y_hi * 2 + y_lo), z: 12, core: 2. Of those that a mesh axis runs over, the one named last changes fastest.
Arguments:
- states: bfloat16 [49152, 3072], P('mesh', 'state'), may hold values from -6 to 6
- cell_ham: bfloat16 [96, 512, 512], P('mesh'), may hold values from -0.25 to 0.25
- projectors: bfloat16 [96, 72, 512], P('mesh'), may hold values from -0.15625 to 0.15625
- slot_atom: int32 [96, 4], P('mesh'), may hold values from 0 to 47, as said below
- coupling: float32 [48, 18], replicated, may hold values from 0.3 to 0.5
- occupancy: float32 [3072], P('state'), may hold values from 0.2 to 2
Outputs:
- filtered: bfloat16 [49152, 3072], P('mesh', 'state')
- density: float32 [49152], P(('mesh', 'state'))
Inputs may be any that keep to these rules, and one draw needn't show every extreme that they name: `slot_atom`: atom a is owned by partition a; cells k * 2 to (k + 1) * 2 - 1 form partition k. Slot 0 of every cell names an atom of the cell's own partition; other slots may name an atom of any partition.
All inputs are finite; a program needn't handle non-finite values.
Results may differ from a plain program's by a relative error of at most 0.006.
Values may be sent and summed in bfloat16 or wider, within the bound.
No kernel may reach another device: no remote copies, remote signals or barrier semaphores. Data moves between devices by JAX's collectives and lax.ppermute only.
A program may use at most 32 MiB of HBM per device.

v0:
```python
import jax
import jax.numpy as jnp
from jax import lax
from jax.sharding import PartitionSpec as P

FACE = 64
DEGREE = 4


def extended(cells, sides, width):
    for axis, dim in sides:
        count = lax.axis_size(axis)
        ends = count - 1
        head = lax.slice_in_dim(cells, 0, width, axis=dim)
        tail = lax.slice_in_dim(cells, cells.shape[dim] - width, cells.shape[dim], axis=dim)
        cells = jnp.concatenate(
            [
                lax.ppermute(tail, axis, [(i, (i + 1) % count) for i in range(ends)]),
                cells,
                lax.ppermute(head, axis, [((i + 1) % count, i) for i in range(ends)]),
            ],
            axis=dim,
        )
    return cells


def shards(states, cell_ham, projectors, slot_atom, coupling, occupancy):
    cells = cell_ham.shape[0]
    nodes = cell_ham.shape[1]
    width = states.shape[1]
    slots = slot_atom.shape[1]
    atoms = coupling.shape[0]
    nproj = coupling.shape[1]
    face = FACE
    flat_atoms = slot_atom.reshape(-1)
    onehot = (flat_atoms[None, :] == jnp.arange(atoms, dtype=jnp.int32)[:, None]).astype(
        jnp.float32
    )
    selector = onehot.astype(jnp.bfloat16)

    def apply_operator(block):
        cellwise = block.reshape(cells, nodes, width)
        local = jnp.einsum("cij,cjs->cis", cell_ham, cellwise, preferred_element_type=jnp.float32)
        coef = jnp.einsum("ckn,cns->cks", projectors, cellwise, preferred_element_type=jnp.float32)
        coef = coef.reshape(cells * slots, nproj * width)
        table = jnp.dot(onehot, coef, precision=lax.Precision.HIGHEST)
        summed = lax.psum(table, "mesh")
        scaled = (summed.reshape(atoms, nproj, width) * coupling[:, :, None]).astype(jnp.bfloat16)
        scaled = scaled.reshape(atoms, nproj * width)
        per_slot = jnp.dot(selector.T, scaled, preferred_element_type=jnp.float32).astype(
            jnp.bfloat16
        )
        per_slot = per_slot.reshape(cells, slots * nproj, width)
        local = local + jnp.einsum(
            "ckn,cks->cns", projectors, per_slot, preferred_element_type=jnp.float32
        )
        lower = local[:, :face]
        upper = local[:, nodes - face :]
        ends = jnp.stack([lower[0], upper[cells - 1]])
        rim = extended(ends, (("mesh", 0),), 1)
        from_below = jnp.concatenate([rim[0:1], upper[: cells - 1]], axis=0)
        from_above = jnp.concatenate([lower[1:], rim[3:4]], axis=0)
        middle = local[:, face : nodes - face]
        total = jnp.concatenate([lower + from_below, middle, upper + from_above], axis=1)
        return total.reshape(cells * nodes, width)

    half_width = 1.5
    center = 0.5
    low_edge = -1.2
    sigma = half_width / (low_edge - center)
    gamma = 2.0 / sigma
    previous = states
    image = apply_operator(states)
    current = ((image - center * states.astype(jnp.float32)) * (sigma / half_width)).astype(
        jnp.bfloat16
    )
    for degree in range(1, DEGREE):
        sigma_new = 1.0 / (gamma - sigma)
        image = apply_operator(current)
        following = (image - center * current.astype(jnp.float32)) * (2.0 * sigma_new / half_width)
        following = following - sigma * sigma_new * previous.astype(jnp.float32)
        previous = current
        current = following.astype(jnp.bfloat16)
        sigma = sigma_new
    values = current.astype(jnp.float32)
    partial_density = jnp.dot(values * values, occupancy, precision=lax.Precision.HIGHEST)
    summed_density = lax.psum_scatter(partial_density, "state", scatter_dimension=0, tiled=True)
    density = summed_density / (width * lax.axis_size("state"))
    return (current, density)


def solution(mesh):
    return jax.shard_map(
        shards,
        mesh=mesh,
        in_specs=(
            P("mesh", "state"),
            P("mesh", None, None),
            P("mesh", None, None),
            P("mesh", None),
            P(),
            P("state"),
        ),
        out_specs=(P("mesh", "state"), P(("mesh", "state"))),
        check_vma=False,
    )
```

profile of v0, /device:TPU:1, one launch (start us, length us, event | category | flops | bytes accessed | tf_op | source)
XLA Modules:
  0.0 1437.3 jit_solution(5547905226406511055)
XLA Ops:
  12.2 1.6 mul.90
  13.9 1.4 fusion.31
  15.3 331.3 %all-reduce.6.cloned.1.call-done = f32[48,3456]{1,0:T(8,128)} async-done(((f32[48,3456]{1,0:T(8,128)}), f32[48,3456]{1,0:T(8,128)}) %all-reduce.6.cloned.1.call-update) | async-done | bytes 663568 | tf_op jit(solution)/shard_map/psum | solution.py:47
  348.0 1.4 fusion.3
  349.6 3.2 collective-permute-start
  352.8 1.9 collective-permute-start.1
  355.0 3.8 collective-permute-done.1
  361.1 1.4 fusion.27
  362.5 328.5 %all-reduce.8.cloned.1.call-done = f32[48,3456]{1,0:T(8,128)} async-done(((f32[48,3456]{1,0:T(8,128)}), f32[48,3456]{1,0:T(8,128)}) %all-reduce.8.cloned.1.call-update) | async-done | bytes 663568 | tf_op jit(solution)/shard_map/psum | solution.py:47
  692.4 1.4 fusion.2
  694.0 3.2 collective-permute-start.2
  697.2 1.9 collective-permute-start.3
  699.4 3.8 collective-permute-done.3
  706.1 329.3 %all-reduce.10.cloned.1.call-done = f32[48,3456]{1,0:T(8,128)} async-done(((f32[48,3456]{1,0:T(8,128)}), f32[48,3456]{1,0:T(8,128)}) %all-reduce.10.cloned.1.call-update) | async-done | bytes 663568 | tf_op jit(solution)/shard_map/psum | solution.py:47
  1035.4 1.9 convolution_convert_fusion.1
  1038.7 3.2 collective-permute-start.4
  1042.0 1.9 collective-permute-start.5
  1044.1 3.8 collective-permute-done.5
  1051.7 328.5 %all-reduce.12.cloned.1.call-done = f32[48,3456]{1,0:T(8,128)} async-done(((f32[48,3456]{1,0:T(8,128)}), f32[48,3456]{1,0:T(8,128)}) %all-reduce.12.cloned.1.call-update) | async-done | bytes 663568 | tf_op jit(solution)/shard_map/psum | solution.py:47
  1381.6 1.4 fusion
  1383.2 3.2 collective-permute-start.6
  1386.4 1.9 collective-permute-start.7
  1390.5 1.8 collective-permute-done.7
  1394.1 36.0 %all-reduce = f32[1024]{0:T(1024)S(1)} all-reduce(f32[1024]{0:T(1024)S(1)} %bitcast.88), channel_id=2, replica_groups=mesh['mesh'=48,'state'=16] {'state'}, use_global_device_ids=true, to_apply=%region_4.0.clone | all-reduce | flops 1024 | bytes 8192
  (76 shorter events, 24.4 us)
Async XLA Ops:
  7.2 6.7 copy-start
  7.2 339.4 %all-reduce.6.cloned.1.call-start = ((), (), s32[]{:S(2)}) async-start(), calls=%async_computation | async-start | bytes 1327104 | tf_op jit(solution)/shard_map/psum | solution.py:47
  8.1 2.8 copy-start.4
  10.8 680.2 %all-reduce.8.cloned.1.call-start = ((), (), s32[]{:S(2)}) async-start(), calls=%async_computation.1 | async-start | bytes 1327104 | tf_op jit(solution)/shard_map/psum | solution.py:47
  12.2 1.6 copy-start.2
  15.3 332.8 %copy-start.1 = (bf16[2,72,512]{2,1,0:T(8,128)(2,1)S(1)}, bf16[2,72,512]{2,1,0:T(8,128)(2,1)}, u32[]{:S(2)}) copy-start(bf16[2,72,512]{2,1,0:T(8,128)(2,1)} %param.8) | copy-start | bytes 442372
  349.6 5.4 collective-permute-start
  352.8 5.9 collective-permute-start.1
  361.1 674.3 %all-reduce.10.cloned.1.call-start = ((), (), s32[]{:S(2)}) async-start(), calls=%async_computation.2 | async-start | bytes 1327104 | tf_op jit(solution)/shard_map/psum | solution.py:47
  694.0 5.4 collective-permute-start.2
  697.2 5.9 collective-permute-start.3
  705.6 674.6 %all-reduce.12.cloned.1.call-start = ((), (), s32[]{:S(2)}) async-start(), calls=%async_computation.3 | async-start | bytes 1327104 | tf_op jit(solution)/shard_map/psum | solution.py:47
  1038.7 5.4 collective-permute-start.4
  1042.0 5.9 collective-permute-start.5
  1383.2 7.3 collective-permute-start.6
  1386.4 5.9 collective-permute-start.7
  1392.9 0.7 copy-start.5
  1393.1 37.6 %copy-start.3 = (bf16[1024,192]{0,1:T(8,128)(2,1)}, bf16[1024,192]{0,1:T(8,128)(2,1)S(1)}, u32[]{:S(2)}) copy-start(bf16[1024,192]{0,1:T(8,128)(2,1)S(1)} %fusion.16) | copy-start | bytes 1179652
Sparse Core Ops, SparseCore 0:
  11.2 335.3 all-reduce.5
  361.2 329.7 all-reduce.7
  705.7 329.6 all-reduce.9
  1050.4 329.7 all-reduce.11
where the time goes:
time: 1440 us
  waiting for transfers between devices  1330 us (92%)
  blocking collectives  36 us (2%)
  matrix products  22.8 us (2%)
  starting transfers between devices  20.7 us (1%)
  between operations  14.8 us (1%)
    psum x4, waiting for transfers between devices, apply_operator(): summed = lax.psum(table, 'mesh')  1320 us
    unnamed x1, blocking collectives  36 us
  transfers between devices with their start and end apart: 12, of which 8 were waited for; matrix products, arithmetic and copies ran while one was open for 1% of the time, Pallas kernels for 0%

commit v1 on v0

v1 whole, which is shorter than its diff:
```python
import functools

import jax
import jax.numpy as jnp
from jax import lax
from jax.experimental import pallas as pl
from jax.experimental.pallas import tpu as pltpu
from jax.sharding import Mesh, PartitionSpec as P

FACE = 64
DEGREE = 4
LANES = 128
NODES = 512
NPROJ = 18
SLOTS = 4
ROWS = SLOTS * NPROJ
PACK = NODES + 80
GROUP = 4
PART = 2 * NODES
CENTER = 0.5
HALF_WIDTH = 1.5
LOW_EDGE = -1.2

BF16 = jnp.bfloat16
F32 = jnp.float32
NT = (((1,), (1,)), ((), ()))


def chebyshev_factors():
    sigma = HALF_WIDTH / (LOW_EDGE - CENTER)
    gamma = 2.0 / sigma
    factors = [(sigma / HALF_WIDTH, 0.0)]
    for _ in range(1, DEGREE):
        sigma_new = 1.0 / (gamma - sigma)
        factors.append((2.0 * sigma_new / HALF_WIDTH, sigma * sigma_new))
        sigma = sigma_new
    return factors


def iota(shape, dim):
    return lax.broadcasted_iota(jnp.int32, shape, dim)


def dot(a, b):
    return jnp.dot(a, b, preferred_element_type=F32)


def dot_nt(a, b):
    return lax.dot_general(a, b, NT, preferred_element_type=F32)


def placers():
    row = iota((LANES, ROWS), 0)
    col = iota((LANES, ROWS), 1)
    first = row == col
    second = ((row < NPROJ) & (row == col)) | ((row >= ROWS) & (row == col + ROWS - NPROJ))
    second = second & (row < 2 * ROWS - NPROJ)
    return first.astype(F32).astype(BF16), second.astype(F32).astype(BF16)


def low_lanes(rows):
    return iota((rows, LANES), 1) < FACE


def pick(rows, at):
    return jnp.sum(jnp.where(iota(rows.shape, 0) == at, rows, 0.0), axis=0, keepdims=True)


def open_kernel(atom_ref, v_ref, ham_ref, proj_ref, out_ref):
    width = v_ref.shape[0]
    piece = width // GROUP
    place0, place1 = placers()
    p0 = dot(place0, proj_ref[0]).astype(BF16)
    p1 = dot(place1, proj_ref[1]).astype(BF16)
    v0 = v_ref[:, :NODES]
    v1 = v_ref[:, NODES:]
    coef = dot_nt(v0, p0) + dot_nt(v1, p1)
    low = dot_nt(v0, ham_ref[0, :LANES, :])
    high = dot_nt(v1, ham_ref[1, NODES - LANES :, :])
    face = jnp.where(low_lanes(width), low, high)
    edge = jnp.where(
        low_lanes(ROWS),
        proj_ref[0, :, :LANES].astype(F32),
        proj_ref[1, :, NODES - LANES :].astype(F32),
    ).astype(BF16)
    lane = iota((16, LANES), 1)
    atoms = jnp.full((16, LANES), -1, jnp.int32)
    for block in range(2 * SLOTS - 1):
        cell, slot = (0, block) if block < SLOTS else (1, block - SLOTS + 1)
        inside = (lane >= block * NPROJ) & (lane < (block + 1) * NPROJ)
        atoms = jnp.where(inside, atom_ref[cell, slot], atoms)
    atoms = atoms.astype(F32).astype(BF16)
    tail = jnp.concatenate(
        [edge[piece:], jnp.zeros((2 * piece - 16 - ROWS, LANES), BF16)], axis=0
    )
    for to in range(GROUP):
        rows = slice(to * piece, (to + 1) * piece)
        out_ref[to, :, :PART] = v_ref[rows, :]
        out_ref[to, :, PART : PART + LANES] = coef[rows].astype(BF16)
        out_ref[to, :, PART + LANES : PART + 2 * LANES] = face[rows].astype(BF16)
        out_ref[to, :, PART + 2 * LANES : PART + 3 * LANES] = edge[:piece]
        out_ref[to, : piece - 16, PART + 3 * LANES :] = tail
        out_ref[to, piece - 16 :, PART + 3 * LANES :] = atoms


def pack_kernel(in_ref, out_ref):
    last = GROUP - 1
    piece = in_ref.shape[1]
    low = low_lanes(piece)
    for part in range(GROUP):
        out_ref[:, part * LANES : (part + 1) * LANES] = in_ref[part, :, :LANES]
    at = GROUP * LANES
    for k in (1, 2, 3):
        lanes = slice(k * LANES, (k + 1) * LANES)
        tile = jnp.where(low, in_ref[0, :, lanes].astype(F32), in_ref[last, :, lanes].astype(F32))
        if k == 3:
            row = iota((piece, LANES), 0)
            first = piece - 16
            for part in range(GROUP):
                atoms = in_ref[part, first:, lanes].astype(F32)
                tile = jnp.where(row == first + part, atoms[:1], tile)
        out_ref[:, at : at + LANES] = tile.astype(BF16)
        at += LANES


def step_kernel(degree, factors, *refs):
    first = degree == 0
    last = degree == DEGREE - 1
    refs = list(refs)
    take = lambda: refs.pop(0)
    place_ref, coup_ref, got_ref, v_ref = take(), take(), take(), take()
    old_ref = None if first else take()
    if first:
        packs = [take() for _ in range(GROUP)]
    else:
        packs = [take() for _ in range(GROUP)]
        proj_ref, near_ref, atoms_ref = take(), take(), take()
    occ_ref = take() if last else None
    next_ref = take()
    if first:
        proj_ref, near_ref, atoms_ref = None, None, None
    if last:
        density_ref = take()
    else:
        message_ref = take()
    if first:
        proj_ref, near_ref, atoms_ref = take(), take(), take()
    local_ref = take()

    groups = got_ref.shape[0]
    piece = v_ref.shape[1]
    me = place_ref[0]
    z = place_ref[1]
    below = jnp.maximum(z - 1, 0)
    above = jnp.minimum(z + 1, groups - 1)
    has_below = (z > 0).astype(F32)
    has_above = (z < groups - 1).astype(F32)
    wide = GROUP * LANES

    for r in range(GROUP):
        part = jnp.bitwise_xor(me, r)
        for cell in range(2):
            ham = packs[r][cell, :NODES, :]
            lanes = slice(cell * NODES, (cell + 1) * NODES)
            local_ref[part, :, lanes] = dot_nt(v_ref[part, :, lanes], ham)

    if first:
        place0, place1 = placers()
        for r in range(GROUP):
            part = jnp.bitwise_xor(me, r)
            for cell, place in ((0, place0), (1, place1)):
                raw = packs[r][cell, NODES : NODES + ROWS, :]
                lanes = slice(cell * NODES, (cell + 1) * NODES)
                proj_ref[part, :, lanes] = dot(place, raw).astype(BF16)
        edge_at = wide + LANES
        for k, group, place in ((0, below, place1), (1, above, place0)):
            tail = got_ref[group, : ROWS - piece, edge_at + LANES :]
            raw = jnp.concatenate([got_ref[group, :, edge_at : edge_at + LANES], tail], axis=0)
            near_ref[k] = dot(place, raw).astype(BF16)
        atoms_ref[...] = jnp.full(atoms_ref.shape, -1.0, F32)
        for group in range(groups):
            rows = got_ref[group, piece - 16 :, edge_at + LANES :].astype(F32)
            for part in range(GROUP):
                atoms_ref[group : group + 1, part * LANES : (part + 1) * LANES] = rows[part : part + 1]

    atoms = atoms_ref[...]
    which = lax.rem(iota(atoms.shape, 1) % LANES, NPROJ).astype(F32)
    codes = jnp.where(atoms < 0, -1.0, atoms * NPROJ + which)
    mine = jnp.concatenate(
        [
            pick(atoms[:16], z),
            pick(atoms[:16, wide - LANES :], below),
            pick(atoms[:16, :LANES], above),
        ],
        axis=1,
    )
    mine_which = lax.rem(iota(mine.shape, 1) % LANES, NPROJ).astype(F32)
    wanted = jnp.where(mine < 0, -2.0, mine * NPROJ + mine_which)
    spread = jnp.transpose(codes)
    total = jnp.zeros((piece, wide + 2 * LANES), F32)
    for group in range(groups):
        match = spread[:, group : group + 1] == wanted
        chosen = jnp.where(match, 1.0, 0.0).astype(BF16)
        total = total + dot(got_ref[group, :, :wide], chosen)
    count = coup_ref.shape[0]
    row = iota((count, LANES), 0).astype(F32)
    scaled = []
    for k in range(GROUP + 2):
        lanes = slice(k * LANES, (k + 1) * LANES)
        factor = jnp.sum(
            jnp.where(row == mine[:, lanes], coup_ref[...], 0.0), axis=0, keepdims=True
        )
        scaled.append((total[:, lanes] * factor).astype(BF16))

    for part in range(GROUP):
        local_ref[part] = local_ref[part] + dot(scaled[part], proj_ref[part])

    low = low_lanes(piece)
    face = slice(wide, wide + LANES)
    from_below = (got_ref[below, :, face].astype(F32) + dot(scaled[GROUP], near_ref[0])) * has_below
    from_above = (
        got_ref[above, :, face].astype(F32) + dot(scaled[GROUP + 1], near_ref[1])
    ) * has_above
    cells = [(part, cell * NODES) for part in range(GROUP) for cell in range(2)]
    heads = [local_ref[part, :, a : a + LANES] for part, a in cells]
    tails = [local_ref[part, :, a + NODES - LANES : a + NODES] for part, a in cells]
    for k, (part, a) in enumerate(cells):
        under = tails[k - 1] if k > 0 else from_below
        over = heads[k + 1] if k + 1 < len(cells) else from_above
        local_ref[part, :, a : a + LANES] = heads[k] + jnp.where(
            low, pltpu.roll(under, FACE, 1), 0.0
        )
        local_ref[part, :, a + NODES - LANES : a + NODES] = tails[k] + jnp.where(
            low, 0.0, pltpu.roll(over, FACE, 1)
        )

    gain, back = factors[degree]
    for part in range(GROUP):
        now = v_ref[part].astype(F32)
        new = (local_ref[part] - CENTER * now) * gain
        if not first:
            new = new - back * old_ref[part].astype(F32)
        new = new.astype(BF16)
        next_ref[part] = new
        if last:
            values = new.astype(F32)
            weight = jnp.broadcast_to(pick(occ_ref[...], me), (8, piece))
            density_ref[part : part + 1, :] = jnp.dot(
                weight, values * values, precision=lax.Precision.HIGHEST, preferred_element_type=F32
            )[:1]
        else:
            message_ref[:, part * LANES : (part + 1) * LANES] = dot_nt(new, proj_ref[part]).astype(
                BF16
            )
    if not last:
        for r in range(GROUP):
            part = jnp.bitwise_xor(me, r)

            @pl.when(part == 0)
            def _():
                tile = dot_nt(next_ref[0, :, :NODES], packs[r][0, :LANES, :])
                local_ref[0, :, :LANES] = tile

            @pl.when(part == GROUP - 1)
            def _():
                tile = dot_nt(
                    next_ref[GROUP - 1, :, NODES:], packs[r][1, NODES - LANES : NODES, :]
                )
                local_ref[0, :, LANES : 2 * LANES] = tile

        message_ref[:, wide:] = jnp.where(
            low, local_ref[0, :, :LANES], local_ref[0, :, LANES : 2 * LANES]
        ).astype(BF16)


def vmem():
    return pl.BlockSpec(memory_space=pltpu.VMEM)


def smem():
    return pl.BlockSpec(memory_space=pltpu.SMEM)


def shape(dims, dtype=BF16):
    return jax.ShapeDtypeStruct(dims, dtype)


def shards(interpret, states, cell_ham, projectors, slot_atom, coupling, occupancy):
    width = states.shape[1]
    piece = width // GROUP
    groups = lax.axis_size("z")
    y_hi = lax.axis_size("yh")
    params = pltpu.CompilerParams(vmem_limit_bytes=32 * 1024 * 1024)
    call = functools.partial(pl.pallas_call, compiler_params=params, interpret=interpret)
    me = 2 * lax.axis_index("yl") + lax.axis_index("c")
    place = jnp.stack([me, lax.axis_index("z")]).astype(jnp.int32)
    coup = jnp.tile(coupling, (1, LANES // NPROJ + 1))[:, :LANES]
    occ = occupancy.reshape(GROUP, piece)

    pack = jnp.concatenate(
        [cell_ham, jnp.pad(projectors, ((0, 0), (0, PACK - NODES - ROWS), (0, 0)))], axis=1
    )
    swap = [(0, 1), (1, 0)]
    ring = 2 * y_hi
    spot = lambda y: (y % 2) * y_hi + y // 2
    up = [(spot(y), spot((y + 1) % ring)) for y in range(ring)]
    down = [(b, a) for a, b in up]
    side = jnp.stack(
        [lax.ppermute(pack[0], ("yl", "yh"), up), lax.ppermute(pack[1], ("yl", "yh"), down)]
    )
    packs = [pack, lax.ppermute(pack, "c", swap), side, lax.ppermute(side, "c", swap)]

    v_t = states.T
    opened = call(
        open_kernel,
        out_shape=shape((GROUP, piece, PART + 4 * LANES)),
        in_specs=[smem(), vmem(), vmem(), vmem()],
        out_specs=vmem(),
    )(slot_atom, v_t, cell_ham, projectors)
    opened = lax.all_to_all(opened, ("yl", "c"), 0, 0)
    v = opened[:, :, :PART]
    message = call(
        pack_kernel,
        out_shape=shape((piece, 7 * LANES)),
        in_specs=[vmem()],
        out_specs=vmem(),
    )(opened[:, :, PART:])

    factors = chebyshev_factors()
    state_shape = shape((GROUP, piece, PART))
    message_shape = shape((piece, 5 * LANES))
    old = None
    kept = []
    for degree in range(DEGREE):
        got = lax.all_gather(message, "z")
        first, last = degree == 0, degree == DEGREE - 1
        ins = [place, coup, got, v] + ([] if first else [old]) + packs + kept
        ins += [occ] if last else []
        outs = [state_shape, shape((GROUP, PART), F32) if last else message_shape]
        if first:
            outs += [
                shape((GROUP, LANES, PART)),
                shape((2, LANES, LANES)),
                shape((LANES, GROUP * LANES), F32),
            ]
        result = call(
            functools.partial(step_kernel, degree, factors),
            out_shape=outs,
            in_specs=[smem()] + [vmem()] * (len(ins) - 1),
            out_specs=[vmem()] * len(outs),
            scratch_shapes=[pltpu.VMEM((GROUP, piece, PART), F32)],
        )(*ins)
        if first:
            kept = list(result[2:])
        old, v, message = v, result[0], result[1]

    filtered = lax.all_to_all(v, ("yl", "c"), 0, 0).reshape(width, PART).T
    parts = GROUP * lax.axis_size("x") * y_hi
    terms = lax.all_to_all(
        message.reshape(parts, GROUP * PART // parts), ("yl", "c", "x", "yh"), 0, 0, tiled=True
    )
    density = jnp.sum(terms, axis=0) / (width * lax.axis_size("x") * y_hi)
    return filtered, density


def build(mesh, interpret=False):
    part = ("z", "yl", "c")
    group = ("x", "yh")
    return jax.shard_map(
        functools.partial(shards, interpret),
        mesh=mesh,
        in_specs=(
            P(part, group),
            P(part, None, None),
            P(part, None, None),
            P(part, None),
            P(),
            P(group),
        ),
        out_specs=(P(part, group), P(part + group)),
        check_vma=False,
    )


def solution(mesh):
    count, groups = mesh.shape["mesh"], mesh.shape["state"]
    devices = mesh.devices.reshape(count // GROUP, 2, 2, groups // 4, 4)
    return build(Mesh(devices, ("z", "yl", "c", "x", "yh")))
```

time: 1440 us -> 201 us (0.14)
  waiting for transfers between devices: 1330 us -> 8.57 us
  blocking collectives: 36 us -> 128 us
  Pallas kernels: 0 us -> 27.8 us
  matrix products: 22.8 us -> 0 us
    psum x4 -> x0, waiting for transfers between devices: 1320 us -> none  [apply_operator(): summed = lax.psum(table, 'mesh')]
    all_gather x0 -> x4, blocking collectives: none -> 88.5 us  [shards(): got = lax.all_gather(message, 'z')]
    all_to_all x0 -> x1, blocking collectives: none -> 39.7 us  [shards(): lax.all_to_all(message.reshape(parts, GROUP * PART // parts), ('yl', 'c',...]
    unnamed x1 -> x0, blocking collectives: 36 us -> none
    pallas_call x0 -> x6, Pallas kernels: none -> 27.8 us  [the longest x4 25.9 us: shards(): call(functools.partial(step_kernel, degree, factors), out_shape=outs, in_...]
    dot_general x21 -> x0, matrix products: 22.8 us -> none  [the longest x4 5.84 us: apply_operator(): jnp.dot(selector.T, scaled, preferred_element_type=jnp.float32)]
    all_to_all x0 -> x2, starting transfers between devices: none -> 17.2 us  [the longest x1 13.2 us: shards(): opened = lax.all_to_all(opened, ('yl', 'c'), 0, 0)]
  transfers between devices with their start and end apart: 12 -> 6, of which waited for: 8 -> 2; matrix products, arithmetic and copies ran while one was open for 1% -> 1% of each run, Pallas kernels for 0% -> 1%
where the time goes in v1:
time: 201 us
  blocking collectives  128 us (64%)
  starting transfers between devices  29.4 us (15%)
  Pallas kernels  27.8 us (14%)
  waiting for transfers between devices  8.57 us (4%)
  other arithmetic  3.45 us (2%)
  local copies, waits for them, and re-layouts  2.19 us (1%)
    all_gather x4, blocking collectives, shards(): got = lax.all_gather(message, 'z')  88.5 us
    all_to_all x1, blocking collectives, shards(): lax.all_to_all(message.reshape(parts, GROUP * PART // parts), ('yl', 'c',...  39.7 us
    pallas_call x4, Pallas kernels, shards(): call(functools.partial(step_kernel, degree, factors), out_shape=outs, in_...  25.9 us
    all_to_all x1, starting transfers between devices, shards(): opened = lax.all_to_all(opened, ('yl', 'c'), 0, 0)  13.2 us
    all_to_all x1, waiting for transfers between devices, shards(): filtered = lax.all_to_all(v, ('yl', 'c'), 0, 0).reshape(width, PART).T  5.97 us
    all_to_all x1, starting transfers between devices, shards(): filtered = lax.all_to_all(v, ('yl', 'c'), 0, 0).reshape(width, PART).T  4.04 us
    ppermute x1, starting transfers between devices, shards(): lax.ppermute(pack[0], ('yl', 'yh'), up)  4.02 us
  transfers between devices with their start and end apart: 6, of which 2 were waited for; matrix products, arithmetic and copies ran while one was open for 1% of the time, Pallas kernels for 1%

profile of v1, /device:TPU:1, one launch (start us, length us, event | category | flops | bytes accessed | tf_op | source)
XLA Modules:
  0.0 200.5 jit_solution(7351528043281603839)
XLA Ops:
  0.6 1.4 fusion.1.refs_4_.refs_5_
  2.1 1.1 slice_bitcast_fusion.1
  3.2 4.0 %collective-permute-start.1 = (bf16[592,512]{1,0:T(8,128)(2,1)}, bf16[592,512]{1,0:T(8,128)(2,1)}, u32[]{:S(2)}, u32[]{:S(2)}) collective-permute-start(bf16[592,512]{1,0:T(8,128)(2,1)} %get-tuple-element.24), channel_id=1, source_target_pairs={{0,32},{32,1},{1,33},{33,2},{2,34},{34,3},{3,35},{35,0},{4,36},{36... | collective-permute-start | bytes 1818632 | tf_op jit(solution)/shard_map/ppermute | solution.py:309
  7.2 3.8 %collective-permute-start.2 = (bf16[592,512]{1,0:T(8,128)(2,1)}, bf16[592,512]{1,0:T(8,128)(2,1)}, u32[]{:S(2)}, u32[]{:S(2)}) collective-permute-start(bf16[592,512]{1,0:T(8,128)(2,1)} %get-tuple-element.25), channel_id=1, source_target_pairs={{32,0},{1,32},{33,1},{2,33},{34,2},{3,34},{35,3},{0,35},{36,4},{5,... | collective-permute-start | bytes 1818632 | tf_op jit(solution)/shard_map/ppermute | solution.py:309
  11.1 1.9 shard_map.77
  13.0 13.2 %all-to-all-start = ((bf16[4,48,1536]{2,1,0:T(8,128)(2,1)}), bf16[4,48,1536]{2,1,0:T(8,128)(2,1)S(1)}, u32[]{:S(2)}, u32[]{:S(2)}) async-start(bf16[4,48,1536]{2,1,0:T(8,128)(2,1)} %shard_map.77), calls=%async_computation | async-start | bytes 1179648 | tf_op jit(solution)/shard_map/all_to_all | solution.py:320
  26.1 1.9 collective-permute-start
  28.1 1.4 pad_maximum_fusion.refs_6_.refs_7_
  29.5 2.4 %collective-permute-start.3 = (bf16[2,592,512]{2,1,0:T(8,128)(2,1)S(1)}, bf16[2,592,512]{2,1,0:T(8,128)(2,1)}, u32[]{:S(2)}, u32[]{:S(2)}) collective-permute-start(bf16[2,592,512]{2,1,0:T(8,128)(2,1)S(1)} %pad_maximum_fusion.refs_6_.refs_7_), channel_id=1, source_target_pairs={{0,16},{16,0},{1,17},{17,1},{2,18},{18,2},{3,19},{19,3},{4,20},{20... | collective-permute-start | bytes 3637256 | tf_op jit(solution)/shard_map/ppermute | solution.py:311
  32.1 0.1 reshape.18.refs_12_
  32.2 2.6 %all-to-all-done = bf16[4,48,1536]{2,1,0:T(8,128)(2,1)S(1)} async-done(((bf16[4,48,1536]{2,1,0:T(8,128)(2,1)}), bf16[4,48,1536]{2,1,0:T(8,128)(2,1)S(1)}, u32[]{:S(2)}, u32[]{:S(2)}) %all-to-all-start) | async-done | bytes 589856 | tf_op jit(solution)/shard_map/all_to_all | solution.py:320
  34.9 29.8 %all-gather = bf16[576,896]{1,0:T(8,128)(2,1)S(1)} all-gather(bf16[48,896]{1,0:T(8,128)(2,1)S(1)} %shard_map.78), channel_id=2, replica_groups=mesh['z'=12,'yl'=2,'c'=2,'x'=4,'yh'=4] {'z'}, dimensions={0}, use_global_device_ids=true | all-gather | bytes 1118208 | tf_op jit(solution)/shard_map/all_gather | solution.py:335
  64.7 6.7 %shard_map.79 = (bf16[4,48,1024]{2,1,0:T(8,128)(2,1)S(1)}, bf16[48,640]{1,0:T(8,128)(2,1)S(1)}, bf16[4,128,1024]{2,1,0:T(8,128)(2,1)S(1)}, bf16[2,128,128]{2,1,0:T(8,128)(2,1)S(1)}, f32[128,512]{1,0:T(8,128)S(1)}) custom-call(s32[2]{0:T(128)S(1)} %pad_add_fusion.refs_0_, f32[48,128]{1,0:T(8,128)S(1)} %copy.12.refs_1_, bf16[12,48,896]{2,1,0:T(8,128)(2,1)S(1)} %bitcast.19, ...), custom_call_target="tpu_custom_call" | custom-call | tf_op jit(solution)/shard_map/pallas_call | solution.py:346
  71.4 20.1 %all-gather.1 = bf16[576,640]{1,0:T(8,128)(2,1)S(1)} all-gather(bf16[48,640]{1,0:T(8,128)(2,1)S(1)} %get-tuple-element.13), channel_id=3, replica_groups=mesh['z'=12,'yl'=2,'c'=2,'x'=4,'yh'=4] {'z'}, dimensions={0}, use_global_device_ids=true | all-gather | bytes 798720 | tf_op jit(solution)/shard_map/all_gather | solution.py:335
  91.5 6.3 %shard_map.80 = (bf16[4,48,1024]{2,1,0:T(8,128)(2,1)S(1)}, bf16[48,640]{1,0:T(8,128)(2,1)S(1)}) custom-call(s32[2]{0:T(128)S(1)} %pad_add_fusion.refs_0_, f32[48,128]{1,0:T(8,128)S(1)} %copy.12.refs_1_, bf16[12,48,640]{2,1,0:T(8,128)(2,1)S(1)} %bitcast.20, bf16[4,48,1024]{2,1,0:T(8,128)(2,1)S(1)} %get-tuple-element.14.refs_3_.refs_4_, ...), custom_call_target="tpu_custom_call" | custom-call | tf_op jit(solution)/shard_map/pallas_call | solution.py:346
  97.7 19.9 %all-gather.2 = bf16[576,640]{1,0:T(8,128)(2,1)S(1)} all-gather(bf16[48,640]{1,0:T(8,128)(2,1)S(1)} %get-tuple-element.18), channel_id=4, replica_groups=mesh['z'=12,'yl'=2,'c'=2,'x'=4,'yh'=4] {'z'}, dimensions={0}, use_global_device_ids=true | all-gather | bytes 798720 | tf_op jit(solution)/shard_map/all_gather | solution.py:335
  117.6 6.3 %shard_map.81 = (bf16[4,48,1024]{2,1,0:T(8,128)(2,1)S(1)}, bf16[48,640]{1,0:T(8,128)(2,1)S(1)}) custom-call(s32[2]{0:T(128)S(1)} %pad_add_fusion.refs_0_, f32[48,128]{1,0:T(8,128)S(1)} %copy.12.refs_1_, bf16[12,48,640]{2,1,0:T(8,128)(2,1)S(1)} %bitcast.21, bf16[4,48,1024]{2,1,0:T(8,128)(2,1)S(1)} %get-tuple-element.19.refs_3_.refs_4_, ...), custom_call_target="tpu_custom_call" | custom-call | tf_op jit(solution)/shard_map/pallas_call | solution.py:346
  123.9 18.8 %all-gather.3 = bf16[576,640]{1,0:T(8,128)(2,1)S(1)} all-gather(bf16[48,640]{1,0:T(8,128)(2,1)S(1)} %get-tuple-element.20), channel_id=5, replica_groups=mesh['z'=12,'yl'=2,'c'=2,'x'=4,'yh'=4] {'z'}, dimensions={0}, use_global_device_ids=true | all-gather | bytes 798720 | tf_op jit(solution)/shard_map/all_gather | solution.py:335
  142.7 6.6 %shard_map.82 = (bf16[4,48,1024]{2,1,0:T(8,128)(2,1)}, f32[4,1024]{1,0:T(4,128)S(1)}) custom-call(s32[2]{0:T(128)S(1)} %pad_add_fusion.refs_0_, f32[48,128]{1,0:T(8,128)S(1)} %copy.12.refs_1_, bf16[12,48,640]{2,1,0:T(8,128)(2,1)S(1)} %bitcast.22, bf16[4,48,1024]{2,1,0:T(8,128)(2,1)S(1)} %get-tuple-element.21.refs_3_, ...), custom_call_target="tpu_custom_call" | custom-call | tf_op jit(solution)/shard_map/pallas_call | solution.py:346
  149.4 39.7 %all_to_all.19 = f32[64,1,64]{2,1,0:T(1,128)S(1)} all-to-all(f32[64,1,64]{2,1,0:T(1,128)S(1)} %bitcast.25), channel_id=1, replica_groups=mesh['z'=12,'yl'=2,'c'=2,'x'=4,'yh'=4] {'yl','c','x','yh'}, dimensions={0} | all-to-all | bytes 32768 | tf_op jit(solution)/shard_map/all_to_all | solution.py:359
  189.2 4.0 %all-to-all-start.1 = ((bf16[4,48,1024]{2,1,0:T(8,128)(2,1)}), bf16[4,48,1024]{2,1,0:T(8,128)(2,1)S(1)}, u32[]{:S(2)}, u32[]{:S(2)}) async-start(bf16[4,48,1024]{2,1,0:T(8,128)(2,1)} %get-tuple-element.22), calls=%async_computation.1 | async-start | bytes 786432 | tf_op jit(solution)/shard_map/all_to_all | solution.py:357
  193.3 0.5 broadcast_multiply_fusion
  193.8 6.0 %all-to-all-done.1 = bf16[4,48,1024]{2,1,0:T(8,128)(2,1)S(1)} async-done(((bf16[4,48,1024]{2,1,0:T(8,128)(2,1)}), bf16[4,48,1024]{2,1,0:T(8,128)(2,1)S(1)}, u32[]{:S(2)}, u32[]{:S(2)}) %all-to-all-start.1) | async-done | bytes 393248 | tf_op jit(solution)/shard_map/all_to_all | solution.py:357
  199.8 0.7 copy.14
  (26 shorter events, 0.4 us)
Async XLA Ops:
  2.0 9.0 %copy-start = (bf16[2,512,512]{2,1,0:T(8,128)(2,1)S(1)}, bf16[2,512,512]{2,1,0:T(8,128)(2,1)}, u32[]{:S(2)}) copy-start(bf16[2,512,512]{2,1,0:T(8,128)(2,1)} %ham_ref.1) | copy-start | bytes 3145732
  2.0 9.0 %copy-start.1 = (bf16[2,72,512]{2,1,0:T(8,128)(2,1)S(1)}, bf16[2,72,512]{2,1,0:T(8,128)(2,1)}, u32[]{:S(2)}) copy-start(bf16[2,72,512]{2,1,0:T(8,128)(2,1)} %proj_ref.1) | copy-start | bytes 442372
  2.1 9.0 %copy-start.2 = (bf16[1024,192]{0,1:T(8,128)(2,1)S(1)}, bf16[1024,192]{0,1:T(8,128)(2,1)}, u32[]{:S(2)}) copy-start(bf16[1024,192]{0,1:T(8,128)(2,1)} %param.6) | copy-start | bytes 1179652
  2.1 9.0 %copy-start.3 = (s32[2,4]{1,0:T(2,128)S(1)}, s32[2,4]{1,0:T(2,128)}, u32[]{:S(2)}) copy-start(s32[2,4]{1,0:T(2,128)} %atom_ref.1) | copy-start | bytes 100
  3.2 24.9 %collective-permute-start.1 = (bf16[592,512]{1,0:T(8,128)(2,1)}, bf16[592,512]{1,0:T(8,128)(2,1)}, u32[]{:S(2)}, u32[]{:S(2)}) collective-permute-start(bf16[592,512]{1,0:T(8,128)(2,1)} %get-tuple-element.24), channel_id=1, source_target_pairs={{0,32},{32,1},{1,33},{33,2},{2,34},{34,3},{3,35},{35,0},{4,36},{36... | collective-permute-start | bytes 1818632 | tf_op jit(solution)/shard_map/ppermute | solution.py:309
  7.2 20.9 %collective-permute-start.2 = (bf16[592,512]{1,0:T(8,128)(2,1)}, bf16[592,512]{1,0:T(8,128)(2,1)}, u32[]{:S(2)}, u32[]{:S(2)}) collective-permute-start(bf16[592,512]{1,0:T(8,128)(2,1)} %get-tuple-element.25), channel_id=1, source_target_pairs={{32,0},{1,32},{33,1},{2,33},{34,2},{3,34},{35,3},{0,35},{36,4},{5,... | collective-permute-start | bytes 1818632 | tf_op jit(solution)/shard_map/ppermute | solution.py:309
  13.0 21.9 %all-to-all-start = ((bf16[4,48,1536]{2,1,0:T(8,128)(2,1)}), bf16[4,48,1536]{2,1,0:T(8,128)(2,1)S(1)}, u32[]{:S(2)}, u32[]{:S(2)}) async-start(bf16[4,48,1536]{2,1,0:T(8,128)(2,1)} %shard_map.77), calls=%async_computation | async-start | bytes 1179648 | tf_op jit(solution)/shard_map/all_to_all | solution.py:320
  26.1 38.6 %collective-permute-start = (bf16[2,592,512]{2,1,0:T(8,128)(2,1)S(1)}, bf16[2,592,512]{2,1,0:T(8,128)(2,1)}, u32[]{:S(2)}, u32[]{:S(2)}) collective-permute-start(bf16[2,592,512]{2,1,0:T(8,128)(2,1)S(1)} %fusion.1.refs_4_.refs_5_), channel_id=1, source_target_pairs={{0,16},{16,0},{1,17},{17,1},{2,18},{18,2},{3,19},{19,3},{4,20},{20... | collective-permute-start | bytes 3637256 | tf_op jit(solution)/shard_map/ppermute | solution.py:311
  28.1 3.8 %copy-start.4 = (f32[48,18]{0,1:T(8,128)S(1)}, f32[48,18]{0,1:T(8,128)}, u32[]{:S(2)}) copy-start(f32[48,18]{0,1:T(8,128)} %param.10) | copy-start | bytes 10372
  28.1 3.9 %copy-start.5 = (f32[192]{0:T(256)S(1)}, f32[192]{0:T(256)}, u32[]{:S(2)}) copy-start(f32[192]{0:T(256)} %param.11) | copy-start | bytes 2308
  29.5 35.2 %collective-permute-start.3 = (bf16[2,592,512]{2,1,0:T(8,128)(2,1)S(1)}, bf16[2,592,512]{2,1,0:T(8,128)(2,1)}, u32[]{:S(2)}, u32[]{:S(2)}) collective-permute-start(bf16[2,592,512]{2,1,0:T(8,128)(2,1)S(1)} %pad_maximum_fusion.refs_6_.refs_7_), channel_id=1, source_target_pairs={{0,16},{16,0},{1,17},{17,1},{2,18},{18,2},{3,19},{19,3},{4,20},{20... | collective-permute-start | bytes 3637256 | tf_op jit(solution)/shard_map/ppermute | solution.py:311
  189.2 10.6 %all-to-all-start.1 = ((bf16[4,48,1024]{2,1,0:T(8,128)(2,1)}), bf16[4,48,1024]{2,1,0:T(8,128)(2,1)S(1)}, u32[]{:S(2)}, u32[]{:S(2)}) async-start(bf16[4,48,1024]{2,1,0:T(8,128)(2,1)} %get-tuple-element.22), calls=%async_computation.1 | async-start | bytes 786432 | tf_op jit(solution)/shard_map/all_to_all | solution.py:357

commit v2 on v1

v2 whole, which is shorter than its diff:
```python
import functools

import jax
import jax.numpy as jnp
from jax import lax
from jax.experimental import pallas as pl
from jax.experimental.pallas import tpu as pltpu
from jax.sharding import Mesh, PartitionSpec as P

FACE = 64
DEGREE = 4
LANES = 128
NODES = 512
NPROJ = 18
SLOTS = 4
ROWS = SLOTS * NPROJ
SHARE = 208
GROUP = 4
PART = 2 * NODES
CENTER = 0.5
HALF_WIDTH = 1.5
LOW_EDGE = -1.2

BF16 = jnp.bfloat16
F32 = jnp.float32
NT = (((1,), (1,)), ((), ()))


def chebyshev_factors():
    sigma = HALF_WIDTH / (LOW_EDGE - CENTER)
    gamma = 2.0 / sigma
    factors = [(sigma / HALF_WIDTH, 0.0)]
    for _ in range(1, DEGREE):
        sigma_new = 1.0 / (gamma - sigma)
        factors.append((2.0 * sigma_new / HALF_WIDTH, sigma * sigma_new))
        sigma = sigma_new
    return factors


def iota(shape, dim):
    return lax.broadcasted_iota(jnp.int32, shape, dim)


def dot(a, b):
    return jnp.dot(a, b, preferred_element_type=F32)


def dot_nt(a, b):
    return lax.dot_general(a, b, NT, preferred_element_type=F32)


def placers():
    row = iota((LANES, ROWS), 0)
    col = iota((LANES, ROWS), 1)
    first = row == col
    second = ((row < NPROJ) & (row == col)) | ((row >= ROWS) & (row == col + ROWS - NPROJ))
    second = second & (row < 2 * ROWS - NPROJ)
    return first.astype(F32).astype(BF16), second.astype(F32).astype(BF16)


def low_lanes(rows):
    return iota((rows, LANES), 1) < FACE


def pick(rows, at):
    return jnp.sum(jnp.where(iota(rows.shape, 0) == at, rows, 0.0), axis=0, keepdims=True)


def open_kernel(atom_ref, v_ref, ham_ref, proj_ref, out_ref):
    width = v_ref.shape[0]
    piece = width // GROUP
    place0, place1 = placers()
    p0 = dot(place0, proj_ref[0]).astype(BF16)
    p1 = dot(place1, proj_ref[1]).astype(BF16)
    v0 = v_ref[:, :NODES]
    v1 = v_ref[:, NODES:]
    coef = dot_nt(v0, p0) + dot_nt(v1, p1)
    low = dot_nt(v0, ham_ref[0, :LANES, :])
    high = dot_nt(v1, ham_ref[1, NODES - LANES :, :])
    face = jnp.where(low_lanes(width), low, high)
    edge = jnp.where(
        low_lanes(ROWS),
        proj_ref[0, :, :LANES].astype(F32),
        proj_ref[1, :, NODES - LANES :].astype(F32),
    ).astype(BF16)
    lane = iota((16, LANES), 1)
    atoms = jnp.full((16, LANES), -1, jnp.int32)
    for block in range(2 * SLOTS - 1):
        cell, slot = (0, block) if block < SLOTS else (1, block - SLOTS + 1)
        inside = (lane >= block * NPROJ) & (lane < (block + 1) * NPROJ)
        atoms = jnp.where(inside, atom_ref[cell, slot], atoms)
    atoms = atoms.astype(F32).astype(BF16)
    tail = jnp.concatenate(
        [edge[piece:], jnp.zeros((2 * piece - 16 - ROWS, LANES), BF16)], axis=0
    )
    for to in range(GROUP):
        rows = slice(to * piece, (to + 1) * piece)
        out_ref[to, :, :LANES] = coef[rows].astype(BF16)
        out_ref[to, :, LANES : 2 * LANES] = face[rows].astype(BF16)
        out_ref[to, :, 2 * LANES : 3 * LANES] = edge[:piece]
        out_ref[to, : piece - 16, 3 * LANES :] = tail
        out_ref[to, piece - 16 :, 3 * LANES :] = atoms


def share_kernel(place_ref, v_ref, ham_ref, proj_ref, *out_refs):
    me = place_ref[0]
    piece = v_ref.shape[0] // GROUP
    local = [dot_nt(v_ref[:, :NODES], ham_ref[0]), dot_nt(v_ref[:, NODES:], ham_ref[1])]
    local = jnp.concatenate(local, axis=1).astype(BF16)
    first = me == 0
    half = FACE // 2
    at = 2 * piece
    for to in range(GROUP):
        rows = slice(to * piece, (to + 1) * piece)
        for r, out_ref in enumerate(out_refs):

            @pl.when(jnp.bitwise_xor(me, r) == to)
            def _():
                out_ref[:piece, :] = v_ref[rows, :]
                out_ref[piece:at, :] = local[rows]

    for out_ref in out_refs:
        for k in range(2):
            lanes = slice(k * NODES, (k + 1) * NODES)

            @pl.when(first)
            def _():
                out_ref[at : at + half, lanes] = ham_ref[0, k * half : (k + 1) * half, :]

            @pl.when(jnp.logical_not(first))
            def _():
                start = NODES - FACE + k * half
                out_ref[at : at + half, lanes] = ham_ref[1, start : start + half, :]

            out_ref[at + half :, lanes] = jnp.concatenate(
                [proj_ref[k], jnp.zeros((SHARE - at - half - ROWS, NODES), BF16)], axis=0
            )


def pack_kernel(in_ref, out_ref):
    last = GROUP - 1
    piece = in_ref.shape[1]
    low = low_lanes(piece)
    for part in range(GROUP):
        out_ref[:, part * LANES : (part + 1) * LANES] = in_ref[part, :, :LANES]
    at = GROUP * LANES
    for k in (1, 2, 3):
        lanes = slice(k * LANES, (k + 1) * LANES)
        tile = jnp.where(low, in_ref[0, :, lanes].astype(F32), in_ref[last, :, lanes].astype(F32))
        if k == 3:
            row = iota((piece, LANES), 0)
            first = piece - 16
            for part in range(GROUP):
                atoms = in_ref[part, first:, lanes].astype(F32)
                tile = jnp.where(row == first + part, atoms[:1], tile)
        out_ref[:, at : at + LANES] = tile.astype(BF16)
        at += LANES


def sum_coefs(place_ref, coup_ref, got_ref, atoms_ref):
    groups = got_ref.shape[0]
    piece = got_ref.shape[1]
    wide = GROUP * LANES
    z = place_ref[1]
    below = jnp.maximum(z - 1, 0)
    above = jnp.minimum(z + 1, groups - 1)
    atoms = atoms_ref[:16, :]
    mine = jnp.concatenate(
        [pick(atoms, z), pick(atoms[:, wide - LANES :], below), pick(atoms[:, :LANES], above)], axis=1
    )
    wanted = jnp.where(mine < 0, -2.0, mine).astype(BF16)
    spread = jnp.transpose(atoms_ref[...]).astype(BF16)
    same = lax.rem(iota((LANES, LANES), 0), NPROJ) == lax.rem(iota((LANES, LANES), 1), NPROJ)
    same = same.astype(F32).astype(BF16)
    same = jnp.concatenate([same] * (GROUP + 2), axis=1)
    same = jnp.concatenate([same] * GROUP, axis=0)
    none = jnp.zeros((), BF16)
    total = jnp.zeros((piece, wide + 2 * LANES), F32)
    for group in range(groups):
        chosen = jnp.where(spread[:, group : group + 1] == wanted, same, none)
        total = total + dot(got_ref[group, :, :wide], chosen)
    row = iota((coup_ref.shape[0], LANES), 0).astype(F32)
    scaled = []
    for k in range(GROUP + 2):
        lanes = slice(k * LANES, (k + 1) * LANES)
        factor = jnp.where(row == mine[:, lanes], coup_ref[...], 0.0)
        factor = jnp.sum(factor, axis=0, keepdims=True)
        scaled.append((total[:, lanes] * factor).astype(BF16))
    return scaled


def add_faces(place_ref, got_ref, near_ref, scaled, local_ref):
    groups = got_ref.shape[0]
    piece = got_ref.shape[1]
    z = place_ref[1]
    below = jnp.maximum(z - 1, 0)
    above = jnp.minimum(z + 1, groups - 1)
    low = low_lanes(piece)
    face = slice(GROUP * LANES, (GROUP + 1) * LANES)
    from_below = got_ref[below, :, face].astype(F32) + dot(scaled[GROUP], near_ref[0])
    from_above = got_ref[above, :, face].astype(F32) + dot(scaled[GROUP + 1], near_ref[1])
    from_below = from_below * (z > 0).astype(F32)
    from_above = from_above * (z < groups - 1).astype(F32)
    cells = [(part, cell * NODES) for part in range(GROUP) for cell in range(2)]
    heads = [local_ref[part, :, a : a + LANES] for part, a in cells]
    tails = [local_ref[part, :, a + NODES - LANES : a + NODES] for part, a in cells]
    for k, (part, a) in enumerate(cells):
        under = tails[k - 1] if k > 0 else from_below
        over = heads[k + 1] if k + 1 < len(cells) else from_above
        local_ref[part, :, a : a + LANES] = heads[k] + jnp.where(
            low, pltpu.roll(under, FACE, 1), 0.0
        )
        local_ref[part, :, a + NODES - LANES : a + NODES] = tails[k] + jnp.where(
            low, 0.0, pltpu.roll(over, FACE, 1)
        )


def write_message(new, proj_ref, edge_ref, message_ref):
    for part in range(GROUP):
        lanes = slice(part * LANES, (part + 1) * LANES)
        message_ref[:, lanes] = dot_nt(new[part], proj_ref[part]).astype(BF16)
    ends = jnp.concatenate([new[0][:, :NODES], new[GROUP - 1][:, NODES:]], axis=1)
    message_ref[:, GROUP * LANES :] = dot_nt(ends, edge_ref[...]).astype(BF16)


def first_kernel(factors, place_ref, coup_ref, got_ref, *refs):
    shares = refs[:GROUP]
    next_ref, message_ref, v_ref, proj_ref, near_ref, edge_ref, atoms_ref, local_ref = refs[GROUP:]
    groups = got_ref.shape[0]
    piece = v_ref.shape[1]
    me = place_ref[0]
    z = place_ref[1]
    below = jnp.maximum(z - 1, 0)
    above = jnp.minimum(z + 1, groups - 1)
    wide = GROUP * LANES
    half = FACE // 2
    at = 2 * piece

    place0, place1 = placers()
    edge_ref[...] = jnp.zeros(edge_ref.shape, BF16)
    for r, share in enumerate(shares):
        part = jnp.bitwise_xor(me, r)
        v_ref[part] = share[:piece, :]
        local_ref[part] = share[piece:at, :].astype(F32)
        for cell, place in ((0, place0), (1, place1)):
            lanes = slice(cell * NODES, (cell + 1) * NODES)
            raw = share[at + half : at + half + ROWS, lanes]
            proj_ref[part, :, lanes] = dot(place, raw).astype(BF16)
        for k, end in ((0, 0), (1, GROUP - 1)):

            @pl.when(part == end)
            def _():
                lanes = slice(k * NODES, (k + 1) * NODES)
                row = k * FACE
                edge_ref[row : row + half, lanes] = share[at : at + half, :NODES]
                edge_ref[row + half : row + FACE, lanes] = share[at : at + half, NODES:]

    edge_at = wide + LANES
    for k, group, place in ((0, below, place1), (1, above, place0)):
        tail = got_ref[group, : ROWS - piece, edge_at + LANES :]
        raw = jnp.concatenate([got_ref[group, :, edge_at : edge_at + LANES], tail], axis=0)
        near_ref[k] = dot(place, raw).astype(BF16)
    atoms_ref[...] = jnp.full(atoms_ref.shape, -1.0, F32)
    for group in range(groups):
        rows = got_ref[group, piece - 16 :, edge_at + LANES :].astype(F32)
        for part in range(GROUP):
            lanes = slice(part * LANES, (part + 1) * LANES)
            atoms_ref[group : group + 1, lanes] = rows[part : part + 1]

    scaled = sum_coefs(place_ref, coup_ref, got_ref, atoms_ref)
    for part in range(GROUP):
        local_ref[part] = local_ref[part] + dot(scaled[part], proj_ref[part])
    add_faces(place_ref, got_ref, near_ref, scaled, local_ref)
    gain, _ = factors[0]
    new = []
    for part in range(GROUP):
        new.append(((local_ref[part] - CENTER * v_ref[part].astype(F32)) * gain).astype(BF16))
        next_ref[part] = new[part]
    write_message(new, proj_ref, edge_ref, message_ref)


def step_kernel(degree, factors, place_ref, coup_ref, got_ref, v_ref, old_ref, ham_ref, *refs):
    last = degree == DEGREE - 1
    proj_ref, near_ref, edge_ref, atoms_ref = refs[:4]
    refs = refs[4:]
    if last:
        occ_ref, next_ref, local_ref, held_ref, sems = refs
    else:
        next_ref, message_ref, local_ref, held_ref, sems = refs
    piece = v_ref.shape[1]
    copies = [
        pltpu.make_async_copy(ham_ref.at[k // 2, k % 2], held_ref.at[k], sems.at[k])
        for k in range(2 * GROUP)
    ]
    for copy in copies:
        copy.start()
    scaled = sum_coefs(place_ref, coup_ref, got_ref, atoms_ref)
    for copy in copies:
        copy.wait()
    for part in range(GROUP):
        for cell in range(2):
            lanes = slice(cell * NODES, (cell + 1) * NODES)
            local = dot_nt(v_ref[part, :, lanes], held_ref[2 * part + cell])
            local_ref[part, :, lanes] = local + dot(scaled[part], proj_ref[part, :, lanes])
    add_faces(place_ref, got_ref, near_ref, scaled, local_ref)

    gain, back = factors[degree]
    new = []
    for part in range(GROUP):
        now = v_ref[part].astype(F32)
        image = (local_ref[part] - CENTER * now) * gain - back * old_ref[part].astype(F32)
        new.append(image.astype(BF16))
        next_ref[part, :piece, :] = new[part]
    if not last:
        write_message(new, proj_ref, edge_ref, message_ref)
        return
    weight = jnp.broadcast_to(pick(occ_ref[...], place_ref[0]), (8, piece))
    row = iota((16, PART), 0)
    for part in range(GROUP):
        values = new[part].astype(F32)
        sums = jnp.dot(
            weight, values * values, precision=lax.Precision.HIGHEST, preferred_element_type=F32
        )[:1]
        high = sums.astype(BF16).astype(F32)
        both = jnp.where(row == 0, high, jnp.where(row == 1, sums - high, 0.0))
        next_ref[part, piece:, :] = both.astype(BF16)


def density_kernel(in_ref, out_ref):
    total = jnp.zeros((2, PART), F32)
    for part in range(GROUP):
        total = total + in_ref[part, :2, :].astype(F32)
    total = total[:1] + total[1:]
    for k in range(PART // LANES):
        tile = total[:, k * LANES : (k + 1) * LANES]
        out_ref[2 * k : 2 * k + 1, :] = tile[:, :FACE]
        out_ref[2 * k + 1 : 2 * k + 2, :] = tile[:, FACE:]


def vmem():
    return pl.BlockSpec(memory_space=pltpu.VMEM)


def smem():
    return pl.BlockSpec(memory_space=pltpu.SMEM)


def shape(dims, dtype=BF16):
    return jax.ShapeDtypeStruct(dims, dtype)


def shards(interpret, states, cell_ham, projectors, slot_atom, coupling, occupancy):
    width = states.shape[1]
    piece = width // GROUP
    y_hi = lax.axis_size("yh")
    spread = lax.axis_size("x") * y_hi
    params = pltpu.CompilerParams(vmem_limit_bytes=32 * 1024 * 1024)
    call = functools.partial(pl.pallas_call, compiler_params=params, interpret=interpret)
    me = 2 * lax.axis_index("yl") + lax.axis_index("c")
    place = jnp.stack([me, lax.axis_index("z")]).astype(jnp.int32)
    coup = jnp.tile(coupling, (1, LANES // NPROJ + 1))[:, :LANES]
    occ = occupancy.reshape(GROUP, piece)
    near = ("yl", "c")

    ham = lax.all_gather(cell_ham, near)
    v_t = states.T
    opened = call(
        open_kernel,
        out_shape=shape((GROUP, piece, 4 * LANES)),
        in_specs=[smem(), vmem(), vmem(), vmem()],
        out_specs=vmem(),
    )(slot_atom, v_t, cell_ham, projectors)
    opened = lax.all_to_all(opened, near, 0, 0)
    shares = call(
        share_kernel,
        out_shape=[shape((SHARE, PART))] * GROUP,
        in_specs=[smem(), vmem(), vmem(), vmem()],
        out_specs=[vmem()] * GROUP,
    )(place, v_t, cell_ham, projectors)
    shares = [shares[0]] + [
        lax.ppermute(shares[r], near, [(k, k ^ r) for k in range(GROUP)]) for r in (1, 2, 3)
    ]
    message = call(
        pack_kernel,
        out_shape=shape((piece, 7 * LANES)),
        in_specs=[vmem()],
        out_specs=vmem(),
    )(opened)

    factors = chebyshev_factors()
    state_shape = shape((GROUP, piece, PART))
    message_shape = shape((piece, 5 * LANES))
    scratch = pltpu.VMEM((GROUP, piece, PART), F32)
    got = lax.all_gather(message, "z")
    v, message, old, *kept = call(
        functools.partial(first_kernel, factors),
        out_shape=[
            state_shape,
            message_shape,
            state_shape,
            shape((GROUP, LANES, PART)),
            shape((2, LANES, LANES)),
            shape((LANES, PART)),
            shape((LANES, GROUP * LANES), F32),
        ],
        in_specs=[smem()] + [vmem()] * (2 + GROUP),
        out_specs=[vmem()] * 7,
        scratch_shapes=[scratch],
    )(place, coup, got, *shares)
    for degree in range(1, DEGREE):
        got = lax.all_gather(message, "z")
        last = degree == DEGREE - 1
        outs = [shape((GROUP, piece + 16, PART))] if last else [state_shape, message_shape]
        ends = [occ] if last else []
        result = call(
            functools.partial(step_kernel, degree, factors),
            out_shape=outs,
            in_specs=[smem()]
            + [vmem()] * 4
            + [pl.BlockSpec(memory_space=pl.ANY)]
            + [vmem()] * (4 + len(ends)),
            out_specs=[vmem()] * len(outs),
            scratch_shapes=[
                scratch,
                pltpu.VMEM((2 * GROUP, NODES, NODES), BF16),
                pltpu.SemaphoreType.DMA((2 * GROUP,)),
            ],
        )(place, coup, got, v, old, ham, *kept, *ends)
        old, v, message = v, result[0], result[-1]

    final = lax.all_to_all(message, near, 0, 0)
    filtered = final[:, :piece, :].reshape(width, PART).T
    terms = call(
        density_kernel,
        out_shape=shape((PART // FACE, FACE), F32),
        grid=(1,),
        in_specs=[pl.BlockSpec((GROUP, 16, PART), lambda i: (0, piece // 16, 0))],
        out_specs=pl.BlockSpec((PART // FACE, FACE), lambda i: (0, 0)),
    )(final)
    terms = lax.all_to_all(
        terms.reshape(spread, PART // spread), ("x", "yh"), 0, 0, tiled=True
    )
    density = jnp.sum(terms, axis=0) / (width * spread)
    return filtered, density


def build(mesh, interpret=False):
    part = ("z", "yl", "c")
    group = ("x", "yh")
    return jax.shard_map(
        functools.partial(shards, interpret),
        mesh=mesh,
        in_specs=(
            P(part, group),
            P(part, None, None),
            P(part, None, None),
            P(part, None),
            P(),
            P(group),
        ),
        out_specs=(P(part, group), P(part + group)),
        check_vma=False,
    )


def solution(mesh):
    count, groups = mesh.shape["mesh"], mesh.shape["state"]
    devices = mesh.devices.reshape(count // GROUP, 2, 2, groups // 4, 4)
    return build(Mesh(devices, ("z", "yl", "c", "x", "yh")))
```

time: 201 us -> 221 us (1.100)
  blocking collectives: 128 us -> 113 us
  between operations: 0.86 us -> 14.2 us
  local copies, waits for them, and re-layouts: 2.19 us -> 15.4 us
  waiting for transfers between devices: 8.57 us -> 19 us
  other arithmetic: 3.45 us -> 0.63 us
    unnamed x14 -> x35, local copies, waits for them, and re-layouts: 0.84 us -> 14.5 us
    all_to_all x1, blocking collectives: 39.7 us -> 27 us  [shards(): final = lax.all_to_all(message, near, 0, 0)]
    ppermute x4 -> x3, waiting for transfers between devices: 0.01 us -> 10.3 us  [shards(): lax.ppermute(shares[r], near, [(k, k ^ r) for k in range(GROUP)])]
    pallas_call x4 -> x3, Pallas kernels: 25.9 us -> 16.8 us  [shards(): call(functools.partial(step_kernel, degree, factors), out_shape=outs, in_...]
    pallas_call x1 -> x4, Pallas kernels: 1.9 us -> 9.23 us  [the longest x1 4.76 us: shards(): call(functools.partial(first_kernel, factors), out_shape=[state_shape, me...]
    all_to_all x2, starting transfers between devices: 17.2 us -> 23.6 us  [the longest x1 13.8 us: shards(): opened = lax.all_to_all(opened, near, 0, 0)]
    ppermute x4 -> x3, starting transfers between devices: 12.2 us -> 7.85 us  [shards(): lax.ppermute(shares[r], near, [(k, k ^ r) for k in range(GROUP)])]
    all_gather x4, blocking collectives: 88.5 us -> 86.1 us  [shards(): got = lax.all_gather(message, 'z')]
  transfers between devices with their start and end apart: 6 -> 6, of which waited for: 2 -> 2; matrix products, arithmetic and copies ran while one was open for 1% -> 0% of each run, Pallas kernels for 1% -> 4%
where the time goes in v2:
time: 221 us; the launch traced here: 220 us
  blocking collectives  113 us (51%)
  starting transfers between devices  31.5 us (14%)
  Pallas kernels  26 us (12%)
  waiting for transfers between devices  19 us (9%)
  local copies, waits for them, and re-layouts  15.4 us (7%)
  between operations  14.2 us (6%)
    all_gather x4, blocking collectives, shards(): got = lax.all_gather(message, 'z')  86.1 us
    all_to_all x1, blocking collectives, shards(): final = lax.all_to_all(message, near, 0, 0)  27 us
    pallas_call x3, Pallas kernels, shards(): call(functools.partial(step_kernel, degree, factors), out_shape=outs, in_...  16.8 us
    unnamed x35, local copies, waits for them, and re-layouts  14.5 us
    all_to_all x1, starting transfers between devices, shards(): opened = lax.all_to_all(opened, near, 0, 0)  13.8 us
    ppermute x3, waiting for transfers between devices, shards(): lax.ppermute(shares[r], near, [(k, k ^ r) for k in range(GROUP)])  10.3 us
    all_to_all x1, starting transfers between devices, shards(): lax.all_to_all(terms.reshape(spread, PART // spread), ('x', 'yh'), 0, 0,...  9.8 us
    all_to_all x1, waiting for transfers between devices, shards(): lax.all_to_all(terms.reshape(spread, PART // spread), ('x', 'yh'), 0, 0,...  8.04 us
  transfers between devices with their start and end apart: 6, of which 2 were waited for; matrix products, arithmetic and copies ran while one was open for 0% of the time, Pallas kernels for 4%

profile of v2, /device:TPU:1, one launch (start us, length us, event | category | flops | bytes accessed | tf_op | source)
XLA Modules:
  0.0 219.9 jit_solution(11069539044967815199)
XLA Ops:
  7.9 1.2 copy-done.2
  9.1 1.0 copy-done.4
  11.7 1.8 shard_map.77
  13.5 13.8 %all-to-all-start = ((bf16[4,48,512]{2,1,0:T(8,128)(2,1)}), bf16[4,48,512]{2,1,0:T(8,128)(2,1)S(1)}, u32[]{:S(2)}, u32[]{:S(2)}) async-start(bf16[4,48,512]{2,1,0:T(8,128)(2,1)} %shard_map.77), calls=%async_computation | async-start | bytes 393216 | tf_op jit(solution)/shard_map/all_to_all | solution.py:373
  27.4 1.2 copy-done.3
  30.5 2.0 shard_map.79
  32.6 2.0 collective-permute-start
  34.5 3.6 %collective-permute-start.1 = (bf16[208,1024]{1,0:T(8,128)(2,1)S(1)}, bf16[208,1024]{1,0:T(8,128)(2,1)S(1)}, u32[]{:S(2)}, u32[]{:S(2)}) collective-permute-start(bf16[208,1024]{1,0:T(8,128)(2,1)S(1)} %get-tuple-element.19), channel_id=1, source_target_pairs={{0,32},{16,48},{32,0},{48,16},{1,33},{17,49},{33,1},{49,17},{2,34}... | collective-permute-start | bytes 1277960 | tf_op jit(solution)/shard_map/ppermute | solution.py:381
  38.1 2.3 %collective-permute-start.2 = (bf16[208,1024]{1,0:T(8,128)(2,1)S(1)}, bf16[208,1024]{1,0:T(8,128)(2,1)S(1)}, u32[]{:S(2)}, u32[]{:S(2)}) collective-permute-start(bf16[208,1024]{1,0:T(8,128)(2,1)S(1)} %get-tuple-element.20), channel_id=1, source_target_pairs={{0,48},{16,32},{32,16},{48,0},{1,49},{17,33},{33,17},{49,1},{2,50}... | collective-permute-start | bytes 1277960 | tf_op jit(solution)/shard_map/ppermute | solution.py:381
  40.7 24.3 %all-gather = bf16[576,896]{1,0:T(8,128)(2,1)S(1)} all-gather(bf16[48,896]{1,0:T(8,128)(2,1)S(1)} %shard_map.78), channel_id=2, replica_groups=mesh['z'=12,'yl'=2,'c'=2,'x'=4,'yh'=4] {'z'}, dimensions={0}, use_global_device_ids=true | all-gather | bytes 1118208 | tf_op jit(solution)/shard_map/all_gather | solution.py:394
  65.8 10.2 %collective-permute-done.2.refs_3_ = bf16[208,1024]{1,0:T(8,128)(2,1)S(1)} collective-permute-done((bf16[208,1024]{1,0:T(8,128)(2,1)S(1)}, bf16[208,1024]{1,0:T(8,128)(2,1)S(1)}, u32[]{:S(2)}, u32[]{:S(2)}) %collective-permute-start.2) | collective-permute-done | bytes 426016 | tf_op jit(solution)/shard_map/ppermute | solution.py:381
  76.8 1.0 copy-done.9
  77.9 1.0 copy-done.11
  78.9 4.8 %shard_map.80 = (bf16[4,48,1024]{2,1,0:T(8,128)(2,1)S(1)}, bf16[48,640]{1,0:T(8,128)(2,1)S(1)}, bf16[4,48,1024]{2,1,0:T(8,128)(2,1)S(1)}, bf16[4,128,1024]{2,1,0...) custom-call(s32[2]{0:T(128)S(1)} %pad_add_fusion.place_ref, ...), custom_call_target="tpu_custom_call" | custom-call | tf_op jit(solution)/shard_map/pallas_call | solution.py:395
  84.4 21.5 %all-gather.1 = bf16[576,640]{1,0:T(8,128)(2,1)S(1)} all-gather(bf16[48,640]{1,0:T(8,128)(2,1)S(1)} %get-tuple-element.21), channel_id=3, replica_groups=mesh['z'=12,'yl'=2,'c'=2,'x'=4,'yh'=4] {'z'}, dimensions={0}, use_global_device_ids=true | all-gather | bytes 798720 | tf_op jit(solution)/shard_map/all_gather | solution.py:411
  106.0 2.2 copy-done
  109.2 5.6 %shard_map.81 = (bf16[4,48,1024]{2,1,0:T(8,128)(2,1)S(1)}, bf16[48,640]{1,0:T(8,128)(2,1)S(1)}) custom-call(s32[2]{0:T(128)S(1)} %pad_add_fusion.place_ref, f32[48,128]{1,0:T(8,128)S(1)} %copy.12.coup_ref, bf16[12,48,640]{2,1,0:T(8,128)(2,1)S(1)} %bitcast.20, bf16[4,48,1024]{2,1,0:T(8,128)(2,1)S(1)} %get-tuple-element.22.v_ref.old_ref, ...), custom_call_target="tpu_custom_call" | custom-call | tf_op jit(solution)/shard_map/pallas_call | solution.py:415
  114.8 19.8 %all-gather.3 = bf16[576,640]{1,0:T(8,128)(2,1)S(1)} all-gather(bf16[48,640]{1,0:T(8,128)(2,1)S(1)} %get-tuple-element.28), channel_id=5, replica_groups=mesh['z'=12,'yl'=2,'c'=2,'x'=4,'yh'=4] {'z'}, dimensions={0}, use_global_device_ids=true | all-gather | bytes 798720 | tf_op jit(solution)/shard_map/all_gather | solution.py:411
  134.5 5.6 %shard_map.82 = (bf16[4,48,1024]{2,1,0:T(8,128)(2,1)S(1)}, bf16[48,640]{1,0:T(8,128)(2,1)S(1)}) custom-call(s32[2]{0:T(128)S(1)} %pad_add_fusion.place_ref, f32[48,128]{1,0:T(8,128)S(1)} %copy.12.coup_ref, bf16[12,48,640]{2,1,0:T(8,128)(2,1)S(1)} %bitcast.21, bf16[4,48,1024]{2,1,0:T(8,128)(2,1)S(1)} %get-tuple-element.29.v_ref.old_ref, ...), custom_call_target="tpu_custom_call" | custom-call | tf_op jit(solution)/shard_map/pallas_call | solution.py:415
  140.1 20.5 %all-gather.4 = bf16[576,640]{1,0:T(8,128)(2,1)S(1)} all-gather(bf16[48,640]{1,0:T(8,128)(2,1)S(1)} %get-tuple-element.30), channel_id=6, replica_groups=mesh['z'=12,'yl'=2,'c'=2,'x'=4,'yh'=4] {'z'}, dimensions={0}, use_global_device_ids=true | all-gather | bytes 798720 | tf_op jit(solution)/shard_map/all_gather | solution.py:411
  160.6 5.6 %shard_map.83 = bf16[4,64,1024]{2,1,0:T(8,128)(2,1)S(1)} custom-call(s32[2]{0:T(128)S(1)} %pad_add_fusion.place_ref, f32[48,128]{1,0:T(8,128)S(1)} %copy.12.coup_ref, bf16[12,48,640]{2,1,0:T(8,128)(2,1)S(1)} %bitcast.22, bf16[4,48,1024]{2,1,0:T(8,128)(2,1)S(1)} %get-tuple-element.31.v_ref, bf16[4,48,1024]{2,1,0:T(8,128)(2,1)S(1)} %get-tuple-element.29.v_ref.old_ref, ...), custom_call_target="tpu_custom_call" | custom-call | tf_op jit(solution)/shard_map/pallas_call | solution.py:415
  166.2 27.0 %all_to_all.19.in_ref = bf16[4,64,1024]{2,1,0:T(8,128)(2,1)S(1)} all-to-all(bf16[4,64,1024]{2,1,0:T(8,128)(2,1)S(1)} %shard_map.83), channel_id=1, replica_groups=mesh['z'=12,'yl'=2,'c'=2,'x'=4,'yh'=4] {'yl','c'}, dimensions={0} | all-to-all | bytes 1048576 | tf_op jit(solution)/shard_map/all_to_all | solution.py:431
  193.9 9.8 %all-to-all-start.2 = ((f32[16,1,64]{2,1,0:T(1,128)}), f32[16,1,64]{2,1,0:T(1,128)S(1)}, u32[]{:S(2)}, u32[]{:S(2)}) async-start(f32[16,1,64]{2,1,0:T(1,128)} %bitcast.11), calls=%async_computation.2 | async-start | bytes 16384 | tf_op jit(solution)/shard_map/all_to_all | solution.py:440
  204.4 8.0 %all-to-all-done.2 = f32[16,1,64]{2,1,0:T(1,128)S(1)} async-done(((f32[16,1,64]{2,1,0:T(1,128)}), f32[16,1,64]{2,1,0:T(1,128)S(1)}, u32[]{:S(2)}, u32[]{:S(2)}) %all-to-all-start.2) | async-done | bytes 4128 | tf_op jit(solution)/shard_map/all_to_all | solution.py:440
  (45 shorter events, 9.8 us)
Async XLA Ops:
  7.2 33.3 %copy-start.15 = (f32[48,18]{0,1:T(8,128)S(1)}, f32[48,18]{0,1:T(8,128)}, u32[]{:S(2)}) copy-start(f32[48,18]{0,1:T(8,128)} %param.10) | copy-start | bytes 10372
  7.2 33.4 %copy-start.16 = (f32[192]{0:T(256)S(1)}, f32[192]{0:T(256)}, u32[]{:S(2)}) copy-start(f32[192]{0:T(256)} %param.11) | copy-start | bytes 2308
  7.2 98.8 %all-gather.7.cloned.1.call-start = ((), (), s32[]{:S(2)}) async-start(), calls=%async_computation.3 | async-start | bytes 5242880 | tf_op jit(solution)/shard_map/all_gather | solution.py:365
  7.9 1.2 copy-start.2
  9.1 1.0 copy-start.4
  10.1 0.9 copy-start.6
  11.1 0.7 copy-start.14
  13.5 27.2 %all-to-all-start = ((bf16[4,48,512]{2,1,0:T(8,128)(2,1)}), bf16[4,48,512]{2,1,0:T(8,128)(2,1)S(1)}, u32[]{:S(2)}, u32[]{:S(2)}) async-start(bf16[4,48,512]{2,1,0:T(8,128)(2,1)} %shard_map.77), calls=%async_computation | async-start | bytes 393216 | tf_op jit(solution)/shard_map/all_to_all | solution.py:373
  27.4 1.2 copy-start.3
  28.6 1.0 copy-start.5
  29.6 0.9 copy-start.7
  32.6 32.5 %collective-permute-start = (bf16[208,1024]{1,0:T(8,128)(2,1)}, bf16[208,1024]{1,0:T(8,128)(2,1)S(1)}, u32[]{:S(2)}, u32[]{:S(2)}) collective-permute-start(bf16[208,1024]{1,0:T(8,128)(2,1)} %get-tuple-element.18), channel_id=1, source_target_pairs={{0,16},{16,0},{32,48},{48,32},{1,17},{17,1},{33,49},{49,33},{2,18}... | collective-permute-start | bytes 1277960 | tf_op jit(solution)/shard_map/ppermute | solution.py:381
  34.5 30.5 %collective-permute-start.1 = (bf16[208,1024]{1,0:T(8,128)(2,1)S(1)}, bf16[208,1024]{1,0:T(8,128)(2,1)S(1)}, u32[]{:S(2)}, u32[]{:S(2)}) collective-permute-start(bf16[208,1024]{1,0:T(8,128)(2,1)S(1)} %get-tuple-element.19), channel_id=1, source_target_pairs={{0,32},{16,48},{32,0},{48,16},{1,33},{17,49},{33,1},{49,17},{2,34}... | collective-permute-start | bytes 1277960 | tf_op jit(solution)/shard_map/ppermute | solution.py:381
  38.1 37.9 %collective-permute-start.2 = (bf16[208,1024]{1,0:T(8,128)(2,1)S(1)}, bf16[208,1024]{1,0:T(8,128)(2,1)S(1)}, u32[]{:S(2)}, u32[]{:S(2)}) collective-permute-start(bf16[208,1024]{1,0:T(8,128)(2,1)S(1)} %get-tuple-element.20), channel_id=1, source_target_pairs={{0,48},{16,32},{32,16},{48,0},{1,49},{17,33},{33,17},{49,1},{2,50}... | collective-permute-start | bytes 1277960 | tf_op jit(solution)/shard_map/ppermute | solution.py:381
  65.0 0.8 copy-start.8
  76.1 0.8 copy-start.10
  76.8 1.0 copy-start.9
  77.9 1.0 copy-start.11
  83.7 0.8 copy-start.12
  106.0 2.2 copy-start
  108.2 1.0 copy-start.13
  109.2 25.4 %copy-start.1 = (bf16[8,512,512]{2,1,0:T(8,128)(2,1)S(1)}, bf16[8,512,512]{2,1,0:T(8,128)(2,1)}, u32[]{:S(2)}) copy-start(bf16[8,512,512]{2,1,0:T(8,128)(2,1)} %all-gather.7.cloned.1.call-done) | copy-start | bytes 12582916
  193.9 18.6 %all-to-all-start.2 = ((f32[16,1,64]{2,1,0:T(1,128)}), f32[16,1,64]{2,1,0:T(1,128)S(1)}, u32[]{:S(2)}, u32[]{:S(2)}) async-start(f32[16,1,64]{2,1,0:T(1,128)} %bitcast.11), calls=%async_computation.2 | async-start | bytes 16384 | tf_op jit(solution)/shard_map/all_to_all | solution.py:440
Sparse Core Ops, SparseCore 0:
  10.4 80.8 all-gather.6

commit v3 on v2

--- a/solution.py
+++ b/solution.py
@@ -14,7 +14,7 @@
 NPROJ = 18
 SLOTS = 4
 ROWS = SLOTS * NPROJ
-SHARE = 208
+SHARE = 128
 GROUP = 4
 PART = 2 * NODES
 CENTER = 0.5
@@ -66,7 +66,17 @@
     return jnp.sum(jnp.where(iota(rows.shape, 0) == at, rows, 0.0), axis=0, keepdims=True)
 
 
-def open_kernel(atom_ref, v_ref, ham_ref, proj_ref, out_ref):
+def open_kernel(atom_ref, v_hbm, ham_hbm, proj_hbm, out_ref, v_ref, ham_ref, proj_ref, sems):
+    copies = [
+        pltpu.make_async_copy(v_hbm, v_ref, sems.at[0]),
+        pltpu.make_async_copy(proj_hbm, proj_ref, sems.at[1]),
+        pltpu.make_async_copy(ham_hbm.at[0, :LANES, :], ham_ref.at[0], sems.at[2]),
+        pltpu.make_async_copy(ham_hbm.at[1, NODES - LANES :, :], ham_ref.at[1], sems.at[3]),
+    ]
+    for copy in copies:
+        copy.start()
+    for copy in copies:
+        copy.wait()
     width = v_ref.shape[0]
     piece = width // GROUP
     place0, place1 = placers()
@@ -75,8 +85,8 @@
     v0 = v_ref[:, :NODES]
     v1 = v_ref[:, NODES:]
     coef = dot_nt(v0, p0) + dot_nt(v1, p1)
-    low = dot_nt(v0, ham_ref[0, :LANES, :])
-    high = dot_nt(v1, ham_ref[1, NODES - LANES :, :])
+    low = dot_nt(v0, ham_ref[0])
+    high = dot_nt(v1, ham_ref[1])
     face = jnp.where(low_lanes(width), low, high)
     edge = jnp.where(
         low_lanes(ROWS),
@@ -102,39 +112,24 @@
         out_ref[to, piece - 16 :, 3 * LANES :] = atoms
 
 
-def share_kernel(place_ref, v_ref, ham_ref, proj_ref, *out_refs):
-    me = place_ref[0]
-    piece = v_ref.shape[0] // GROUP
-    local = [dot_nt(v_ref[:, :NODES], ham_ref[0]), dot_nt(v_ref[:, NODES:], ham_ref[1])]
-    local = jnp.concatenate(local, axis=1).astype(BF16)
-    first = me == 0
-    half = FACE // 2
-    at = 2 * piece
+def share_kernel(v_hbm, proj_hbm, out_ref, proj_ref, sems):
+    piece = v_hbm.shape[0] // GROUP
+    copies = [pltpu.make_async_copy(proj_hbm, proj_ref, sems.at[GROUP])]
     for to in range(GROUP):
-        rows = slice(to * piece, (to + 1) * piece)
-        for r, out_ref in enumerate(out_refs):
-
-            @pl.when(jnp.bitwise_xor(me, r) == to)
-            def _():
-                out_ref[:piece, :] = v_ref[rows, :]
-                out_ref[piece:at, :] = local[rows]
-
-    for out_ref in out_refs:
-        for k in range(2):
-            lanes = slice(k * NODES, (k + 1) * NODES)
-
-            @pl.when(first)
-            def _():
-                out_ref[at : at + half, lanes] = ham_ref[0, k * half : (k + 1) * half, :]
-
-            @pl.when(jnp.logical_not(first))
-            def _():
-                start = NODES - FACE + k * half
-                out_ref[at : at + half, lanes] = ham_ref[1, start : start + half, :]
-
-            out_ref[at + half :, lanes] = jnp.concatenate(
-                [proj_ref[k], jnp.zeros((SHARE - at - half - ROWS, NODES), BF16)], axis=0
-            )
+        rows = pl.ds(to * piece, piece)
+        copies.append(
+            pltpu.make_async_copy(v_hbm.at[rows, :], out_ref.at[to, pl.ds(0, piece), :], sems.at[to])
+        )
+    for copy in copies:
+        copy.start()
+    copies[0].wait()
+    pad = jnp.zeros((SHARE - piece - ROWS, NODES), BF16)
+    for k in range(2):
+        rows = jnp.concatenate([proj_ref[k], pad], axis=0)
+        for to in range(GROUP):
+            out_ref[to, piece:, k * NODES : (k + 1) * NODES] = rows
+    for copy in copies[1:]:
+        copy.wait()
 
 
 def pack_kernel(in_ref, out_ref):
@@ -215,17 +210,49 @@
         )
 
 
-def write_message(new, proj_ref, edge_ref, message_ref):
+def fetch_hams(ham_refs, held_ref, sems):
+    copies = [
+        pltpu.make_async_copy(ham_refs[k // 2].at[k % 2], held_ref.at[k], sems.at[k])
+        for k in range(2 * GROUP)
+    ]
+    for copy in copies:
+        copy.start()
+    return copies
+
+
+def add_local(me, v_ref, held_ref, local_ref):
+    for r in range(GROUP):
+        part = jnp.bitwise_xor(me, r)
+        for cell in range(2):
+            lanes = slice(cell * NODES, (cell + 1) * NODES)
+            local_ref[part, :, lanes] += dot_nt(v_ref[part, :, lanes], held_ref[2 * r + cell])
+
+
+def write_message(me, new, held_ref, proj_ref, edge_ref, message_ref):
     for part in range(GROUP):
         lanes = slice(part * LANES, (part + 1) * LANES)
         message_ref[:, lanes] = dot_nt(new[part], proj_ref[part]).astype(BF16)
     ends = jnp.concatenate([new[0][:, :NODES], new[GROUP - 1][:, NODES:]], axis=1)
+    for r in range(GROUP):
+        part = jnp.bitwise_xor(me, r)
+
+        @pl.when(part == 0)
+        def _():
+            edge_ref[:FACE, :NODES] = held_ref[2 * r, :FACE, :]
+            edge_ref[:FACE, NODES:] = jnp.zeros((FACE, NODES), BF16)
+
+        @pl.when(part == GROUP - 1)
+        def _():
+            edge_ref[FACE:, :NODES] = jnp.zeros((FACE, NODES), BF16)
+            edge_ref[FACE:, NODES:] = held_ref[2 * r + 1, NODES - FACE :, :]
+
     message_ref[:, GROUP * LANES :] = dot_nt(ends, edge_ref[...]).astype(BF16)
 
 
 def first_kernel(factors, place_ref, coup_ref, got_ref, *refs):
-    shares = refs[:GROUP]
-    next_ref, message_ref, v_ref, proj_ref, near_ref, edge_ref, atoms_ref, local_ref = refs[GROUP:]
+    hams, refs = refs[:GROUP], refs[GROUP:]
+    share_hbm, next_ref, message_ref, v_ref, proj_ref, near_ref, atoms_ref = refs[:7]
+    local_ref, held_ref, edge_ref, share_ref, sems = refs[7:]
     groups = got_ref.shape[0]
     piece = v_ref.shape[1]
     me = place_ref[0]
@@ -233,28 +260,22 @@
     below = jnp.maximum(z - 1, 0)
     above = jnp.minimum(z + 1, groups - 1)
     wide = GROUP * LANES
-    half = FACE // 2
-    at = 2 * piece
+    shared = [
+        pltpu.make_async_copy(
+            share_hbm.at[part, pl.ds(piece, SHARE - piece), :], share_ref.at[part], sems.at[8 + part]
+        )
+        for part in range(GROUP)
+    ] + [
+        pltpu.make_async_copy(
+            share_hbm.at[part, pl.ds(0, piece), :], v_ref.at[part], sems.at[8 + GROUP + part]
+        )
+        for part in range(GROUP)
+    ]
+    for copy in shared:
+        copy.start()
+    copies = fetch_hams(hams, held_ref, sems)
 
     place0, place1 = placers()
-    edge_ref[...] = jnp.zeros(edge_ref.shape, BF16)
-    for r, share in enumerate(shares):
-        part = jnp.bitwise_xor(me, r)
-        v_ref[part] = share[:piece, :]
-        local_ref[part] = share[piece:at, :].astype(F32)
-        for cell, place in ((0, place0), (1, place1)):
-            lanes = slice(cell * NODES, (cell + 1) * NODES)
-            raw = share[at + half : at + half + ROWS, lanes]
-            proj_ref[part, :, lanes] = dot(place, raw).astype(BF16)
-        for k, end in ((0, 0), (1, GROUP - 1)):
-
-            @pl.when(part == end)
-            def _():
-                lanes = slice(k * NODES, (k + 1) * NODES)
-                row = k * FACE
-                edge_ref[row : row + half, lanes] = share[at : at + half, :NODES]
-                edge_ref[row + half : row + FACE, lanes] = share[at : at + half, NODES:]
-
     edge_at = wide + LANES
     for k, group, place in ((0, below, place1), (1, above, place0)):
         tail = got_ref[group, : ROWS - piece, edge_at + LANES :]
@@ -266,79 +287,98 @@
         for part in range(GROUP):
             lanes = slice(part * LANES, (part + 1) * LANES)
             atoms_ref[group : group + 1, lanes] = rows[part : part + 1]
-
     scaled = sum_coefs(place_ref, coup_ref, got_ref, atoms_ref)
+
+    for copy in shared:
+        copy.wait()
     for part in range(GROUP):
-        local_ref[part] = local_ref[part] + dot(scaled[part], proj_ref[part])
+        for cell, place in ((0, place0), (1, place1)):
+            lanes = slice(cell * NODES, (cell + 1) * NODES)
+            proj_ref[part, :, lanes] = dot(place, share_ref[part, :ROWS, lanes]).astype(BF16)
+        local_ref[part] = dot(scaled[part], proj_ref[part])
+    for copy in copies:
+        copy.wait()
+    add_local(me, v_ref, held_ref, local_ref)
     add_faces(place_ref, got_ref, near_ref, scaled, local_ref)
     gain, _ = factors[0]
     new = []
     for part in range(GROUP):
         new.append(((local_ref[part] - CENTER * v_ref[part].astype(F32)) * gain).astype(BF16))
         next_ref[part] = new[part]
-    write_message(new, proj_ref, edge_ref, message_ref)
-
-
-def step_kernel(degree, factors, place_ref, coup_ref, got_ref, v_ref, old_ref, ham_ref, *refs):
+    write_message(me, new, held_ref, proj_ref, edge_ref, message_ref)
+
+
+def step_kernel(degree, factors, place_ref, coup_ref, got_ref, *refs):
     last = degree == DEGREE - 1
-    proj_ref, near_ref, edge_ref, atoms_ref = refs[:4]
-    refs = refs[4:]
+    hams, refs = refs[:GROUP], refs[GROUP:]
+    v_ref, old_ref, proj_ref, near_ref, atoms_ref = refs[:5]
+    refs = refs[5:]
     if last:
-        occ_ref, next_ref, local_ref, held_ref, sems = refs
+        occ_ref, density_ref, *next_refs = refs[: 2 + GROUP]
+        refs = refs[2 + GROUP :]
     else:
-        next_ref, message_ref, local_ref, held_ref, sems = refs
+        next_ref, message_ref = refs[:2]
+        refs = refs[2:]
+    local_ref, held_ref, edge_ref, sems = refs
     piece = v_ref.shape[1]
-    copies = [
-        pltpu.make_async_copy(ham_ref.at[k // 2, k % 2], held_ref.at[k], sems.at[k])
-        for k in range(2 * GROUP)
-    ]
-    for copy in copies:
-        copy.start()
+    me = place_ref[0]
+    copies = fetch_hams(hams, held_ref, sems)
     scaled = sum_coefs(place_ref, coup_ref, got_ref, atoms_ref)
+    for part in range(GROUP):
+        local_ref[part] = dot(scaled[part], proj_ref[part])
     for copy in copies:
         copy.wait()
-    for part in range(GROUP):
-        for cell in range(2):
-            lanes = slice(cell * NODES, (cell + 1) * NODES)
-            local = dot_nt(v_ref[part, :, lanes], held_ref[2 * part + cell])
-            local_ref[part, :, lanes] = local + dot(scaled[part], proj_ref[part, :, lanes])
+    add_local(me, v_ref, held_ref, local_ref)
     add_faces(place_ref, got_ref, near_ref, scaled, local_ref)
 
     gain, back = factors[degree]
-    new = []
-    for part in range(GROUP):
+    if not last:
+        new = []
+        for part in range(GROUP):
+            now = v_ref[part].astype(F32)
+            image = (local_ref[part] - CENTER * now) * gain - back * old_ref[part].astype(F32)
+            new.append(image.astype(BF16))
+            next_ref[part] = new[part]
+        write_message(me, new, held_ref, proj_ref, edge_ref, message_ref)
+        return
+    weight = jnp.broadcast_to(pick(occ_ref[...], me), (8, piece))
+    for r in range(GROUP):
+        part = jnp.bitwise_xor(me, r)
         now = v_ref[part].astype(F32)
         image = (local_ref[part] - CENTER * now) * gain - back * old_ref[part].astype(F32)
-        new.append(image.astype(BF16))
-        next_ref[part, :piece, :] = new[part]
-    if not last:
-        write_message(new, proj_ref, edge_ref, message_ref)
-        return
-    weight = jnp.broadcast_to(pick(occ_ref[...], place_ref[0]), (8, piece))
-    row = iota((16, PART), 0)
-    for part in range(GROUP):
-        values = new[part].astype(F32)
+        image = image.astype(BF16)
+        next_refs[r][...] = image
+        values = image.astype(F32)
         sums = jnp.dot(
             weight, values * values, precision=lax.Precision.HIGHEST, preferred_element_type=F32
         )[:1]
-        high = sums.astype(BF16).astype(F32)
-        both = jnp.where(row == 0, high, jnp.where(row == 1, sums - high, 0.0))
-        next_ref[part, piece:, :] = both.astype(BF16)
-
-
-def density_kernel(in_ref, out_ref):
-    total = jnp.zeros((2, PART), F32)
-    for part in range(GROUP):
-        total = total + in_ref[part, :2, :].astype(F32)
-    total = total[:1] + total[1:]
-    for k in range(PART // LANES):
-        tile = total[:, k * LANES : (k + 1) * LANES]
-        out_ref[2 * k : 2 * k + 1, :] = tile[:, :FACE]
-        out_ref[2 * k + 1 : 2 * k + 2, :] = tile[:, FACE:]
+        for k in range(PART // LANES):
+            tile = sums[:, k * LANES : (k + 1) * LANES]
+            density_ref[part, 2 * k : 2 * k + 1, :] = tile[:, :FACE]
+            density_ref[part, 2 * k + 1 : 2 * k + 2, :] = tile[:, FACE:]
+
+
+def join_kernel(place_ref, *refs):
+    ins, (out_ref, sems) = refs[:GROUP], refs[GROUP:]
+    piece = ins[0].shape[0]
+    copies = []
+    for r in range(GROUP):
+        start = pl.multiple_of(jnp.bitwise_xor(place_ref[0], r) * piece, 16)
+        copies.append(
+            pltpu.make_async_copy(ins[r], out_ref.at[pl.ds(start, piece), :], sems.at[r])
+        )
+    for copy in copies:
+        copy.start()
+    for copy in copies:
+        copy.wait()
 
 
 def vmem():
     return pl.BlockSpec(memory_space=pltpu.VMEM)
+
+
+def hbm():
+    return pl.BlockSpec(memory_space=pltpu.HBM)
 
 
 def smem():
@@ -354,43 +394,65 @@
     piece = width // GROUP
     y_hi = lax.axis_size("yh")
     spread = lax.axis_size("x") * y_hi
-    params = pltpu.CompilerParams(vmem_limit_bytes=32 * 1024 * 1024)
-    call = functools.partial(pl.pallas_call, compiler_params=params, interpret=interpret)
+
+    def call(kernel, megabytes=32, **kw):
+        params = pltpu.CompilerParams(vmem_limit_bytes=megabytes * 1024 * 1024)
+        return pl.pallas_call(kernel, compiler_params=params, interpret=interpret, **kw)
+
     me = 2 * lax.axis_index("yl") + lax.axis_index("c")
     place = jnp.stack([me, lax.axis_index("z")]).astype(jnp.int32)
     coup = jnp.tile(coupling, (1, LANES // NPROJ + 1))[:, :LANES]
     occ = occupancy.reshape(GROUP, piece)
     near = ("yl", "c")
 
-    ham = lax.all_gather(cell_ham, near)
+    dma = pltpu.SemaphoreType.DMA
+
+    swap = [(0, 1), (1, 0)]
+    ring = 2 * y_hi
+    spot = lambda y, core: ((y % 2) * 2 + core) * y_hi + y // 2
+    across = [(spot(y, c), spot((y + 1 - 2 * c) % ring, c)) for y in range(ring) for c in (0, 1)]
+    ham_y = lax.ppermute(cell_ham, ("yl", "c", "yh"), across)
+    hams = [cell_ham, lax.ppermute(cell_ham, "c", swap), ham_y, lax.ppermute(ham_y, "c", swap)]
+
     v_t = states.T
     opened = call(
         open_kernel,
+        megabytes=60,
         out_shape=shape((GROUP, piece, 4 * LANES)),
-        in_specs=[smem(), vmem(), vmem(), vmem()],
+        in_specs=[smem()] + [hbm()] * 3,
         out_specs=vmem(),
+        scratch_shapes=[
+            pltpu.VMEM((width, PART), BF16),
+            pltpu.VMEM((2, LANES, NODES), BF16),
+            pltpu.VMEM((2, ROWS, NODES), BF16),
+            dma((4,)),
+        ],
     )(slot_atom, v_t, cell_ham, projectors)
     opened = lax.all_to_all(opened, near, 0, 0)
     shares = call(
         share_kernel,
-        out_shape=[shape((SHARE, PART))] * GROUP,
-        in_specs=[smem(), vmem(), vmem(), vmem()],
-        out_specs=[vmem()] * GROUP,
-    )(place, v_t, cell_ham, projectors)
-    shares = [shares[0]] + [
-        lax.ppermute(shares[r], near, [(k, k ^ r) for k in range(GROUP)]) for r in (1, 2, 3)
-    ]
+        megabytes=60,
+        out_shape=shape((GROUP, SHARE, PART)),
+        in_specs=[hbm(), hbm()],
+        out_specs=vmem(),
+        scratch_shapes=[pltpu.VMEM((2, ROWS, NODES), BF16), dma((GROUP + 1,))],
+    )(v_t, projectors)
     message = call(
         pack_kernel,
         out_shape=shape((piece, 7 * LANES)),
         in_specs=[vmem()],
         out_specs=vmem(),
     )(opened)
+    shares = lax.all_to_all(shares, near, 0, 0)
 
     factors = chebyshev_factors()
     state_shape = shape((GROUP, piece, PART))
     message_shape = shape((piece, 5 * LANES))
-    scratch = pltpu.VMEM((GROUP, piece, PART), F32)
+    scratch = [
+        pltpu.VMEM((GROUP, piece, PART), F32),
+        pltpu.VMEM((2 * GROUP, NODES, NODES), BF16),
+        pltpu.VMEM((LANES, PART), BF16),
+    ]
     got = lax.all_gather(message, "z")
     v, message, old, *kept = call(
         functools.partial(first_kernel, factors),
@@ -400,48 +462,46 @@
             state_shape,
             shape((GROUP, LANES, PART)),
             shape((2, LANES, LANES)),
-            shape((LANES, PART)),
             shape((LANES, GROUP * LANES), F32),
         ],
-        in_specs=[smem()] + [vmem()] * (2 + GROUP),
-        out_specs=[vmem()] * 7,
-        scratch_shapes=[scratch],
-    )(place, coup, got, *shares)
+        in_specs=[smem()] + [vmem()] * 2 + [hbm()] * (GROUP + 1),
+        out_specs=[vmem()] * 6,
+        scratch_shapes=scratch
+        + [pltpu.VMEM((GROUP, SHARE - piece, PART), BF16), dma((4 * GROUP,))],
+    )(place, coup, got, *hams, shares)
     for degree in range(1, DEGREE):
         got = lax.all_gather(message, "z")
         last = degree == DEGREE - 1
-        outs = [shape((GROUP, piece + 16, PART))] if last else [state_shape, message_shape]
+        outs = [state_shape, message_shape]
+        if last:
+            outs = [shape((GROUP, PART // FACE, FACE), F32)] + [shape((piece, PART))] * GROUP
         ends = [occ] if last else []
         result = call(
             functools.partial(step_kernel, degree, factors),
             out_shape=outs,
-            in_specs=[smem()]
-            + [vmem()] * 4
-            + [pl.BlockSpec(memory_space=pl.ANY)]
-            + [vmem()] * (4 + len(ends)),
+            in_specs=[smem()] + [vmem()] * 2 + [hbm()] * GROUP + [vmem()] * (5 + len(ends)),
             out_specs=[vmem()] * len(outs),
-            scratch_shapes=[
-                scratch,
-                pltpu.VMEM((2 * GROUP, NODES, NODES), BF16),
-                pltpu.SemaphoreType.DMA((2 * GROUP,)),
-            ],
-        )(place, coup, got, v, old, ham, *kept, *ends)
-        old, v, message = v, result[0], result[-1]
-
-    final = lax.all_to_all(message, near, 0, 0)
-    filtered = final[:, :piece, :].reshape(width, PART).T
-    terms = call(
-        density_kernel,
-        out_shape=shape((PART // FACE, FACE), F32),
-        grid=(1,),
-        in_specs=[pl.BlockSpec((GROUP, 16, PART), lambda i: (0, piece // 16, 0))],
-        out_specs=pl.BlockSpec((PART // FACE, FACE), lambda i: (0, 0)),
-    )(final)
+            scratch_shapes=scratch + [dma((2 * GROUP,))],
+        )(place, coup, got, *hams, v, old, *kept, *ends)
+        old, v, message = v, result[0], result[1]
+
+    density, *pieces = result
+    pieces = [pieces[0]] + [
+        lax.ppermute(pieces[r], near, [(k, k ^ r) for k in range(GROUP)]) for r in (1, 2, 3)
+    ]
+    filtered = call(
+        join_kernel,
+        out_shape=shape((width, PART)),
+        in_specs=[smem()] + [hbm()] * GROUP,
+        out_specs=hbm(),
+        scratch_shapes=[dma((GROUP,))],
+    )(place, *pieces)
+    parts = GROUP * spread
     terms = lax.all_to_all(
-        terms.reshape(spread, PART // spread), ("x", "yh"), 0, 0, tiled=True
+        density.reshape(parts, GROUP * PART // parts), near + ("x", "yh"), 0, 0, tiled=True
     )
     density = jnp.sum(terms, axis=0) / (width * spread)
-    return filtered, density
+    return filtered.T, density
 
 
 def build(mesh, interpret=False):

time: 221 us -> 199 us (0.900)
  starting transfers between devices: 31.5 us -> 67 us
  blocking collectives: 113 us -> 86.1 us
  between operations: 14.2 us -> 1 us
  waiting for transfers between devices: 19 us -> 6.43 us
  local copies, waits for them, and re-layouts: 15.4 us -> 3.27 us
  Pallas kernels: 26 us -> 33.8 us
    all_to_all x1 -> x2, starting transfers between devices: 9.8 us -> 38.9 us  [the longest x1 30.9 us: shards(): lax.all_to_all(density.reshape(parts, GROUP * PART // parts), near + ('x'...]
    all_to_all x1 -> x0, blocking collectives: 27 us -> none  [shards(): final = lax.all_to_all(message, near, 0, 0)]
    unnamed x35 -> x13, local copies, waits for them, and re-layouts: 14.5 us -> 3.16 us
    ppermute x3 -> x6, starting transfers between devices: 7.85 us -> 18.2 us  [the longest x3 7.87 us: shards(): lax.ppermute(pieces[r], near, [(k, k ^ r) for k in range(GROUP)])]
    ppermute x3 -> x6, waiting for transfers between devices: 10.3 us -> 2.66 us  [the longest x3 2.66 us: shards(): lax.ppermute(pieces[r], near, [(k, k ^ r) for k in range(GROUP)])]
    all_to_all x1 -> x2, waiting for transfers between devices: 8.04 us -> 1.44 us  [the longest x1 1.43 us: shards(): lax.all_to_all(density.reshape(parts, GROUP * PART // parts), near + ('x'...]
    all_to_all x1, starting transfers between devices: 13.8 us -> 9.85 us  [shards(): opened = lax.all_to_all(opened, near, 0, 0)]
    pallas_call x3, Pallas kernels: 16.8 us -> 20.6 us  [shards(): call(functools.partial(step_kernel, degree, factors), out_shape=outs, in_...]
  transfers between devices with their start and end apart: 6 -> 9, of which waited for: 2 -> 3; matrix products, arithmetic and copies ran while one was open for 0% -> 0% of each run, Pallas kernels for 4% -> 3%
where the time goes in v3:
time: 199 us; the launch traced here: 198 us
  blocking collectives  86.1 us (43%)
  starting transfers between devices  67 us (34%)
  Pallas kernels  33.8 us (17%)
  waiting for transfers between devices  6.43 us (3%)
  local copies, waits for them, and re-layouts  3.27 us (2%)
    all_gather x4, blocking collectives, shards(): got = lax.all_gather(message, 'z')  86.1 us
    all_to_all x1, starting transfers between devices, shards(): lax.all_to_all(density.reshape(parts, GROUP * PART // parts), near + ('x'...  30.9 us
    pallas_call x3, Pallas kernels, shards(): call(functools.partial(step_kernel, degree, factors), out_shape=outs, in_...  20.6 us
    all_to_all x1, starting transfers between devices, shards(): opened = lax.all_to_all(opened, near, 0, 0)  9.85 us
    all_to_all x1, starting transfers between devices, shards(): shares = lax.all_to_all(shares, near, 0, 0)  8.05 us
    ppermute x3, starting transfers between devices, shards(): lax.ppermute(pieces[r], near, [(k, k ^ r) for k in range(GROUP)])  7.87 us
    pallas_call x1, Pallas kernels, shards(): call(functools.partial(first_kernel, factors), out_shape=[state_shape, me...  6.67 us
    ppermute x1, starting transfers between devices, shards(): ham_y = lax.ppermute(cell_ham, ('yl', 'c', 'yh'), across)  5.93 us
  transfers between devices with their start and end apart: 9, of which 3 were waited for; matrix products, arithmetic and copies ran while one was open for 0% of the time, Pallas kernels for 3%

profile of v3, /device:TPU:1, one launch (start us, length us, event | category | flops | bytes accessed | tf_op | source)
XLA Modules:
  0.0 198.3 jit_solution(2852993424646392772)
XLA Ops:
  0.6 5.9 %collective-permute-start.1 = (bf16[2,512,512]{2,1,0:T(8,128)(2,1)}, bf16[2,512,512]{2,1,0:T(8,128)(2,1)S(1)}, u32[]{:S(2)}, u32[]{:S(2)}) collective-permute-start(bf16[2,512,512]{2,1,0:T(8,128)(2,1)} %refs_0_.7), channel_id=1, source_target_pairs={{0,32},{16,51},{32,1},{48,16},{1,33},{17,48},{33,2},{49,17},{2,34}... | collective-permute-start | bytes 3145736 | tf_op jit(solution)/shard_map/ppermute | solution.py:414
  6.6 3.1 %shard_map.77 = bf16[4,48,512]{2,1,0:T(8,128)(2,1)} custom-call(s32[2,4]{1,0:T(2,128)} %atom_ref.1, bf16[192,1024]{1,0:T(8,128)(2,1)} %bitcast.17, bf16[2,512,512]{2,1,0:T(8,128)(2,1)} %refs_0_.7, bf16[2,72,512]{2,1,0:T(8,128)(2,1)} %proj_hbm.3), custom_call_target="tpu_custom_call" | custom-call | tf_op jit(solution)/shard_map/pallas_call | solution.py:418
  9.6 9.9 %all-to-all-start = ((bf16[4,48,512]{2,1,0:T(8,128)(2,1)}), bf16[4,48,512]{2,1,0:T(8,128)(2,1)S(1)}, u32[]{:S(2)}, u32[]{:S(2)}) async-start(bf16[4,48,512]{2,1,0:T(8,128)(2,1)} %shard_map.77), calls=%async_computation | async-start | bytes 393216 | tf_op jit(solution)/shard_map/all_to_all | solution.py:431
  19.5 2.1 %shard_map.79 = bf16[4,128,1024]{2,1,0:T(8,128)(2,1)} custom-call(bf16[192,1024]{1,0:T(8,128)(2,1)} %bitcast.18, bf16[2,72,512]{2,1,0:T(8,128)(2,1)} %proj_hbm.3), custom_call_target="tpu_custom_call" | custom-call | tf_op jit(solution)/shard_map/pallas_call | solution.py:432
  21.6 2.3 %all-to-all-done.in_ref = bf16[4,48,512]{2,1,0:T(8,128)(2,1)S(1)} async-done(((bf16[4,48,512]{2,1,0:T(8,128)(2,1)}), bf16[4,48,512]{2,1,0:T(8,128)(2,1)S(1)}, u32[]{:S(2)}, u32[]{:S(2)}) %all-to-all-start) | async-done | bytes 196640 | tf_op jit(solution)/shard_map/all_to_all | solution.py:431
  24.0 8.0 %all-to-all-start.1 = ((bf16[4,128,1024]{2,1,0:T(8,128)(2,1)}), bf16[4,128,1024]{2,1,0:T(8,128)(2,1)}, u32[]{:S(2)}, u32[]{:S(2)}) async-start(bf16[4,128,1024]{2,1,0:T(8,128)(2,1)} %shard_map.79), calls=%async_computation.1 | async-start | bytes 2097152 | tf_op jit(solution)/shard_map/all_to_all | solution.py:446
  32.0 2.0 %collective-permute-start = (bf16[2,512,512]{2,1,0:T(8,128)(2,1)S(1)}, bf16[2,512,512]{2,1,0:T(8,128)(2,1)S(1)}, u32[]{:S(2)}, u32[]{:S(2)}) collective-permute-start(bf16[2,512,512]{2,1,0:T(8,128)(2,1)S(1)} %copy-done), channel_id=1, source_target_pairs={{0,16},{16,0},{1,17},{17,1},{2,18},{18,2},{3,19},{19,3},{4,20},{20... | collective-permute-start | bytes 3145736 | tf_op jit(solution)/shard_map/ppermute | solution.py:415
  34.1 2.4 %collective-permute-start.2 = (bf16[2,512,512]{2,1,0:T(8,128)(2,1)S(1)}, bf16[2,512,512]{2,1,0:T(8,128)(2,1)}, u32[]{:S(2)}, u32[]{:S(2)}) collective-permute-start(bf16[2,512,512]{2,1,0:T(8,128)(2,1)S(1)} %collective-permute-done.1.refs_2_), channel_id=1, source_target_pairs={{0,16},{16,0},{1,17},{17,1},{2,18},{18,2},{3,19},{19,3},{4,20},{20... | collective-permute-start | bytes 3145736 | tf_op jit(solution)/shard_map/ppermute | solution.py:415
  37.4 27.3 %all-gather = bf16[576,896]{1,0:T(8,128)(2,1)} all-gather(bf16[48,896]{1,0:T(8,128)(2,1)S(1)} %shard_map.78), channel_id=2, replica_groups=mesh['z'=12,'yl'=2,'c'=2,'x'=4,'yh'=4] {'z'}, dimensions={0}, use_global_device_ids=true | all-gather | bytes 1118208 | tf_op jit(solution)/shard_map/all_gather | solution.py:456
  64.8 1.2 copy-done.1
  66.0 6.7 %shard_map.80 = (bf16[4,48,1024]{2,1,0:T(8,128)(2,1)S(1)}, bf16[48,640]{1,0:T(8,128)(2,1)S(1)}, bf16[4,48,1024]{2,1,0:T(8,128)(2,1)S(1)}, bf16[4,128,1024]{2,1,0...) custom-call(s32[2]{0:T(128)S(1)} %pad_add_fusion.place_ref, f32[48,128]{1,0:T(8,128)S(1)} %copy.12.coup_ref, ...), custom_call_target="tpu_custom_call" | custom-call | tf_op jit(solution)/shard_map/pallas_call | solution.py:457
  72.7 19.9 %all-gather.1 = bf16[576,640]{1,0:T(8,128)(2,1)S(1)} all-gather(bf16[48,640]{1,0:T(8,128)(2,1)S(1)} %get-tuple-element.17), channel_id=3, replica_groups=mesh['z'=12,'yl'=2,'c'=2,'x'=4,'yh'=4] {'z'}, dimensions={0}, use_global_device_ids=true | all-gather | bytes 798720 | tf_op jit(solution)/shard_map/all_gather | solution.py:473
  92.6 6.5 %shard_map.81 = (bf16[4,48,1024]{2,1,0:T(8,128)(2,1)S(1)}, bf16[48,640]{1,0:T(8,128)(2,1)S(1)}) custom-call(s32[2]{0:T(128)S(1)} %pad_add_fusion.place_ref, f32[48,128]{1,0:T(8,128)S(1)} %copy.12.coup_ref, bf16[12,48,640]{2,1,0:T(8,128)(2,1)S(1)} %bitcast.15, bf16[2,512,512]{2,1,0:T(8,128)(2,1)S(1)} %copy-done, ...), custom_call_target="tpu_custom_call" | custom-call | tf_op jit(solution)/shard_map/pallas_call | solution.py:479
  99.1 19.9 %all-gather.2 = bf16[576,640]{1,0:T(8,128)(2,1)S(1)} all-gather(bf16[48,640]{1,0:T(8,128)(2,1)S(1)} %get-tuple-element.23), channel_id=4, replica_groups=mesh['z'=12,'yl'=2,'c'=2,'x'=4,'yh'=4] {'z'}, dimensions={0}, use_global_device_ids=true | all-gather | bytes 798720 | tf_op jit(solution)/shard_map/all_gather | solution.py:473
  118.9 6.7 %shard_map.82 = (bf16[4,48,1024]{2,1,0:T(8,128)(2,1)S(1)}, bf16[48,640]{1,0:T(8,128)(2,1)S(1)}) custom-call(s32[2]{0:T(128)S(1)} %pad_add_fusion.place_ref, f32[48,128]{1,0:T(8,128)S(1)} %copy.12.coup_ref, bf16[12,48,640]{2,1,0:T(8,128)(2,1)S(1)} %bitcast.16, bf16[2,512,512]{2,1,0:T(8,128)(2,1)S(1)} %copy-done, ...), custom_call_target="tpu_custom_call" | custom-call | tf_op jit(solution)/shard_map/pallas_call | solution.py:479
  125.6 19.0 %all-gather.3 = bf16[576,640]{1,0:T(8,128)(2,1)S(1)} all-gather(bf16[48,640]{1,0:T(8,128)(2,1)S(1)} %get-tuple-element.25), channel_id=5, replica_groups=mesh['z'=12,'yl'=2,'c'=2,'x'=4,'yh'=4] {'z'}, dimensions={0}, use_global_device_ids=true | all-gather | bytes 798720 | tf_op jit(solution)/shard_map/all_gather | solution.py:473
  144.6 7.4 %shard_map.83 = (f32[4,16,64]{2,1,0:T(8,128)}, bf16[48,1024]{1,0:T(8,128)(2,1)S(1)}, bf16[48,1024]{1,0:T(8,128)(2,1)S(1)}, bf16[48,1024]{1,0:T(8,128)(2,1)S(1)}, bf16[48,1024]{1,0:T(8,128)(2,1)S(1)}) custom-call(s32[2]{0:T(128)S(1)} %pad_add_fusion.place_ref, f32[48,128]{1,0:T(8,128)S(1)} %copy.12.coup_ref, bf16[12,48,640]{2,1,0:T(8,128)(2,1)S(1)} %bitcast.14, ...), custom_call_target="tpu_custom_call" | custom-call | tf_op jit(solution)/shard_map/pallas_call | solution.py:479
  153.3 30.9 %all-to-all-start.2 = ((f32[64,1,64]{2,1,0:T(1,128)}), f32[64,1,64]{2,1,0:T(1,128)S(1)}, u32[]{:S(2)}, u32[]{:S(2)}) async-start(f32[64,1,64]{2,1,0:T(1,128)} %bitcast.9), calls=%async_computation.2 | async-start | bytes 65536 | tf_op jit(solution)/shard_map/all_to_all | solution.py:500
  184.2 2.4 %collective-permute-start.3 = (bf16[48,1024]{1,0:T(8,128)(2,1)}, bf16[48,1024]{1,0:T(8,128)(2,1)S(1)}, u32[]{:S(2)}, u32[]{:S(2)}) collective-permute-start(bf16[48,1024]{1,0:T(8,128)(2,1)} %copy-done.3), channel_id=1, source_target_pairs={{0,16},{16,0},{32,48},{48,32},{1,17},{17,1},{33,49},{49,33},{2,18}... | collective-permute-start | bytes 294920 | tf_op jit(solution)/shard_map/ppermute | solution.py:490
  186.6 3.3 %collective-permute-start.4 = (bf16[48,1024]{1,0:T(8,128)(2,1)}, bf16[48,1024]{1,0:T(8,128)(2,1)S(1)}, u32[]{:S(2)}, u32[]{:S(2)}) collective-permute-start(bf16[48,1024]{1,0:T(8,128)(2,1)} %copy-done.2), channel_id=1, source_target_pairs={{0,32},{16,48},{32,0},{48,16},{1,33},{17,49},{33,1},{49,17},{2,34}... | collective-permute-start | bytes 294920 | tf_op jit(solution)/shard_map/ppermute | solution.py:490
  189.9 2.2 %collective-permute-start.5 = (bf16[48,1024]{1,0:T(8,128)(2,1)S(1)}, bf16[48,1024]{1,0:T(8,128)(2,1)S(1)}, u32[]{:S(2)}, u32[]{:S(2)}) collective-permute-start(bf16[48,1024]{1,0:T(8,128)(2,1)S(1)} %get-tuple-element.30), channel_id=1, source_target_pairs={{0,48},{16,32},{32,16},{48,0},{1,49},{17,33},{33,17},{49,1},{2,50}... | collective-permute-start | bytes 294920 | tf_op jit(solution)/shard_map/ppermute | solution.py:490
  192.1 1.4 all-to-all-done.2
  194.1 2.7 %collective-permute-done.5.refs_3_ = bf16[48,1024]{1,0:T(8,128)(2,1)S(1)} collective-permute-done((bf16[48,1024]{1,0:T(8,128)(2,1)S(1)}, bf16[48,1024]{1,0:T(8,128)(2,1)S(1)}, u32[]{:S(2)}, u32[]{:S(2)}) %collective-permute-start.5) | collective-permute-done | bytes 98336 | tf_op jit(solution)/shard_map/ppermute | solution.py:490
  196.8 1.3 shard_map.84
  (26 shorter events, 2.8 us)
Async XLA Ops:
  0.6 33.4 %collective-permute-start.1 = (bf16[2,512,512]{2,1,0:T(8,128)(2,1)}, bf16[2,512,512]{2,1,0:T(8,128)(2,1)S(1)}, u32[]{:S(2)}, u32[]{:S(2)}) collective-permute-start(bf16[2,512,512]{2,1,0:T(8,128)(2,1)} %refs_0_.7), channel_id=1, source_target_pairs={{0,32},{16,51},{32,1},{48,16},{1,33},{17,48},{33,2},{49,17},{2,34}... | collective-permute-start | bytes 3145736 | tf_op jit(solution)/shard_map/ppermute | solution.py:414
  9.6 14.3 %all-to-all-start = ((bf16[4,48,512]{2,1,0:T(8,128)(2,1)}), bf16[4,48,512]{2,1,0:T(8,128)(2,1)S(1)}, u32[]{:S(2)}, u32[]{:S(2)}) async-start(bf16[4,48,512]{2,1,0:T(8,128)(2,1)} %shard_map.77), calls=%async_computation | async-start | bytes 393216 | tf_op jit(solution)/shard_map/all_to_all | solution.py:431
  21.6 10.4 %copy-start = (bf16[2,512,512]{2,1,0:T(8,128)(2,1)S(1)}, bf16[2,512,512]{2,1,0:T(8,128)(2,1)}, u32[]{:S(2)}) copy-start(bf16[2,512,512]{2,1,0:T(8,128)(2,1)} %refs_0_.7) | copy-start | bytes 3145732
  24.0 40.8 %all-to-all-start.1 = ((bf16[4,128,1024]{2,1,0:T(8,128)(2,1)}), bf16[4,128,1024]{2,1,0:T(8,128)(2,1)}, u32[]{:S(2)}, u32[]{:S(2)}) async-start(bf16[4,128,1024]{2,1,0:T(8,128)(2,1)} %shard_map.79), calls=%async_computation.1 | async-start | bytes 2097152 | tf_op jit(solution)/shard_map/all_to_all | solution.py:446
  32.0 4.5 %copy-start.4 = (f32[48,18]{0,1:T(8,128)S(1)}, f32[48,18]{0,1:T(8,128)}, u32[]{:S(2)}) copy-start(f32[48,18]{0,1:T(8,128)} %param.10) | copy-start | bytes 10372
  32.0 32.8 %collective-permute-start = (bf16[2,512,512]{2,1,0:T(8,128)(2,1)S(1)}, bf16[2,512,512]{2,1,0:T(8,128)(2,1)S(1)}, u32[]{:S(2)}, u32[]{:S(2)}) collective-permute-start(bf16[2,512,512]{2,1,0:T(8,128)(2,1)S(1)} %copy-done), channel_id=1, source_target_pairs={{0,16},{16,0},{1,17},{17,1},{2,18},{18,2},{3,19},{19,3},{4,20},{20... | collective-permute-start | bytes 3145736 | tf_op jit(solution)/shard_map/ppermute | solution.py:415
  34.1 30.7 %collective-permute-start.2 = (bf16[2,512,512]{2,1,0:T(8,128)(2,1)S(1)}, bf16[2,512,512]{2,1,0:T(8,128)(2,1)}, u32[]{:S(2)}, u32[]{:S(2)}) collective-permute-start(bf16[2,512,512]{2,1,0:T(8,128)(2,1)S(1)} %collective-permute-done.1.refs_2_), channel_id=1, source_target_pairs={{0,16},{16,0},{1,17},{17,1},{2,18},{18,2},{3,19},{19,3},{4,20},{20... | collective-permute-start | bytes 3145736 | tf_op jit(solution)/shard_map/ppermute | solution.py:415
  36.6 0.7 copy-start.5
  64.8 1.2 copy-start.1
  152.0 0.6 copy-start.2
  152.7 0.6 copy-start.3
  153.3 40.2 %all-to-all-start.2 = ((f32[64,1,64]{2,1,0:T(1,128)}), f32[64,1,64]{2,1,0:T(1,128)S(1)}, u32[]{:S(2)}, u32[]{:S(2)}) async-start(f32[64,1,64]{2,1,0:T(1,128)} %bitcast.9), calls=%async_computation.2 | async-start | bytes 65536 | tf_op jit(solution)/shard_map/all_to_all | solution.py:500
  184.2 9.9 %collective-permute-start.3 = (bf16[48,1024]{1,0:T(8,128)(2,1)}, bf16[48,1024]{1,0:T(8,128)(2,1)S(1)}, u32[]{:S(2)}, u32[]{:S(2)}) collective-permute-start(bf16[48,1024]{1,0:T(8,128)(2,1)} %copy-done.3), channel_id=1, source_target_pairs={{0,16},{16,0},{32,48},{48,32},{1,17},{17,1},{33,49},{49,33},{2,18}... | collective-permute-start | bytes 294920 | tf_op jit(solution)/shard_map/ppermute | solution.py:490
  186.6 7.6 %collective-permute-start.4 = (bf16[48,1024]{1,0:T(8,128)(2,1)}, bf16[48,1024]{1,0:T(8,128)(2,1)S(1)}, u32[]{:S(2)}, u32[]{:S(2)}) collective-permute-start(bf16[48,1024]{1,0:T(8,128)(2,1)} %copy-done.2), channel_id=1, source_target_pairs={{0,32},{16,48},{32,0},{48,16},{1,33},{17,49},{33,1},{49,17},{2,34}... | collective-permute-start | bytes 294920 | tf_op jit(solution)/shard_map/ppermute | solution.py:490
  189.9 6.9 %collective-permute-start.5 = (bf16[48,1024]{1,0:T(8,128)(2,1)S(1)}, bf16[48,1024]{1,0:T(8,128)(2,1)S(1)}, u32[]{:S(2)}, u32[]{:S(2)}) collective-permute-start(bf16[48,1024]{1,0:T(8,128)(2,1)S(1)} %get-tuple-element.30), channel_id=1, source_target_pairs={{0,48},{16,32},{32,16},{48,0},{1,49},{17,33},{33,17},{49,1},{2,50}... | collective-permute-start | bytes 294920 | tf_op jit(solution)/shard_map/ppermute | solution.py:490

commit v4 on v3

v4 whole, which is shorter than its diff:
```python
import functools

import jax
import jax.numpy as jnp
from jax import lax
from jax.experimental import pallas as pl
from jax.experimental.pallas import tpu as pltpu
from jax.sharding import Mesh, PartitionSpec as P

FACE = 64
DEGREE = 4
LANES = 128
NODES = 512
NPROJ = 18
SLOTS = 4
ROWS = SLOTS * NPROJ
GROUP = 4
PART = 2 * NODES
PIECE = 48
BLOCKS = 8
PROJ = NPROJ * BLOCKS
SPAN = NPROJ * PIECE
WIDE = 7 * LANES
BODY = GROUP * BLOCKS
PADDED = 80
PACK = PART + 2 * PADDED
HEAD = 32
CENTER = 0.5
HALF_WIDTH = 1.5
LOW_EDGE = -1.2

BF16 = jnp.bfloat16
F32 = jnp.float32
NT = (((1,), (1,)), ((), ()))
TN = (((0,), (0,)), ((), ()))


def chebyshev_factors():
    sigma = HALF_WIDTH / (LOW_EDGE - CENTER)
    gamma = 2.0 / sigma
    factors = [(sigma / HALF_WIDTH, 0.0)]
    for _ in range(1, DEGREE):
        sigma_new = 1.0 / (gamma - sigma)
        factors.append((2.0 * sigma_new / HALF_WIDTH, sigma * sigma_new))
        sigma = sigma_new
    return factors


def iota(shape, dim):
    return lax.broadcasted_iota(jnp.int32, shape, dim)


def dot(a, b):
    return jnp.dot(a, b, preferred_element_type=F32)


def dot_nt(a, b):
    return lax.dot_general(a, b, NT, preferred_element_type=F32)


def dot_tn(a, b):
    return lax.dot_general(a, b, TN, preferred_element_type=F32)


def exact(a, b):
    return jnp.dot(a, b, precision=lax.Precision.HIGHEST, preferred_element_type=F32)


def placers():
    row = iota((PROJ, ROWS), 0)
    col = iota((PROJ, ROWS), 1)
    which = row // BLOCKS
    block = row % BLOCKS
    first = (block < SLOTS) & (col == block * NPROJ + which)
    slot = block - SLOTS + 1
    second = ((block == 0) & (col == which)) | (
        (block >= SLOTS) & (block < 2 * SLOTS - 1) & (col == slot * NPROJ + which)
    )
    return first.astype(F32).astype(BF16), second.astype(F32).astype(BF16)


def low_lanes(rows):
    return iota((rows, LANES), 1) < FACE


def pick(rows, at):
    return jnp.sum(jnp.where(iota(rows.shape, 0) == at, rows, 0.0), axis=0, keepdims=True)


def run(copies):
    for copy in copies:
        copy.start()
    return copies


def finish(copies):
    for copy in copies:
        copy.wait()


def tile(k):
    return slice(k * LANES, (k + 1) * LANES)


def eight(k):
    return slice(k * 8, (k + 1) * 8)


def open_kernel(atom_ref, v_hbm, ham_hbm, proj_hbm, out_ref, v_ref, ham_ref, proj_ref, wide_ref, sems):
    copies = run(
        [
            pltpu.make_async_copy(v_hbm, v_ref, sems.at[0]),
            pltpu.make_async_copy(proj_hbm, proj_ref, sems.at[1]),
            pltpu.make_async_copy(ham_hbm.at[0, :LANES, :], ham_ref.at[0], sems.at[2]),
            pltpu.make_async_copy(ham_hbm.at[1, NODES - LANES :, :], ham_ref.at[1], sems.at[3]),
        ]
    )
    place0, place1 = placers()
    wide_ref[...] = jnp.zeros(wide_ref.shape, F32)
    lane = iota((8, LANES), 1)
    atoms = jnp.full((8, LANES), -1, jnp.int32)
    for block in range(2 * SLOTS - 1):
        cell, slot = (0, block) if block < SLOTS else (1, block - SLOTS + 1)
        atoms = jnp.where(lane == block, atom_ref[cell, slot], atoms)
    atoms = atoms.astype(F32)
    finish(copies)
    width = v_ref.shape[0]
    p0 = dot(place0, proj_ref[0]).astype(BF16)
    p1 = dot(place1, proj_ref[1]).astype(BF16)
    v0 = v_ref[:, :NODES]
    v1 = v_ref[:, NODES:]
    coef = dot_nt(p0, v0) + dot_nt(p1, v1)
    face = jnp.where(low_lanes(width), dot_nt(v0, ham_ref[0]), dot_nt(v1, ham_ref[1]))
    edge = jnp.where(
        low_lanes(ROWS),
        proj_ref[0, :, :LANES].astype(F32),
        proj_ref[1, :, NODES - LANES :].astype(F32),
    )
    for to in range(GROUP):
        for i in range(NPROJ):
            wide_ref[to, :8, i * PIECE : (i + 1) * PIECE] = coef[
                eight(i), to * PIECE : (to + 1) * PIECE
            ]
        for k in range(PIECE // 8):
            wide_ref[to, 8:16, tile(k)] = face[eight(to * (PIECE // 8) + k)]
        wide_ref[to, 8:16, tile(6)] = atoms
        for k in range(8):
            wide_ref[to, 16:24, tile(k)] = edge[eight(k)]
        wide_ref[to, 24:32, :LANES] = edge[eight(8)]
        out_ref[to, :HEAD, :] = wide_ref[to].astype(BF16)
        out_ref[to, HEAD:, :] = v_ref[to * PIECE : (to + 1) * PIECE, :]


def share_kernel(ham_hbm, proj_hbm, out, proj_ref, pad_ref, sems):
    hams = run(
        [
            pltpu.make_async_copy(ham_hbm.at[k], out.at[pl.ds(k * NODES, NODES), :], sems.at[k])
            for k in range(2)
        ]
    )
    proj_in = run([pltpu.make_async_copy(proj_hbm, proj_ref, sems.at[2])])
    finish(proj_in)
    pad = jnp.zeros((PADDED - ROWS, NODES), BF16)
    for k in range(2):
        pad_ref[k * PADDED : (k + 1) * PADDED, :] = jnp.concatenate([proj_ref[k], pad], axis=0)
    projs = run([pltpu.make_async_copy(pad_ref, out.at[pl.ds(PART, 2 * PADDED), :], sems.at[3])])
    finish(hams + projs)


def place_face(face, wide_ref):
    wide_ref[:BODY, WIDE:] = face[:BODY]
    for k in range(PIECE - BODY):
        row = (k % GROUP) * BLOCKS + BLOCKS - 1
        wide_ref[row : row + 1, tile(k // GROUP)] = face[BODY + k : BODY + k + 1]


def read_face(got_ref, group):
    body = got_ref[group, :BODY, :].astype(F32)
    rows = [body[:, WIDE:]]
    for k in range(PIECE - BODY):
        row = (k % GROUP) * BLOCKS + BLOCKS - 1
        rows.append(body[row : row + 1, tile(k // GROUP)])
    return jnp.concatenate(rows, axis=0)


def pack_kernel(in_ref, out_ref, wide_ref):
    last = GROUP - 1
    low = low_lanes(8)
    wide_ref[...] = jnp.zeros(wide_ref.shape, F32)
    pieces = [in_ref[part, :HEAD, :].astype(F32) for part in range(GROUP)]
    both = lambda rows, k: jnp.where(low, pieces[0][rows, tile(k)], pieces[last][rows, tile(k)])
    lane = iota((8, LANES), 1)
    atoms = jnp.full((8, LANES), -1.0, F32)
    for part in range(GROUP):
        wide_ref[eight(part), :WIDE] = pieces[part][:8, :WIDE]
        own = pieces[part][8:16, tile(6)]
        if part:
            own = pltpu.roll(own, part * BLOCKS, 1)
        atoms = jnp.where(lane // BLOCKS == part, own, atoms)
    face = jnp.concatenate([both(slice(8, 16), k) for k in range(PIECE // 8)], axis=0)
    place_face(face, wide_ref)
    ninth = both(slice(24, 32), 0)
    for k in range(8):
        wide_ref[BODY:, tile(k)] = both(slice(16, 24), k)
        row = (k % GROUP) * BLOCKS + BLOCKS - 1
        wide_ref[row : row + 1, tile(4 + k // GROUP)] = ninth[k : k + 1]
    wide_ref[BLOCKS - 1 : BLOCKS, tile(6)] = atoms[:1]
    out_ref[...] = wide_ref[...].astype(BF16)


def beside(place_ref, groups):
    z = place_ref[1]
    return z, jnp.maximum(z - 1, 0), jnp.minimum(z + 1, groups - 1)


def choose(place_ref, coupling_ref, got_ref, pick_ref, factor_ref):
    groups = got_ref.shape[0]
    z, below, above = beside(place_ref, groups)
    lane = iota((8, LANES), 1)
    named = lambda group: jnp.broadcast_to(
        got_ref[group, :16, tile(6)].astype(F32)[BLOCKS - 1 : BLOCKS], (8, LANES)
    )
    shift = lambda x, by: pltpu.roll(x, by, 1) if by else x
    per = LANES // BODY
    tiles = []
    for start in range(0, groups, per):
        x = jnp.full((8, LANES), -1.0, F32)
        for k in range(min(per, groups - start)):
            x = jnp.where(lane // BODY == k, shift(named(start + k), k * BODY), x)
        tiles.append(x)
    mine = jnp.where(lane < BODY, named(z), -1.0)
    mine = jnp.where(lane // BLOCKS == GROUP, shift(named(below), BLOCKS), mine)
    mine = jnp.where(lane // BLOCKS == GROUP + 1, shift(named(above), BODY + BLOCKS), mine)
    mine = jnp.where(mine < 0, -2.0, mine)
    column = jnp.transpose(jnp.concatenate([mine] * (LANES // 8), axis=0))[:PIECE]
    for k, x in enumerate(tiles):
        match = column == jnp.concatenate([x] * (PIECE // 8), axis=0)
        pick_ref[:, tile(k)] = jnp.where(match, 1.0, 0.0).astype(BF16)
    count = coupling_ref.shape[0]
    atom = iota((PIECE, LANES), 1).astype(F32)
    owner = jnp.where(column == atom, 1.0, 0.0)[:, :count]
    expand = jnp.where(iota((NPROJ, WIDE), 1) // PIECE == iota((NPROJ, WIDE), 0), 1.0, 0.0)
    factor_ref[...] = exact(exact(owner, coupling_ref[...]), expand)


def sum_coefs(got_ref, pick_ref, factor_ref, scaled_ref):
    groups = got_ref.shape[0]
    blocks = jnp.concatenate([got_ref[group, :BODY, :WIDE] for group in range(groups)], axis=0)
    total = dot(pick_ref[:, : groups * BODY], blocks) * factor_ref[...]
    for i in range(NPROJ):
        column = total[:, i * PIECE : (i + 1) * PIECE]
        for k in range(GROUP + 2):
            scaled_ref[k, eight(i), :] = column[eight(k)]
    return [scaled_ref[k].astype(BF16) for k in range(GROUP + 2)]


def add_faces(place_ref, got_ref, near_ref, scaled, local_ref):
    groups = got_ref.shape[0]
    z, below, above = beside(place_ref, groups)
    low = low_lanes(PIECE)
    from_below = read_face(got_ref, below) + dot_tn(scaled[GROUP], near_ref[0])
    from_above = read_face(got_ref, above) + dot_tn(scaled[GROUP + 1], near_ref[1])
    from_below = from_below * (z > 0).astype(F32)
    from_above = from_above * (z < groups - 1).astype(F32)
    cells = [(part, cell * NODES) for part in range(GROUP) for cell in range(2)]
    heads = [local_ref[part, :, a : a + LANES] for part, a in cells]
    tails = [local_ref[part, :, a + NODES - LANES : a + NODES] for part, a in cells]
    for k, (part, a) in enumerate(cells):
        under = tails[k - 1] if k > 0 else from_below
        over = heads[k + 1] if k + 1 < len(cells) else from_above
        local_ref[part, :, a : a + LANES] = heads[k] + jnp.where(
            low, pltpu.roll(under, FACE, 1), 0.0
        )
        local_ref[part, :, a + NODES - LANES : a + NODES] = tails[k] + jnp.where(
            low, 0.0, pltpu.roll(over, FACE, 1)
        )


def fetch_hams(packs, held_ref, sems):
    return run(
        [
            pltpu.make_async_copy(
                packs[k // 2].at[pl.ds((k % 2) * NODES, NODES), :], held_ref.at[k], sems.at[k]
            )
            for k in range(2 * GROUP)
        ]
    )


def add_local(me, v_ref, held_ref, local_ref):
    for r in range(GROUP):
        part = jnp.bitwise_xor(me, r)
        for cell in range(2):
            lanes = slice(cell * NODES, (cell + 1) * NODES)
            local_ref[part, :, lanes] += dot_nt(v_ref[part, :, lanes], held_ref[2 * r + cell])


def write_message(me, new, held_ref, proj_ref, edge_ref, wide_ref, message_ref):
    for r in range(GROUP):
        part = jnp.bitwise_xor(me, r)

        @pl.when(part == 0)
        def _():
            edge_ref[:FACE, :NODES] = held_ref[2 * r, :FACE, :]
            edge_ref[:FACE, NODES:] = jnp.zeros((FACE, NODES), BF16)

        @pl.when(part == GROUP - 1)
        def _():
            edge_ref[FACE:, :NODES] = jnp.zeros((FACE, NODES), BF16)
            edge_ref[FACE:, NODES:] = held_ref[2 * r + 1, NODES - FACE :, :]

    ends = jnp.concatenate([new[0][:, :NODES], new[GROUP - 1][:, NODES:]], axis=1)
    face = dot_nt(ends, edge_ref[...])
    wide_ref[:, SPAN:WIDE] = jnp.zeros((BODY, WIDE - SPAN), F32)
    for part in range(GROUP):
        coef = dot_nt(proj_ref[part], new[part])
        for i in range(NPROJ):
            wide_ref[eight(part), i * PIECE : (i + 1) * PIECE] = coef[eight(i)]
    place_face(face, wide_ref)
    message_ref[...] = wide_ref[...].astype(BF16)


def first_kernel(factors, place_ref, coupling_ref, got_ref, open_hbm, *refs):
    packs, refs = refs[:GROUP], refs[GROUP:]
    next_ref, message_ref, v_ref, proj_ref, near_ref, pick_ref, factor_ref = refs[:7]
    local_ref, held_ref, edge_ref, wide_ref, scaled_ref, raw_ref, sems = refs[7:]
    groups = got_ref.shape[0]
    me = place_ref[0]
    _, below, above = beside(place_ref, groups)
    copies = []
    for r in range(GROUP):
        at = 2 * GROUP + 2 * r
        copies += [
            pltpu.make_async_copy(packs[r].at[pl.ds(PART, 2 * PADDED), :], raw_ref.at[r], sems.at[at]),
            pltpu.make_async_copy(
                open_hbm.at[r, pl.ds(HEAD, PIECE), :], v_ref.at[r], sems.at[at + 1]
            ),
        ]
    run(copies)
    hams = fetch_hams(packs, held_ref, sems)

    place0, place1 = placers()
    for k, group, place in ((0, below, place1), (1, above, place0)):
        rows = got_ref[group].astype(F32)
        raw = [rows[BODY:, tile(j)] for j in range(8)]
        for j in range(8):
            row = (j % GROUP) * BLOCKS + BLOCKS - 1
            raw.append(rows[row : row + 1, tile(4 + j // GROUP)])
        near_ref[k] = dot(place, jnp.concatenate(raw, axis=0).astype(BF16)).astype(BF16)
    choose(place_ref, coupling_ref, got_ref, pick_ref, factor_ref)
    scaled = sum_coefs(got_ref, pick_ref, factor_ref, scaled_ref)

    finish(copies)
    for r in range(GROUP):
        part = jnp.bitwise_xor(me, r)
        for cell, place in ((0, place0), (1, place1)):
            raw = raw_ref[r, cell * PADDED : (cell + 1) * PADDED, :][:ROWS]
            lanes = slice(cell * NODES, (cell + 1) * NODES)
            proj_ref[part, :, lanes] = dot(place, raw).astype(BF16)
    for part in range(GROUP):
        local_ref[part] = dot_tn(scaled[part], proj_ref[part])
    finish(hams)
    add_local(me, v_ref, held_ref, local_ref)
    add_faces(place_ref, got_ref, near_ref, scaled, local_ref)
    gain, _ = factors[0]
    new = []
    for part in range(GROUP):
        new.append(((local_ref[part] - CENTER * v_ref[part].astype(F32)) * gain).astype(BF16))
        next_ref[part] = new[part]
    write_message(me, new, held_ref, proj_ref, edge_ref, wide_ref, message_ref)


def step_kernel(degree, factors, place_ref, got_ref, *refs):
    last = degree == DEGREE - 1
    packs, refs = refs[:GROUP], refs[GROUP:]
    v_ref, old_ref, proj_ref, near_ref, pick_ref, factor_ref = refs[:6]
    refs = refs[6:]
    if last:
        occ_ref, density_ref, *next_refs = refs[: 2 + GROUP]
        refs = refs[2 + GROUP :]
    else:
        next_ref, message_ref = refs[:2]
        refs = refs[2:]
    local_ref, held_ref, edge_ref, wide_ref, scaled_ref, sems = refs
    me = place_ref[0]
    hams = fetch_hams(packs, held_ref, sems)
    scaled = sum_coefs(got_ref, pick_ref, factor_ref, scaled_ref)
    for part in range(GROUP):
        local_ref[part] = dot_tn(scaled[part], proj_ref[part])
    finish(hams)
    add_local(me, v_ref, held_ref, local_ref)
    add_faces(place_ref, got_ref, near_ref, scaled, local_ref)

    gain, back = factors[degree]

    def image(part):
        now = v_ref[part].astype(F32)
        value = (local_ref[part] - CENTER * now) * gain - back * old_ref[part].astype(F32)
        return value.astype(BF16)

    if not last:
        new = [image(part) for part in range(GROUP)]
        for part in range(GROUP):
            next_ref[part] = new[part]
        write_message(me, new, held_ref, proj_ref, edge_ref, wide_ref, message_ref)
        return
    weight = jnp.transpose(jnp.broadcast_to(pick(occ_ref[...], me), (LANES, LANES)))[:PIECE]
    for r in range(GROUP):
        part = jnp.bitwise_xor(me, r)
        new = image(part)
        next_refs[r][...] = new
        values = new.astype(F32)
        for k in range(PART // LANES):
            term = values[:, tile(k)]
            sums = jnp.sum(term * term * weight, axis=0, keepdims=True)
            density_ref[part, 2 * k : 2 * k + 1, :] = sums[:, :FACE]
            density_ref[part, 2 * k + 1 : 2 * k + 2, :] = sums[:, FACE:]


def join_kernel(place_ref, *refs):
    ins, (out_ref, sems) = refs[:GROUP], refs[GROUP:]
    copies = []
    for r in range(GROUP):
        start = pl.multiple_of(jnp.bitwise_xor(place_ref[0], r) * PIECE, 16)
        copies.append(
            pltpu.make_async_copy(ins[r], out_ref.at[pl.ds(start, PIECE), :], sems.at[r])
        )
    run(copies)
    finish(copies)


def vmem():
    return pl.BlockSpec(memory_space=pltpu.VMEM)


def hbm():
    return pl.BlockSpec(memory_space=pltpu.HBM)


def smem():
    return pl.BlockSpec(memory_space=pltpu.SMEM)


def shape(dims, dtype=BF16):
    return jax.ShapeDtypeStruct(dims, dtype)


def shards(interpret, states, cell_ham, projectors, slot_atom, coupling, occupancy):
    width = states.shape[1]
    groups = lax.axis_size("z")
    spread = lax.axis_size("x") * lax.axis_size("yh")
    dma = pltpu.SemaphoreType.DMA
    near = ("yl", "c")
    ring = 2 * lax.axis_size("yh")

    def call(kernel, megabytes=24, **kw):
        params = pltpu.CompilerParams(vmem_limit_bytes=megabytes * 1024 * 1024)
        return pl.pallas_call(kernel, compiler_params=params, interpret=interpret, **kw)

    me = 2 * lax.axis_index("yl") + lax.axis_index("c")
    place = jnp.stack([me, lax.axis_index("z")]).astype(jnp.int32)
    occ = jnp.pad(occupancy.reshape(GROUP, PIECE), ((0, 0), (0, LANES - PIECE)))
    v_t = states.T
    opened = call(
        open_kernel,
        megabytes=60,
        out_shape=shape((GROUP, HEAD + PIECE, PART)),
        in_specs=[smem()] + [hbm()] * 3,
        out_specs=vmem(),
        scratch_shapes=[
            pltpu.VMEM((width, PART), BF16),
            pltpu.VMEM((2, LANES, NODES), BF16),
            pltpu.VMEM((2, ROWS, NODES), BF16),
            pltpu.VMEM((GROUP, HEAD, PART), F32),
            dma((4,)),
        ],
    )(slot_atom, v_t, cell_ham, projectors)
    opened = lax.all_to_all(opened, near, 0, 0)
    pack = call(
        share_kernel,
        megabytes=60,
        out_shape=shape((PACK, NODES)),
        in_specs=[hbm()] * 2,
        out_specs=hbm(),
        scratch_shapes=[
            pltpu.VMEM((2, ROWS, NODES), BF16),
            pltpu.VMEM((2 * PADDED, NODES), BF16),
            dma((4,)),
        ],
    )(cell_ham, projectors)
    message = call(
        pack_kernel,
        out_shape=shape((BODY + 8, PART)),
        in_specs=[vmem()],
        out_specs=vmem(),
        scratch_shapes=[pltpu.VMEM((BODY + 8, PART), F32)],
    )(opened)
    spot = lambda y, core: ((y % 2) * 2 + core) * (ring // 2) + y // 2

    def across(flip):
        return [
            (spot(y, c), spot((y + 1 - 2 * c) % ring, c ^ flip)) for y in range(ring) for c in (0, 1)
        ]

    beside_core = lax.ppermute(pack, "c", [(0, 1), (1, 0)])
    late, message = lax.optimization_barrier((pack, message))
    axes = ("yl", "c", "yh")
    packs = [
        pack,
        beside_core,
        lax.ppermute(late, axes, across(0)),
        lax.ppermute(late, axes, across(1)),
    ]

    factors = chebyshev_factors()
    state_shape = shape((GROUP, PIECE, PART))
    message_shape = shape((BODY, PART))
    scratch = [
        pltpu.VMEM((GROUP, PIECE, PART), F32),
        pltpu.VMEM((2 * GROUP, NODES, NODES), BF16),
        pltpu.VMEM((LANES, PART), BF16),
        pltpu.VMEM((BODY, PART), F32),
        pltpu.VMEM((GROUP + 2, PROJ, PIECE), F32),
    ]
    got = lax.all_gather(message, "z")
    v, message, old, *kept = call(
        functools.partial(first_kernel, factors),
        out_shape=[
            state_shape,
            message_shape,
            state_shape,
            shape((GROUP, PROJ, PART)),
            shape((2, PROJ, LANES)),
            shape((PIECE, -(-groups * BODY // LANES) * LANES)),
            shape((PIECE, WIDE), F32),
        ],
        in_specs=[smem()] + [vmem()] * 2 + [hbm()] * (GROUP + 1),
        out_specs=[vmem()] * 7,
        scratch_shapes=scratch
        + [pltpu.VMEM((GROUP, 2 * PADDED, NODES), BF16), dma((4 * GROUP,))],
    )(place, coupling, got, opened, *packs)
    for degree in range(1, DEGREE):
        got = lax.all_gather(message, "z")
        last = degree == DEGREE - 1
        outs = [state_shape, message_shape]
        if last:
            outs = [shape((GROUP, PART // FACE, FACE), F32)] + [shape((PIECE, PART))] * GROUP
        ends = [occ] if last else []
        result = call(
            functools.partial(step_kernel, degree, factors),
            out_shape=outs,
            in_specs=[smem(), vmem()] + [hbm()] * GROUP + [vmem()] * (6 + len(ends)),
            out_specs=[vmem()] * len(outs),
            scratch_shapes=scratch + [dma((2 * GROUP,))],
        )(place, got, *packs, v, old, *kept, *ends)
        old, v, message = v, result[0], result[1]

    density, *pieces = result
    pieces = [pieces[0]] + [
        lax.ppermute(pieces[r], near, [(k, k ^ r) for k in range(GROUP)]) for r in (1, 2, 3)
    ]
    filtered = call(
        join_kernel,
        out_shape=shape((width, PART)),
        in_specs=[smem()] + [hbm()] * GROUP,
        out_specs=hbm(),
        scratch_shapes=[dma((GROUP,))],
    )(place, *pieces)
    parts = GROUP * spread
    terms = lax.all_to_all(
        density.reshape(parts, GROUP * PART // parts), near + ("x", "yh"), 0, 0, tiled=True
    )
    density = jnp.sum(terms, axis=0) / (width * spread)
    return filtered.T, density


def build(mesh, interpret=False):
    part = ("z", "yl", "c")
    group = ("x", "yh")
    return jax.shard_map(
        functools.partial(shards, interpret),
        mesh=mesh,
        in_specs=(
            P(part, group),
            P(part, None, None),
            P(part, None, None),
            P(part, None),
            P(),
            P(group),
        ),
        out_specs=(P(part, group), P(part + group)),
        check_vma=False,
    )


def solution(mesh):
    count, groups = mesh.shape["mesh"], mesh.shape["state"]
    devices = mesh.devices.reshape(count // GROUP, 2, 2, groups // 4, 4)
    return build(Mesh(devices, ("z", "yl", "c", "x", "yh")))
```

time: 199 us -> 211 us (1.060)
  Pallas kernels: 33.8 us -> 58.3 us
  starting transfers between devices: 67 us -> 56.5 us
  blocking collectives: 86.1 us -> 89.7 us
  local copies, waits for them, and re-layouts: 3.27 us -> 0.19 us
  waiting for transfers between devices: 6.43 us -> 4.1 us
    pallas_call x3, Pallas kernels: 5.21 us -> 36.3 us  [the longest x1 32.9 us: shards(): call(share_kernel, megabytes=60, out_shape=shape((PACK, NODES)), in_specs...]
    all_to_all x1 -> x0, starting transfers between devices: 8.05 us -> none  [shards(): shares = lax.all_to_all(shares, near, 0, 0)]
    pallas_call x3, Pallas kernels: 20.6 us -> 14.9 us  [shards(): call(functools.partial(step_kernel, degree, factors), out_shape=outs, in_...]
    all_to_all x1, starting transfers between devices: 30.9 us -> 25.4 us  [shards(): lax.all_to_all(density.reshape(parts, GROUP * PART // parts), near + ('x'...]
    all_to_all x1, starting transfers between devices: 9.85 us -> 14 us  [shards(): opened = lax.all_to_all(opened, near, 0, 0)]
    all_gather x4, blocking collectives: 86.1 us -> 89.7 us  [shards(): got = lax.all_gather(message, 'z')]
    unnamed x13 -> x7, local copies, waits for them, and re-layouts: 3.16 us -> 0.1 us
    all_to_all x1, waiting for transfers between devices: 2.33 us -> 0.01 us  [shards(): opened = lax.all_to_all(opened, near, 0, 0)]
  transfers between devices with their start and end apart: 9 -> 8, of which waited for: 3 -> 2; matrix products, arithmetic and copies ran while one was open for 0% -> 0% of each run, Pallas kernels for 3% -> 16%
where the time goes in v4:
time: 211 us; the launch traced here: 210 us
  blocking collectives  89.7 us (43%)
  Pallas kernels  58.3 us (28%)
  starting transfers between devices  56.5 us (27%)
  waiting for transfers between devices  4.1 us (2%)
    all_gather x4, blocking collectives, shards(): got = lax.all_gather(message, 'z')  89.7 us
    pallas_call x1, Pallas kernels, shards(): call(share_kernel, megabytes=60, out_shape=shape((PACK, NODES)), in_specs...  32.9 us
    all_to_all x1, starting transfers between devices, shards(): lax.all_to_all(density.reshape(parts, GROUP * PART // parts), near + ('x'...  25.4 us
    pallas_call x3, Pallas kernels, shards(): call(functools.partial(step_kernel, degree, factors), out_shape=outs, in_...  14.9 us
    all_to_all x1, starting transfers between devices, shards(): opened = lax.all_to_all(opened, near, 0, 0)  14 us
    ppermute x3, starting transfers between devices, shards(): lax.ppermute(pieces[r], near, [(k, k ^ r) for k in range(GROUP)])  7.87 us
    pallas_call x1, Pallas kernels, shards(): call(functools.partial(first_kernel, factors), out_shape=[state_shape, me...  5.8 us
    ppermute x1, starting transfers between devices, shards(): lax.ppermute(late, axes, across(1))  5.18 us
  transfers between devices with their start and end apart: 8, of which 2 were waited for; matrix products, arithmetic and copies ran while one was open for 0% of the time, Pallas kernels for 16%

profile of v4, /device:TPU:1, one launch (start us, length us, event | category | flops | bytes accessed | tf_op | source)
XLA Modules:
  0.0 210.3 jit_solution(9966869553221833706)
XLA Ops:
  0.6 3.3 %shard_map.78 = bf16[4,80,1024]{2,1,0:T(8,128)(2,1)} custom-call(s32[2,4]{1,0:T(2,128)} %atom_ref.1, bf16[192,1024]{1,0:T(8,128)(2,1)} %bitcast.16, bf16[2,512,512]{2,1,0:T(8,128)(2,1)} %ham_hbm.3, bf16[2,72,512]{2,1,0:T(8,128)(2,1)} %proj_hbm.3), custom_call_target="tpu_custom_call" | custom-call | tf_op jit(solution)/shard_map/pallas_call | solution.py:464
  4.0 14.0 %all-to-all-start = ((bf16[4,80,1024]{2,1,0:T(8,128)(2,1)}), bf16[4,80,1024]{2,1,0:T(8,128)(2,1)S(1)}, u32[]{:S(2)}, u32[]{:S(2)}) async-start(bf16[4,80,1024]{2,1,0:T(8,128)(2,1)} %shard_map.78), calls=%async_computation | async-start | bytes 1310720 | tf_op jit(solution)/shard_map/all_to_all | solution.py:478
  18.0 32.9 %shard_map.77.refs_0_ = bf16[1184,512]{1,0:T(8,128)(2,1)} custom-call(bf16[2,512,512]{2,1,0:T(8,128)(2,1)} %ham_hbm.3, bf16[2,72,512]{2,1,0:T(8,128)(2,1)} %proj_hbm.3), custom_call_target="tpu_custom_call" | custom-call | tf_op jit(solution)/shard_map/pallas_call | solution.py:479
  50.9 2.1 %collective-permute-start = (bf16[1184,512]{1,0:T(8,128)(2,1)}, bf16[1184,512]{1,0:T(8,128)(2,1)S(1)}, u32[]{:S(2)}, u32[]{:S(2)}) collective-permute-start(bf16[1184,512]{1,0:T(8,128)(2,1)} %shard_map.77.refs_0_), channel_id=1, source_target_pairs={{0,16},{16,0},{1,17},{17,1},{2,18},{18,2},{3,19},{19,3},{4,20},{20... | collective-permute-start | bytes 3637256 | tf_op jit(solution)/shard_map/ppermute | solution.py:505
  53.1 1.9 collective-permute-start.1
  55.0 5.2 %collective-permute-start.2 = (bf16[1184,512]{1,0:T(8,128)(2,1)}, bf16[1184,512]{1,0:T(8,128)(2,1)}, u32[]{:S(2)}, u32[]{:S(2)}) collective-permute-start(bf16[1184,512]{1,0:T(8,128)(2,1)} %shard_map.77.refs_0_), channel_id=1, source_target_pairs={{0,48},{16,35},{32,17},{48,0},{1,49},{17,32},{33,18},{49,1},{2,50}... | collective-permute-start | bytes 3637256 | tf_op jit(solution)/shard_map/ppermute | solution.py:512
  60.2 0.1 copy.9.coupling_ref
  60.5 26.6 %all-gather = bf16[480,1024]{1,0:T(8,128)(2,1)S(1)} all-gather(bf16[40,1024]{1,0:T(8,128)(2,1)S(1)} %shard_map.79), channel_id=2, replica_groups=mesh['z'=12,'yl'=2,'c'=2,'x'=4,'yh'=4] {'z'}, dimensions={0}, use_global_device_ids=true | all-gather | bytes 1064960 | tf_op jit(solution)/shard_map/all_gather | solution.py:525
  87.1 5.8 %shard_map.80 = (bf16[4,48,1024]{2,1,0:T(8,128)(2,1)S(1)}, bf16[32,1024]{1,0:T(8,128)(2,1)S(1)}, bf16[4,48,1024]{2,1,0:T(8,128)(2,1)S(1)}, bf16[4,144,1024]{2,1,...) custom-call(s32[2]{0:T(128)S(1)} %pad_add_fusion.place_ref, ...), custom_call_target="tpu_custom_call" | custom-call | tf_op jit(solution)/shard_map/pallas_call | solution.py:526
  92.9 23.4 %all-gather.1 = bf16[384,1024]{1,0:T(8,128)(2,1)S(1)} all-gather(bf16[32,1024]{1,0:T(8,128)(2,1)S(1)} %get-tuple-element.22), channel_id=3, replica_groups=mesh['z'=12,'yl'=2,'c'=2,'x'=4,'yh'=4] {'z'}, dimensions={0}, use_global_device_ids=true | all-gather | bytes 851968 | tf_op jit(solution)/shard_map/all_gather | solution.py:543
  116.3 4.7 %shard_map.81 = (bf16[4,48,1024]{2,1,0:T(8,128)(2,1)S(1)}, bf16[32,1024]{1,0:T(8,128)(2,1)S(1)}) custom-call(s32[2]{0:T(128)S(1)} %pad_add_fusion.place_ref, bf16[12,32,1024]{2,1,0:T(8,128)(2,1)S(1)} %bitcast.13, bf16[1184,512]{1,0:T(8,128)(2,1)S(1)} %copy-done, bf16[1184,512]{1,0:T(8,128)(2,1)S(1)} %collective-permute-done.refs_1_, ...), custom_call_target="tpu_custom_call" | custom-call | tf_op jit(solution)/shard_map/pallas_call | solution.py:549
  121.0 19.9 %all-gather.2 = bf16[384,1024]{1,0:T(8,128)(2,1)S(1)} all-gather(bf16[32,1024]{1,0:T(8,128)(2,1)S(1)} %get-tuple-element.29), channel_id=4, replica_groups=mesh['z'=12,'yl'=2,'c'=2,'x'=4,'yh'=4] {'z'}, dimensions={0}, use_global_device_ids=true | all-gather | bytes 851968 | tf_op jit(solution)/shard_map/all_gather | solution.py:543
  140.9 4.7 %shard_map.82 = (bf16[4,48,1024]{2,1,0:T(8,128)(2,1)S(1)}, bf16[32,1024]{1,0:T(8,128)(2,1)S(1)}) custom-call(s32[2]{0:T(128)S(1)} %pad_add_fusion.place_ref, bf16[12,32,1024]{2,1,0:T(8,128)(2,1)S(1)} %bitcast.14, bf16[1184,512]{1,0:T(8,128)(2,1)S(1)} %copy-done, bf16[1184,512]{1,0:T(8,128)(2,1)S(1)} %collective-permute-done.refs_1_, ...), custom_call_target="tpu_custom_call" | custom-call | tf_op jit(solution)/shard_map/pallas_call | solution.py:549
  145.6 19.9 %all-gather.3 = bf16[384,1024]{1,0:T(8,128)(2,1)S(1)} all-gather(bf16[32,1024]{1,0:T(8,128)(2,1)S(1)} %get-tuple-element.31), channel_id=5, replica_groups=mesh['z'=12,'yl'=2,'c'=2,'x'=4,'yh'=4] {'z'}, dimensions={0}, use_global_device_ids=true | all-gather | bytes 851968 | tf_op jit(solution)/shard_map/all_gather | solution.py:543
  165.5 5.4 %shard_map.83 = (f32[4,16,64]{2,1,0:T(8,128)}, bf16[48,1024]{1,0:T(8,128)(2,1)S(1)}, bf16[48,1024]{1,0:T(8,128)(2,1)S(1)}, bf16[48,1024]{1,0:T(8,128)(2,1)S(1)}, bf16[48,1024]{1,0:T(8,128)(2,1)S(1)}) custom-call(s32[2]{0:T(128)S(1)} %pad_add_fusion.place_ref, bf16[12,32,1024]{2,1,0:T(8,128)(2,1)S(1)} %bitcast.12, bf16[1184,512]{1,0:T(8,128)(2,1)S(1)} %copy-done, ...), custom_call_target="tpu_custom_call" | custom-call | tf_op jit(solution)/shard_map/pallas_call | solution.py:549
  170.9 25.4 %all-to-all-start.1 = ((f32[64,1,64]{2,1,0:T(1,128)}), f32[64,1,64]{2,1,0:T(1,128)S(1)}, u32[]{:S(2)}, u32[]{:S(2)}) async-start(f32[64,1,64]{2,1,0:T(1,128)} %bitcast.9), calls=%async_computation.1 | async-start | bytes 65536 | tf_op jit(solution)/shard_map/all_to_all | solution.py:570
  196.4 2.4 %collective-permute-start.3 = (bf16[48,1024]{1,0:T(8,128)(2,1)S(1)}, bf16[48,1024]{1,0:T(8,128)(2,1)S(1)}, u32[]{:S(2)}, u32[]{:S(2)}) collective-permute-start(bf16[48,1024]{1,0:T(8,128)(2,1)S(1)} %get-tuple-element.34), channel_id=1, source_target_pairs={{0,16},{16,0},{32,48},{48,32},{1,17},{17,1},{33,49},{49,33},{2,18}... | collective-permute-start | bytes 294920 | tf_op jit(solution)/shard_map/ppermute | solution.py:560
  198.7 3.3 %collective-permute-start.4 = (bf16[48,1024]{1,0:T(8,128)(2,1)S(1)}, bf16[48,1024]{1,0:T(8,128)(2,1)S(1)}, u32[]{:S(2)}, u32[]{:S(2)}) collective-permute-start(bf16[48,1024]{1,0:T(8,128)(2,1)S(1)} %get-tuple-element.35), channel_id=1, source_target_pairs={{0,32},{16,48},{32,0},{48,16},{1,33},{17,49},{33,1},{49,17},{2,34}... | collective-permute-start | bytes 294920 | tf_op jit(solution)/shard_map/ppermute | solution.py:560
  202.0 2.2 %collective-permute-start.5 = (bf16[48,1024]{1,0:T(8,128)(2,1)S(1)}, bf16[48,1024]{1,0:T(8,128)(2,1)S(1)}, u32[]{:S(2)}, u32[]{:S(2)}) collective-permute-start(bf16[48,1024]{1,0:T(8,128)(2,1)S(1)} %get-tuple-element.36), channel_id=1, source_target_pairs={{0,48},{16,32},{32,16},{48,0},{1,49},{17,33},{33,17},{49,1},{2,50}... | collective-permute-start | bytes 294920 | tf_op jit(solution)/shard_map/ppermute | solution.py:560
  204.3 1.4 all-to-all-done.1
  205.6 0.1 reduce_sum.9
  205.7 0.5 broadcast_multiply_fusion
  206.2 2.7 %collective-permute-done.5.refs_3_ = bf16[48,1024]{1,0:T(8,128)(2,1)S(1)} collective-permute-done((bf16[48,1024]{1,0:T(8,128)(2,1)S(1)}, bf16[48,1024]{1,0:T(8,128)(2,1)S(1)}, u32[]{:S(2)}, u32[]{:S(2)}) %collective-permute-start.5) | collective-permute-done | bytes 98336 | tf_op jit(solution)/shard_map/ppermute | solution.py:560
  209.0 1.3 shard_map.84
  (16 shorter events, 0.3 us)
Async XLA Ops:
  4.0 49.0 %all-to-all-start = ((bf16[4,80,1024]{2,1,0:T(8,128)(2,1)}), bf16[4,80,1024]{2,1,0:T(8,128)(2,1)S(1)}, u32[]{:S(2)}, u32[]{:S(2)}) async-start(bf16[4,80,1024]{2,1,0:T(8,128)(2,1)} %shard_map.78), calls=%async_computation | async-start | bytes 1310720 | tf_op jit(solution)/shard_map/all_to_all | solution.py:478
  18.0 42.2 %copy-start.1 = (f32[48,18]{0,1:T(8,128)S(1)}, f32[48,18]{0,1:T(8,128)}, u32[]{:S(2)}) copy-start(f32[48,18]{0,1:T(8,128)} %param.10) | copy-start | bytes 10372
  18.0 42.3 %copy-start.2 = (f32[192]{0:T(256)S(1)}, f32[192]{0:T(256)}, u32[]{:S(2)}) copy-start(f32[192]{0:T(256)} %param.11) | copy-start | bytes 2308
  50.9 36.2 %copy-start = (bf16[1184,512]{1,0:T(8,128)(2,1)S(1)}, bf16[1184,512]{1,0:T(8,128)(2,1)}, u32[]{:S(2)}) copy-start(bf16[1184,512]{1,0:T(8,128)(2,1)} %shard_map.77.refs_0_) | copy-start | bytes 3637252
  50.9 36.2 %collective-permute-start = (bf16[1184,512]{1,0:T(8,128)(2,1)}, bf16[1184,512]{1,0:T(8,128)(2,1)S(1)}, u32[]{:S(2)}, u32[]{:S(2)}) collective-permute-start(bf16[1184,512]{1,0:T(8,128)(2,1)} %shard_map.77.refs_0_), channel_id=1, source_target_pairs={{0,16},{16,0},{1,17},{17,1},{2,18},{18,2},{3,19},{19,3},{4,20},{20... | collective-permute-start | bytes 3637256 | tf_op jit(solution)/shard_map/ppermute | solution.py:505
  53.1 34.0 %collective-permute-start.1 = (bf16[1184,512]{1,0:T(8,128)(2,1)}, bf16[1184,512]{1,0:T(8,128)(2,1)}, u32[]{:S(2)}, u32[]{:S(2)}) collective-permute-start(bf16[1184,512]{1,0:T(8,128)(2,1)} %shard_map.77.refs_0_), channel_id=1, source_target_pairs={{0,32},{16,51},{32,1},{48,16},{1,33},{17,48},{33,2},{49,17},{2,34}... | collective-permute-start | bytes 3637256 | tf_op jit(solution)/shard_map/ppermute | solution.py:511
  55.0 32.1 %collective-permute-start.2 = (bf16[1184,512]{1,0:T(8,128)(2,1)}, bf16[1184,512]{1,0:T(8,128)(2,1)}, u32[]{:S(2)}, u32[]{:S(2)}) collective-permute-start(bf16[1184,512]{1,0:T(8,128)(2,1)} %shard_map.77.refs_0_), channel_id=1, source_target_pairs={{0,48},{16,35},{32,17},{48,0},{1,49},{17,32},{33,18},{49,1},{2,50}... | collective-permute-start | bytes 3637256 | tf_op jit(solution)/shard_map/ppermute | solution.py:512
  170.9 34.7 %all-to-all-start.1 = ((f32[64,1,64]{2,1,0:T(1,128)}), f32[64,1,64]{2,1,0:T(1,128)S(1)}, u32[]{:S(2)}, u32[]{:S(2)}) async-start(f32[64,1,64]{2,1,0:T(1,128)} %bitcast.9), calls=%async_computation.1 | async-start | bytes 65536 | tf_op jit(solution)/shard_map/all_to_all | solution.py:570
  196.4 9.9 %collective-permute-start.3 = (bf16[48,1024]{1,0:T(8,128)(2,1)S(1)}, bf16[48,1024]{1,0:T(8,128)(2,1)S(1)}, u32[]{:S(2)}, u32[]{:S(2)}) collective-permute-start(bf16[48,1024]{1,0:T(8,128)(2,1)S(1)} %get-tuple-element.34), channel_id=1, source_target_pairs={{0,16},{16,0},{32,48},{48,32},{1,17},{17,1},{33,49},{49,33},{2,18}... | collective-permute-start | bytes 294920 | tf_op jit(solution)/shard_map/ppermute | solution.py:560
  198.7 7.5 %collective-permute-start.4 = (bf16[48,1024]{1,0:T(8,128)(2,1)S(1)}, bf16[48,1024]{1,0:T(8,128)(2,1)S(1)}, u32[]{:S(2)}, u32[]{:S(2)}) collective-permute-start(bf16[48,1024]{1,0:T(8,128)(2,1)S(1)} %get-tuple-element.35), channel_id=1, source_target_pairs={{0,32},{16,48},{32,0},{48,16},{1,33},{17,49},{33,1},{49,17},{2,34}... | collective-permute-start | bytes 294920 | tf_op jit(solution)/shard_map/ppermute | solution.py:560
  202.0 6.9 %collective-permute-start.5 = (bf16[48,1024]{1,0:T(8,128)(2,1)S(1)}, bf16[48,1024]{1,0:T(8,128)(2,1)S(1)}, u32[]{:S(2)}, u32[]{:S(2)}) collective-permute-start(bf16[48,1024]{1,0:T(8,128)(2,1)S(1)} %get-tuple-element.36), channel_id=1, source_target_pairs={{0,48},{16,32},{32,16},{48,0},{1,49},{17,33},{33,17},{49,1},{2,50}... | collective-permute-start | bytes 294920 | tf_op jit(solution)/shard_map/ppermute | solution.py:560

commit v5 on v4

--- a/solution.py
+++ b/solution.py
@@ -151,20 +151,18 @@
         out_ref[to, HEAD:, :] = v_ref[to * PIECE : (to + 1) * PIECE, :]
 
 
-def share_kernel(ham_hbm, proj_hbm, out, proj_ref, pad_ref, sems):
-    hams = run(
-        [
-            pltpu.make_async_copy(ham_hbm.at[k], out.at[pl.ds(k * NODES, NODES), :], sems.at[k])
-            for k in range(2)
-        ]
-    )
-    proj_in = run([pltpu.make_async_copy(proj_hbm, proj_ref, sems.at[2])])
-    finish(proj_in)
+def share_kernel(ham_hbm, proj_hbm, out_ref, proj_ref, sems):
+    copies = [
+        pltpu.make_async_copy(ham_hbm.at[k], out_ref.at[pl.ds(k * NODES, NODES), :], sems.at[k])
+        for k in range(2)
+    ]
+    copies = run([pltpu.make_async_copy(proj_hbm, proj_ref, sems.at[2])] + copies)
+    copies[0].wait()
     pad = jnp.zeros((PADDED - ROWS, NODES), BF16)
     for k in range(2):
-        pad_ref[k * PADDED : (k + 1) * PADDED, :] = jnp.concatenate([proj_ref[k], pad], axis=0)
-    projs = run([pltpu.make_async_copy(pad_ref, out.at[pl.ds(PART, 2 * PADDED), :], sems.at[3])])
-    finish(hams + projs)
+        start = PART + k * PADDED
+        out_ref[start : start + PADDED, :] = jnp.concatenate([proj_ref[k], pad], axis=0)
+    finish(copies[1:])
 
 
 def place_face(face, wide_ref):
@@ -481,12 +479,8 @@
         megabytes=60,
         out_shape=shape((PACK, NODES)),
         in_specs=[hbm()] * 2,
-        out_specs=hbm(),
-        scratch_shapes=[
-            pltpu.VMEM((2, ROWS, NODES), BF16),
-            pltpu.VMEM((2 * PADDED, NODES), BF16),
-            dma((4,)),
-        ],
+        out_specs=vmem(),
+        scratch_shapes=[pltpu.VMEM((2, ROWS, NODES), BF16), dma((3,))],
     )(cell_ham, projectors)
     message = call(
         pack_kernel,

time: 211 us -> 184 us (0.87)
  Pallas kernels: 58.3 us -> 27.8 us
  waiting for transfers between devices: 4.1 us -> 9.34 us
    pallas_call x1, Pallas kernels: 32.9 us -> 2.36 us  [shards(): call(share_kernel, megabytes=60, out_shape=shape((PACK, NODES)), in_specs...]
    all_to_all x1, waiting for transfers between devices: 0.01 us -> 4.9 us  [shards(): opened = lax.all_to_all(opened, near, 0, 0)]
  transfers between devices with their start and end apart: 8 -> 8, of which waited for: 2 -> 4; matrix products, arithmetic and copies ran while one was open for 0% -> 0% of each run, Pallas kernels for 16% -> 1%
where the time goes in v5:
time: 184 us; the launch traced here: 183 us
  blocking collectives  89 us (48%)
  starting transfers between devices  55.7 us (30%)
  Pallas kernels  27.8 us (15%)
  waiting for transfers between devices  9.34 us (5%)
    all_gather x4, blocking collectives, shards(): got = lax.all_gather(message, 'z')  89 us
    all_to_all x1, starting transfers between devices, shards(): lax.all_to_all(density.reshape(parts, GROUP * PART // parts), near + ('x'...  24.2 us
    pallas_call x3, Pallas kernels, shards(): call(functools.partial(step_kernel, degree, factors), out_shape=outs, in_...  14.9 us
    all_to_all x1, starting transfers between devices, shards(): opened = lax.all_to_all(opened, near, 0, 0)  14 us
    ppermute x3, starting transfers between devices, shards(): lax.ppermute(pieces[r], near, [(k, k ^ r) for k in range(GROUP)])  7.87 us
    pallas_call x1, Pallas kernels, shards(): call(functools.partial(first_kernel, factors), out_shape=[state_shape, me...  5.81 us
    ppermute x1, starting transfers between devices, shards(): lax.ppermute(late, axes, across(1))  5.61 us
    all_to_all x1, waiting for transfers between devices, shards(): opened = lax.all_to_all(opened, near, 0, 0)  4.9 us
  transfers between devices with their start and end apart: 8, of which 4 were waited for; matrix products, arithmetic and copies ran while one was open for 0% of the time, Pallas kernels for 1%

profile of v5, /device:TPU:1, one launch (start us, length us, event | category | flops | bytes accessed | tf_op | source)
XLA Modules:
  0.0 183.4 jit_solution(11567379066352408708)
XLA Ops:
  0.6 3.3 %shard_map.78 = bf16[4,80,1024]{2,1,0:T(8,128)(2,1)} custom-call(s32[2,4]{1,0:T(2,128)} %atom_ref.1, bf16[192,1024]{1,0:T(8,128)(2,1)} %bitcast.16, bf16[2,512,512]{2,1,0:T(8,128)(2,1)} %ham_hbm.3, bf16[2,72,512]{2,1,0:T(8,128)(2,1)} %proj_hbm.3), custom_call_target="tpu_custom_call" | custom-call | tf_op jit(solution)/shard_map/pallas_call | solution.py:462
  4.0 14.0 %all-to-all-start = ((bf16[4,80,1024]{2,1,0:T(8,128)(2,1)}), bf16[4,80,1024]{2,1,0:T(8,128)(2,1)S(1)}, u32[]{:S(2)}, u32[]{:S(2)}) async-start(bf16[4,80,1024]{2,1,0:T(8,128)(2,1)} %shard_map.78), calls=%async_computation | async-start | bytes 1310720 | tf_op jit(solution)/shard_map/all_to_all | solution.py:476
  18.0 2.4 %shard_map.77.refs_0_ = bf16[1184,512]{1,0:T(8,128)(2,1)} custom-call(bf16[2,512,512]{2,1,0:T(8,128)(2,1)} %ham_hbm.3, bf16[2,72,512]{2,1,0:T(8,128)(2,1)} %proj_hbm.3), custom_call_target="tpu_custom_call" | custom-call | tf_op jit(solution)/shard_map/pallas_call | solution.py:477
  20.3 2.1 %collective-permute-start = (bf16[1184,512]{1,0:T(8,128)(2,1)}, bf16[1184,512]{1,0:T(8,128)(2,1)S(1)}, u32[]{:S(2)}, u32[]{:S(2)}) collective-permute-start(bf16[1184,512]{1,0:T(8,128)(2,1)} %shard_map.77.refs_0_), channel_id=1, source_target_pairs={{0,16},{16,0},{1,17},{17,1},{2,18},{18,2},{3,19},{19,3},{4,20},{20... | collective-permute-start | bytes 3637256 | tf_op jit(solution)/shard_map/ppermute | solution.py:499
  22.4 4.9 %all-to-all-done.in_ref.open_hbm = bf16[4,80,1024]{2,1,0:T(8,128)(2,1)S(1)} async-done(((bf16[4,80,1024]{2,1,0:T(8,128)(2,1)}), bf16[4,80,1024]{2,1,0:T(8,128)(2,1)S(1)}, u32[]{:S(2)}, u32[]{:S(2)}) %all-to-all-start) | async-done | bytes 655392 | tf_op jit(solution)/shard_map/all_to_all | solution.py:476
  27.4 1.9 %collective-permute-start.1 = (bf16[1184,512]{1,0:T(8,128)(2,1)}, bf16[1184,512]{1,0:T(8,128)(2,1)}, u32[]{:S(2)}, u32[]{:S(2)}) collective-permute-start(bf16[1184,512]{1,0:T(8,128)(2,1)} %shard_map.77.refs_0_), channel_id=1, source_target_pairs={{0,32},{16,51},{32,1},{48,16},{1,33},{17,48},{33,2},{49,17},{2,34}... | collective-permute-start | bytes 3637256 | tf_op jit(solution)/shard_map/ppermute | solution.py:505
  29.3 5.6 %collective-permute-start.2 = (bf16[1184,512]{1,0:T(8,128)(2,1)}, bf16[1184,512]{1,0:T(8,128)(2,1)}, u32[]{:S(2)}, u32[]{:S(2)}) collective-permute-start(bf16[1184,512]{1,0:T(8,128)(2,1)} %shard_map.77.refs_0_), channel_id=1, source_target_pairs={{0,48},{16,35},{32,17},{48,0},{1,49},{17,32},{33,18},{49,1},{2,50}... | collective-permute-start | bytes 3637256 | tf_op jit(solution)/shard_map/ppermute | solution.py:506
  35.2 25.0 %all-gather = bf16[480,1024]{1,0:T(8,128)(2,1)S(1)} all-gather(bf16[40,1024]{1,0:T(8,128)(2,1)S(1)} %shard_map.79), channel_id=2, replica_groups=mesh['z'=12,'yl'=2,'c'=2,'x'=4,'yh'=4] {'z'}, dimensions={0}, use_global_device_ids=true | all-gather | bytes 1064960 | tf_op jit(solution)/shard_map/all_gather | solution.py:519
  60.2 0.3 collective-permute-done.2.refs_3_
  60.6 5.8 %shard_map.80 = (bf16[4,48,1024]{2,1,0:T(8,128)(2,1)S(1)}, bf16[32,1024]{1,0:T(8,128)(2,1)S(1)}, bf16[4,48,1024]{2,1,0:T(8,128)(2,1)S(1)}, bf16[4,144,1024]{2,1,...) custom-call(s32[2]{0:T(128)S(1)} %pad_add_fusion.place_ref, ...), custom_call_target="tpu_custom_call" | custom-call | tf_op jit(solution)/shard_map/pallas_call | solution.py:520
  66.4 23.9 %all-gather.1 = bf16[384,1024]{1,0:T(8,128)(2,1)S(1)} all-gather(bf16[32,1024]{1,0:T(8,128)(2,1)S(1)} %get-tuple-element.22), channel_id=3, replica_groups=mesh['z'=12,'yl'=2,'c'=2,'x'=4,'yh'=4] {'z'}, dimensions={0}, use_global_device_ids=true | all-gather | bytes 851968 | tf_op jit(solution)/shard_map/all_gather | solution.py:537
  90.3 4.8 %shard_map.81 = (bf16[4,48,1024]{2,1,0:T(8,128)(2,1)S(1)}, bf16[32,1024]{1,0:T(8,128)(2,1)S(1)}) custom-call(s32[2]{0:T(128)S(1)} %pad_add_fusion.place_ref, bf16[12,32,1024]{2,1,0:T(8,128)(2,1)S(1)} %bitcast.13, bf16[1184,512]{1,0:T(8,128)(2,1)S(1)} %copy-done, bf16[1184,512]{1,0:T(8,128)(2,1)S(1)} %collective-permute-done.refs_1_, ...), custom_call_target="tpu_custom_call" | custom-call | tf_op jit(solution)/shard_map/pallas_call | solution.py:543
  95.1 19.9 %all-gather.2 = bf16[384,1024]{1,0:T(8,128)(2,1)S(1)} all-gather(bf16[32,1024]{1,0:T(8,128)(2,1)S(1)} %get-tuple-element.29), channel_id=4, replica_groups=mesh['z'=12,'yl'=2,'c'=2,'x'=4,'yh'=4] {'z'}, dimensions={0}, use_global_device_ids=true | all-gather | bytes 851968 | tf_op jit(solution)/shard_map/all_gather | solution.py:537
  114.9 4.7 %shard_map.82 = (bf16[4,48,1024]{2,1,0:T(8,128)(2,1)S(1)}, bf16[32,1024]{1,0:T(8,128)(2,1)S(1)}) custom-call(s32[2]{0:T(128)S(1)} %pad_add_fusion.place_ref, bf16[12,32,1024]{2,1,0:T(8,128)(2,1)S(1)} %bitcast.14, bf16[1184,512]{1,0:T(8,128)(2,1)S(1)} %copy-done, bf16[1184,512]{1,0:T(8,128)(2,1)S(1)} %collective-permute-done.refs_1_, ...), custom_call_target="tpu_custom_call" | custom-call | tf_op jit(solution)/shard_map/pallas_call | solution.py:543
  119.7 20.2 %all-gather.3 = bf16[384,1024]{1,0:T(8,128)(2,1)S(1)} all-gather(bf16[32,1024]{1,0:T(8,128)(2,1)S(1)} %get-tuple-element.31), channel_id=5, replica_groups=mesh['z'=12,'yl'=2,'c'=2,'x'=4,'yh'=4] {'z'}, dimensions={0}, use_global_device_ids=true | all-gather | bytes 851968 | tf_op jit(solution)/shard_map/all_gather | solution.py:537
  139.9 5.4 %shard_map.83 = (f32[4,16,64]{2,1,0:T(8,128)}, bf16[48,1024]{1,0:T(8,128)(2,1)S(1)}, bf16[48,1024]{1,0:T(8,128)(2,1)S(1)}, bf16[48,1024]{1,0:T(8,128)(2,1)S(1)}, bf16[48,1024]{1,0:T(8,128)(2,1)S(1)}) custom-call(s32[2]{0:T(128)S(1)} %pad_add_fusion.place_ref, bf16[12,32,1024]{2,1,0:T(8,128)(2,1)S(1)} %bitcast.12, bf16[1184,512]{1,0:T(8,128)(2,1)S(1)} %copy-done, ...), custom_call_target="tpu_custom_call" | custom-call | tf_op jit(solution)/shard_map/pallas_call | solution.py:543
  145.3 24.2 %all-to-all-start.1 = ((f32[64,1,64]{2,1,0:T(1,128)}), f32[64,1,64]{2,1,0:T(1,128)S(1)}, u32[]{:S(2)}, u32[]{:S(2)}) async-start(f32[64,1,64]{2,1,0:T(1,128)} %bitcast.9), calls=%async_computation.1 | async-start | bytes 65536 | tf_op jit(solution)/shard_map/all_to_all | solution.py:564
  169.5 2.4 %collective-permute-start.3 = (bf16[48,1024]{1,0:T(8,128)(2,1)S(1)}, bf16[48,1024]{1,0:T(8,128)(2,1)S(1)}, u32[]{:S(2)}, u32[]{:S(2)}) collective-permute-start(bf16[48,1024]{1,0:T(8,128)(2,1)S(1)} %get-tuple-element.34), channel_id=1, source_target_pairs={{0,16},{16,0},{32,48},{48,32},{1,17},{17,1},{33,49},{49,33},{2,18}... | collective-permute-start | bytes 294920 | tf_op jit(solution)/shard_map/ppermute | solution.py:554
  171.9 3.3 %collective-permute-start.4 = (bf16[48,1024]{1,0:T(8,128)(2,1)S(1)}, bf16[48,1024]{1,0:T(8,128)(2,1)S(1)}, u32[]{:S(2)}, u32[]{:S(2)}) collective-permute-start(bf16[48,1024]{1,0:T(8,128)(2,1)S(1)} %get-tuple-element.35), channel_id=1, source_target_pairs={{0,32},{16,48},{32,0},{48,16},{1,33},{17,49},{33,1},{49,17},{2,34}... | collective-permute-start | bytes 294920 | tf_op jit(solution)/shard_map/ppermute | solution.py:554
  175.2 2.2 %collective-permute-start.5 = (bf16[48,1024]{1,0:T(8,128)(2,1)S(1)}, bf16[48,1024]{1,0:T(8,128)(2,1)S(1)}, u32[]{:S(2)}, u32[]{:S(2)}) collective-permute-start(bf16[48,1024]{1,0:T(8,128)(2,1)S(1)} %get-tuple-element.36), channel_id=1, source_target_pairs={{0,48},{16,32},{32,16},{48,0},{1,49},{17,33},{33,17},{49,1},{2,50}... | collective-permute-start | bytes 294920 | tf_op jit(solution)/shard_map/ppermute | solution.py:554
  177.4 1.4 all-to-all-done.1
  178.9 0.5 broadcast_multiply_fusion
  179.4 2.7 %collective-permute-done.5.refs_3_ = bf16[48,1024]{1,0:T(8,128)(2,1)S(1)} collective-permute-done((bf16[48,1024]{1,0:T(8,128)(2,1)S(1)}, bf16[48,1024]{1,0:T(8,128)(2,1)S(1)}, u32[]{:S(2)}, u32[]{:S(2)}) %collective-permute-start.5) | collective-permute-done | bytes 98336 | tf_op jit(solution)/shard_map/ppermute | solution.py:554
  182.1 1.3 shard_map.84
  (16 shorter events, 0.4 us)
Async XLA Ops:
  4.0 23.4 %all-to-all-start = ((bf16[4,80,1024]{2,1,0:T(8,128)(2,1)}), bf16[4,80,1024]{2,1,0:T(8,128)(2,1)S(1)}, u32[]{:S(2)}, u32[]{:S(2)}) async-start(bf16[4,80,1024]{2,1,0:T(8,128)(2,1)} %shard_map.78), calls=%async_computation | async-start | bytes 1310720 | tf_op jit(solution)/shard_map/all_to_all | solution.py:476
  18.0 17.0 %copy-start.1 = (f32[48,18]{0,1:T(8,128)S(1)}, f32[48,18]{0,1:T(8,128)}, u32[]{:S(2)}) copy-start(f32[48,18]{0,1:T(8,128)} %param.10) | copy-start | bytes 10372
  18.0 17.1 %copy-start.2 = (f32[192]{0:T(256)S(1)}, f32[192]{0:T(256)}, u32[]{:S(2)}) copy-start(f32[192]{0:T(256)} %param.11) | copy-start | bytes 2308
  20.3 40.2 %copy-start = (bf16[1184,512]{1,0:T(8,128)(2,1)S(1)}, bf16[1184,512]{1,0:T(8,128)(2,1)}, u32[]{:S(2)}) copy-start(bf16[1184,512]{1,0:T(8,128)(2,1)} %shard_map.77.refs_0_) | copy-start | bytes 3637252
  20.3 39.9 %collective-permute-start = (bf16[1184,512]{1,0:T(8,128)(2,1)}, bf16[1184,512]{1,0:T(8,128)(2,1)S(1)}, u32[]{:S(2)}, u32[]{:S(2)}) collective-permute-start(bf16[1184,512]{1,0:T(8,128)(2,1)} %shard_map.77.refs_0_), channel_id=1, source_target_pairs={{0,16},{16,0},{1,17},{17,1},{2,18},{18,2},{3,19},{19,3},{4,20},{20... | collective-permute-start | bytes 3637256 | tf_op jit(solution)/shard_map/ppermute | solution.py:499
  27.4 32.8 %collective-permute-start.1 = (bf16[1184,512]{1,0:T(8,128)(2,1)}, bf16[1184,512]{1,0:T(8,128)(2,1)}, u32[]{:S(2)}, u32[]{:S(2)}) collective-permute-start(bf16[1184,512]{1,0:T(8,128)(2,1)} %shard_map.77.refs_0_), channel_id=1, source_target_pairs={{0,32},{16,51},{32,1},{48,16},{1,33},{17,48},{33,2},{49,17},{2,34}... | collective-permute-start | bytes 3637256 | tf_op jit(solution)/shard_map/ppermute | solution.py:505
  29.3 31.2 %collective-permute-start.2 = (bf16[1184,512]{1,0:T(8,128)(2,1)}, bf16[1184,512]{1,0:T(8,128)(2,1)}, u32[]{:S(2)}, u32[]{:S(2)}) collective-permute-start(bf16[1184,512]{1,0:T(8,128)(2,1)} %shard_map.77.refs_0_), channel_id=1, source_target_pairs={{0,48},{16,35},{32,17},{48,0},{1,49},{17,32},{33,18},{49,1},{2,50}... | collective-permute-start | bytes 3637256 | tf_op jit(solution)/shard_map/ppermute | solution.py:506
  145.3 33.5 %all-to-all-start.1 = ((f32[64,1,64]{2,1,0:T(1,128)}), f32[64,1,64]{2,1,0:T(1,128)S(1)}, u32[]{:S(2)}, u32[]{:S(2)}) async-start(f32[64,1,64]{2,1,0:T(1,128)} %bitcast.9), calls=%async_computation.1 | async-start | bytes 65536 | tf_op jit(solution)/shard_map/all_to_all | solution.py:564
  169.5 9.9 %collective-permute-start.3 = (bf16[48,1024]{1,0:T(8,128)(2,1)S(1)}, bf16[48,1024]{1,0:T(8,128)(2,1)S(1)}, u32[]{:S(2)}, u32[]{:S(2)}) collective-permute-start(bf16[48,1024]{1,0:T(8,128)(2,1)S(1)} %get-tuple-element.34), channel_id=1, source_target_pairs={{0,16},{16,0},{32,48},{48,32},{1,17},{17,1},{33,49},{49,33},{2,18}... | collective-permute-start | bytes 294920 | tf_op jit(solution)/shard_map/ppermute | solution.py:554
  171.9 7.5 %collective-permute-start.4 = (bf16[48,1024]{1,0:T(8,128)(2,1)S(1)}, bf16[48,1024]{1,0:T(8,128)(2,1)S(1)}, u32[]{:S(2)}, u32[]{:S(2)}) collective-permute-start(bf16[48,1024]{1,0:T(8,128)(2,1)S(1)} %get-tuple-element.35), channel_id=1, source_target_pairs={{0,32},{16,48},{32,0},{48,16},{1,33},{17,49},{33,1},{49,17},{2,34}... | collective-permute-start | bytes 294920 | tf_op jit(solution)/shard_map/ppermute | solution.py:554
  175.2 6.9 %collective-permute-start.5 = (bf16[48,1024]{1,0:T(8,128)(2,1)S(1)}, bf16[48,1024]{1,0:T(8,128)(2,1)S(1)}, u32[]{:S(2)}, u32[]{:S(2)}) collective-permute-start(bf16[48,1024]{1,0:T(8,128)(2,1)S(1)} %get-tuple-element.36), channel_id=1, source_target_pairs={{0,48},{16,32},{32,16},{48,0},{1,49},{17,33},{33,17},{49,1},{2,50}... | collective-permute-start | bytes 294920 | tf_op jit(solution)/shard_map/ppermute | solution.py:554

commit v6 on v5

--- a/solution.py
+++ b/solution.py
@@ -320,8 +320,8 @@
 
 def first_kernel(factors, place_ref, coupling_ref, got_ref, open_hbm, *refs):
     packs, refs = refs[:GROUP], refs[GROUP:]
-    next_ref, message_ref, v_ref, proj_ref, near_ref, pick_ref, factor_ref = refs[:7]
-    local_ref, held_ref, edge_ref, wide_ref, scaled_ref, raw_ref, sems = refs[7:]
+    next_ref, message_ref, v_ref, held_ref, proj_ref, near_ref, pick_ref, factor_ref = refs[:8]
+    local_ref, edge_ref, wide_ref, scaled_ref, raw_ref, sems = refs[8:]
     groups = got_ref.shape[0]
     me = place_ref[0]
     _, below, above = beside(place_ref, groups)
@@ -370,22 +370,19 @@
 
 def step_kernel(degree, factors, place_ref, got_ref, *refs):
     last = degree == DEGREE - 1
-    packs, refs = refs[:GROUP], refs[GROUP:]
-    v_ref, old_ref, proj_ref, near_ref, pick_ref, factor_ref = refs[:6]
-    refs = refs[6:]
+    v_ref, old_ref, held_ref, proj_ref, near_ref, pick_ref, factor_ref = refs[:7]
+    refs = refs[7:]
     if last:
         occ_ref, density_ref, *next_refs = refs[: 2 + GROUP]
         refs = refs[2 + GROUP :]
     else:
         next_ref, message_ref = refs[:2]
         refs = refs[2:]
-    local_ref, held_ref, edge_ref, wide_ref, scaled_ref, sems = refs
+    local_ref, edge_ref, wide_ref, scaled_ref = refs
     me = place_ref[0]
-    hams = fetch_hams(packs, held_ref, sems)
     scaled = sum_coefs(got_ref, pick_ref, factor_ref, scaled_ref)
     for part in range(GROUP):
         local_ref[part] = dot_tn(scaled[part], proj_ref[part])
-    finish(hams)
     add_local(me, v_ref, held_ref, local_ref)
     add_faces(place_ref, got_ref, near_ref, scaled, local_ref)
 
@@ -497,13 +494,12 @@
         ]
 
     beside_core = lax.ppermute(pack, "c", [(0, 1), (1, 0)])
-    late, message = lax.optimization_barrier((pack, message))
     axes = ("yl", "c", "yh")
     packs = [
         pack,
         beside_core,
-        lax.ppermute(late, axes, across(0)),
-        lax.ppermute(late, axes, across(1)),
+        lax.ppermute(pack, axes, across(0)),
+        lax.ppermute(pack, axes, across(1)),
     ]
 
     factors = chebyshev_factors()
@@ -511,7 +507,6 @@
     message_shape = shape((BODY, PART))
     scratch = [
         pltpu.VMEM((GROUP, PIECE, PART), F32),
-        pltpu.VMEM((2 * GROUP, NODES, NODES), BF16),
         pltpu.VMEM((LANES, PART), BF16),
         pltpu.VMEM((BODY, PART), F32),
         pltpu.VMEM((GROUP + 2, PROJ, PIECE), F32),
@@ -523,13 +518,14 @@
             state_shape,
             message_shape,
             state_shape,
+            shape((2 * GROUP, NODES, NODES)),
             shape((GROUP, PROJ, PART)),
             shape((2, PROJ, LANES)),
             shape((PIECE, -(-groups * BODY // LANES) * LANES)),
             shape((PIECE, WIDE), F32),
         ],
         in_specs=[smem()] + [vmem()] * 2 + [hbm()] * (GROUP + 1),
-        out_specs=[vmem()] * 7,
+        out_specs=[vmem()] * 8,
         scratch_shapes=scratch
         + [pltpu.VMEM((GROUP, 2 * PADDED, NODES), BF16), dma((4 * GROUP,))],
     )(place, coupling, got, opened, *packs)
@@ -543,10 +539,10 @@
         result = call(
             functools.partial(step_kernel, degree, factors),
             out_shape=outs,
-            in_specs=[smem(), vmem()] + [hbm()] * GROUP + [vmem()] * (6 + len(ends)),
+            in_specs=[smem()] + [vmem()] * (8 + len(ends)),
             out_specs=[vmem()] * len(outs),
-            scratch_shapes=scratch + [dma((2 * GROUP,))],
-        )(place, got, *packs, v, old, *kept, *ends)
+            scratch_shapes=scratch,
+        )(place, got, v, old, *kept, *ends)
         old, v, message = v, result[0], result[1]
 
     density, *pieces = result

time: 184 us -> 176 us (0.957)
  waiting for transfers between devices: 9.34 us -> 4.1 us
  Pallas kernels: 27.8 us -> 23.5 us
    all_to_all x1, waiting for transfers between devices: 4.9 us -> 0.01 us  [shards(): opened = lax.all_to_all(opened, near, 0, 0)]
    pallas_call x3, Pallas kernels: 14.9 us -> 10.7 us  [shards(): call(functools.partial(step_kernel, degree, factors), out_shape=outs, in_...]
  transfers between devices with their start and end apart: 8 -> 8, of which waited for: 4 -> 2; matrix products, arithmetic and copies ran while one was open for 0% -> 0% of each run, Pallas kernels for 1% -> 1%
where the time goes in v6:
time: 176 us
  blocking collectives  89.8 us (51%)
  starting transfers between devices  56.6 us (32%)
  Pallas kernels  23.5 us (13%)
  waiting for transfers between devices  4.1 us (2%)
    all_gather x4, blocking collectives, shards(): got = lax.all_gather(message, 'z')  89.8 us
    all_to_all x1, starting transfers between devices, shards(): lax.all_to_all(density.reshape(parts, GROUP * PART // parts), near + ('x'...  25.5 us
    all_to_all x1, starting transfers between devices, shards(): opened = lax.all_to_all(opened, near, 0, 0)  14 us
    pallas_call x3, Pallas kernels, shards(): call(functools.partial(step_kernel, degree, factors), out_shape=outs, in_...  10.7 us
    ppermute x3, starting transfers between devices, shards(): lax.ppermute(pieces[r], near, [(k, k ^ r) for k in range(GROUP)])  7.87 us
    pallas_call x1, Pallas kernels, shards(): call(functools.partial(first_kernel, factors), out_shape=[state_shape, me...  5.82 us
    ppermute x1, starting transfers between devices, shards(): lax.ppermute(pack, axes, across(1))  5.2 us
  transfers between devices with their start and end apart: 8, of which 2 were waited for; matrix products, arithmetic and copies ran while one was open for 0% of the time, Pallas kernels for 1%

profile of v6, /device:TPU:1, one launch (start us, length us, event | category | flops | bytes accessed | tf_op | source)
XLA Modules:
  0.0 175.7 jit_solution(7940136882899201200)
XLA Ops:
  0.6 3.3 %shard_map.77 = bf16[4,80,1024]{2,1,0:T(8,128)(2,1)} custom-call(s32[2,4]{1,0:T(2,128)} %atom_ref.1, bf16[192,1024]{1,0:T(8,128)(2,1)} %bitcast.16, bf16[2,512,512]{2,1,0:T(8,128)(2,1)} %ham_hbm.3, bf16[2,72,512]{2,1,0:T(8,128)(2,1)} %proj_hbm.3), custom_call_target="tpu_custom_call" | custom-call | tf_op jit(solution)/shard_map/pallas_call | solution.py:459
  4.0 14.0 %all-to-all-start = ((bf16[4,80,1024]{2,1,0:T(8,128)(2,1)}), bf16[4,80,1024]{2,1,0:T(8,128)(2,1)S(1)}, u32[]{:S(2)}, u32[]{:S(2)}) async-start(bf16[4,80,1024]{2,1,0:T(8,128)(2,1)} %shard_map.77), calls=%async_computation | async-start | bytes 1310720 | tf_op jit(solution)/shard_map/all_to_all | solution.py:473
  17.9 2.4 %shard_map.79.refs_0_ = bf16[1184,512]{1,0:T(8,128)(2,1)} custom-call(bf16[2,512,512]{2,1,0:T(8,128)(2,1)} %ham_hbm.3, bf16[2,72,512]{2,1,0:T(8,128)(2,1)} %proj_hbm.3), custom_call_target="tpu_custom_call" | custom-call | tf_op jit(solution)/shard_map/pallas_call | solution.py:474
  20.3 2.1 %collective-permute-start = (bf16[1184,512]{1,0:T(8,128)(2,1)}, bf16[1184,512]{1,0:T(8,128)(2,1)S(1)}, u32[]{:S(2)}, u32[]{:S(2)}) collective-permute-start(bf16[1184,512]{1,0:T(8,128)(2,1)} %shard_map.79.refs_0_), channel_id=1, source_target_pairs={{0,16},{16,0},{1,17},{17,1},{2,18},{18,2},{3,19},{19,3},{4,20},{20... | collective-permute-start | bytes 3637256 | tf_op jit(solution)/shard_map/ppermute | solution.py:496
  22.4 1.9 %collective-permute-start.1 = (bf16[1184,512]{1,0:T(8,128)(2,1)}, bf16[1184,512]{1,0:T(8,128)(2,1)}, u32[]{:S(2)}, u32[]{:S(2)}) collective-permute-start(bf16[1184,512]{1,0:T(8,128)(2,1)} %shard_map.79.refs_0_), channel_id=1, source_target_pairs={{0,32},{16,51},{32,1},{48,16},{1,33},{17,48},{33,2},{49,17},{2,34}... | collective-permute-start | bytes 3637256 | tf_op jit(solution)/shard_map/ppermute | solution.py:501
  24.3 5.2 %collective-permute-start.2 = (bf16[1184,512]{1,0:T(8,128)(2,1)}, bf16[1184,512]{1,0:T(8,128)(2,1)}, u32[]{:S(2)}, u32[]{:S(2)}) collective-permute-start(bf16[1184,512]{1,0:T(8,128)(2,1)} %shard_map.79.refs_0_), channel_id=1, source_target_pairs={{0,48},{16,35},{32,17},{48,0},{1,49},{17,32},{33,18},{49,1},{2,50}... | collective-permute-start | bytes 3637256 | tf_op jit(solution)/shard_map/ppermute | solution.py:502
  29.6 0.1 copy.9.coupling_ref
  29.9 26.5 %all-gather = bf16[480,1024]{1,0:T(8,128)(2,1)S(1)} all-gather(bf16[40,1024]{1,0:T(8,128)(2,1)S(1)} %shard_map.78), channel_id=2, replica_groups=mesh['z'=12,'yl'=2,'c'=2,'x'=4,'yh'=4] {'z'}, dimensions={0}, use_global_device_ids=true | all-gather | bytes 1064960 | tf_op jit(solution)/shard_map/all_gather | solution.py:514
  56.4 5.8 %shard_map.80 = (bf16[4,48,1024]{2,1,0:T(8,128)(2,1)S(1)}, bf16[32,1024]{1,0:T(8,128)(2,1)S(1)}, bf16[4,48,1024]{2,1,0:T(8,128)(2,1)S(1)}, bf16[8,512,512]{2,1,0...) custom-call(s32[2]{0:T(128)S(1)} %pad_add_fusion.place_ref, ...), custom_call_target="tpu_custom_call" | custom-call | tf_op jit(solution)/shard_map/pallas_call | solution.py:515
  62.2 23.5 %all-gather.1 = bf16[384,1024]{1,0:T(8,128)(2,1)S(1)} all-gather(bf16[32,1024]{1,0:T(8,128)(2,1)S(1)} %get-tuple-element.19), channel_id=3, replica_groups=mesh['z'=12,'yl'=2,'c'=2,'x'=4,'yh'=4] {'z'}, dimensions={0}, use_global_device_ids=true | all-gather | bytes 851968 | tf_op jit(solution)/shard_map/all_gather | solution.py:533
  85.7 3.5 %shard_map.81 = (bf16[4,48,1024]{2,1,0:T(8,128)(2,1)S(1)}, bf16[32,1024]{1,0:T(8,128)(2,1)S(1)}) custom-call(s32[2]{0:T(128)S(1)} %pad_add_fusion.place_ref, bf16[12,32,1024]{2,1,0:T(8,128)(2,1)S(1)} %bitcast.12, bf16[4,48,1024]{2,1,0:T(8,128)(2,1)S(1)} %get-tuple-element.20.refs_0_.refs_1_, bf16[4,48,1024]{2,1,0:T(8,128)(2,1)S(1)} %get-tuple-element.21.refs_1_, ...), custom_call_target="tpu_custom_call" | custom-call | tf_op jit(solution)/shard_map/pallas_call | solution.py:539
  89.2 19.9 %all-gather.2 = bf16[384,1024]{1,0:T(8,128)(2,1)S(1)} all-gather(bf16[32,1024]{1,0:T(8,128)(2,1)S(1)} %get-tuple-element.27), channel_id=4, replica_groups=mesh['z'=12,'yl'=2,'c'=2,'x'=4,'yh'=4] {'z'}, dimensions={0}, use_global_device_ids=true | all-gather | bytes 851968 | tf_op jit(solution)/shard_map/all_gather | solution.py:533
  109.1 3.5 %shard_map.82 = (bf16[4,48,1024]{2,1,0:T(8,128)(2,1)S(1)}, bf16[32,1024]{1,0:T(8,128)(2,1)S(1)}) custom-call(s32[2]{0:T(128)S(1)} %pad_add_fusion.place_ref, bf16[12,32,1024]{2,1,0:T(8,128)(2,1)S(1)} %bitcast.13, bf16[4,48,1024]{2,1,0:T(8,128)(2,1)S(1)} %get-tuple-element.28.refs_0_.refs_1_, bf16[4,48,1024]{2,1,0:T(8,128)(2,1)S(1)} %get-tuple-element.20.refs_0_.refs_1_, ...), custom_call_target="tpu_custom_call" | custom-call | tf_op jit(solution)/shard_map/pallas_call | solution.py:539
  112.6 20.0 %all-gather.3 = bf16[384,1024]{1,0:T(8,128)(2,1)S(1)} all-gather(bf16[32,1024]{1,0:T(8,128)(2,1)S(1)} %get-tuple-element.29), channel_id=5, replica_groups=mesh['z'=12,'yl'=2,'c'=2,'x'=4,'yh'=4] {'z'}, dimensions={0}, use_global_device_ids=true | all-gather | bytes 851968 | tf_op jit(solution)/shard_map/all_gather | solution.py:533
  132.6 3.7 %shard_map.83 = (f32[4,16,64]{2,1,0:T(8,128)}, bf16[48,1024]{1,0:T(8,128)(2,1)S(1)}, bf16[48,1024]{1,0:T(8,128)(2,1)S(1)}, bf16[48,1024]{1,0:T(8,128)(2,1)S(1)}, bf16[48,1024]{1,0:T(8,128)(2,1)S(1)}) custom-call(s32[2]{0:T(128)S(1)} %pad_add_fusion.place_ref, bf16[12,32,1024]{2,1,0:T(8,128)(2,1)S(1)} %bitcast.14, ...), custom_call_target="tpu_custom_call" | custom-call | tf_op jit(solution)/shard_map/pallas_call | solution.py:539
  136.2 25.5 %all-to-all-start.1 = ((f32[64,1,64]{2,1,0:T(1,128)}), f32[64,1,64]{2,1,0:T(1,128)S(1)}, u32[]{:S(2)}, u32[]{:S(2)}) async-start(f32[64,1,64]{2,1,0:T(1,128)} %bitcast.9), calls=%async_computation.1 | async-start | bytes 65536 | tf_op jit(solution)/shard_map/all_to_all | solution.py:560
  161.8 2.4 %collective-permute-start.3 = (bf16[48,1024]{1,0:T(8,128)(2,1)S(1)}, bf16[48,1024]{1,0:T(8,128)(2,1)S(1)}, u32[]{:S(2)}, u32[]{:S(2)}) collective-permute-start(bf16[48,1024]{1,0:T(8,128)(2,1)S(1)} %get-tuple-element.32), channel_id=1, source_target_pairs={{0,16},{16,0},{32,48},{48,32},{1,17},{17,1},{33,49},{49,33},{2,18}... | collective-permute-start | bytes 294920 | tf_op jit(solution)/shard_map/ppermute | solution.py:550
  164.1 3.3 %collective-permute-start.4 = (bf16[48,1024]{1,0:T(8,128)(2,1)S(1)}, bf16[48,1024]{1,0:T(8,128)(2,1)S(1)}, u32[]{:S(2)}, u32[]{:S(2)}) collective-permute-start(bf16[48,1024]{1,0:T(8,128)(2,1)S(1)} %get-tuple-element.33), channel_id=1, source_target_pairs={{0,32},{16,48},{32,0},{48,16},{1,33},{17,49},{33,1},{49,17},{2,34}... | collective-permute-start | bytes 294920 | tf_op jit(solution)/shard_map/ppermute | solution.py:550
  167.4 2.2 %collective-permute-start.5 = (bf16[48,1024]{1,0:T(8,128)(2,1)S(1)}, bf16[48,1024]{1,0:T(8,128)(2,1)S(1)}, u32[]{:S(2)}, u32[]{:S(2)}) collective-permute-start(bf16[48,1024]{1,0:T(8,128)(2,1)S(1)} %get-tuple-element.34), channel_id=1, source_target_pairs={{0,48},{16,32},{32,16},{48,0},{1,49},{17,33},{33,17},{49,1},{2,50}... | collective-permute-start | bytes 294920 | tf_op jit(solution)/shard_map/ppermute | solution.py:550
  169.6 1.4 all-to-all-done.1
  171.0 0.1 reduce_sum.9
  171.1 0.5 broadcast_multiply_fusion
  171.6 2.7 %collective-permute-done.5.refs_3_ = bf16[48,1024]{1,0:T(8,128)(2,1)S(1)} collective-permute-done((bf16[48,1024]{1,0:T(8,128)(2,1)S(1)}, bf16[48,1024]{1,0:T(8,128)(2,1)S(1)}, u32[]{:S(2)}, u32[]{:S(2)}) %collective-permute-start.5) | collective-permute-done | bytes 98336 | tf_op jit(solution)/shard_map/ppermute | solution.py:550
  174.3 1.3 shard_map.84
  (16 shorter events, 0.3 us)
Async XLA Ops:
  4.0 25.9 %all-to-all-start = ((bf16[4,80,1024]{2,1,0:T(8,128)(2,1)}), bf16[4,80,1024]{2,1,0:T(8,128)(2,1)S(1)}, u32[]{:S(2)}, u32[]{:S(2)}) async-start(bf16[4,80,1024]{2,1,0:T(8,128)(2,1)} %shard_map.77), calls=%async_computation | async-start | bytes 1310720 | tf_op jit(solution)/shard_map/all_to_all | solution.py:473
  17.9 11.6 %copy-start.1 = (f32[48,18]{0,1:T(8,128)S(1)}, f32[48,18]{0,1:T(8,128)}, u32[]{:S(2)}) copy-start(f32[48,18]{0,1:T(8,128)} %param.10) | copy-start | bytes 10372
  17.9 11.7 %copy-start.2 = (f32[192]{0:T(256)S(1)}, f32[192]{0:T(256)}, u32[]{:S(2)}) copy-start(f32[192]{0:T(256)} %param.11) | copy-start | bytes 2308
  20.3 36.1 %copy-start = (bf16[1184,512]{1,0:T(8,128)(2,1)S(1)}, bf16[1184,512]{1,0:T(8,128)(2,1)}, u32[]{:S(2)}) copy-start(bf16[1184,512]{1,0:T(8,128)(2,1)} %shard_map.79.refs_0_) | copy-start | bytes 3637252
  20.3 36.1 %collective-permute-start = (bf16[1184,512]{1,0:T(8,128)(2,1)}, bf16[1184,512]{1,0:T(8,128)(2,1)S(1)}, u32[]{:S(2)}, u32[]{:S(2)}) collective-permute-start(bf16[1184,512]{1,0:T(8,128)(2,1)} %shard_map.79.refs_0_), channel_id=1, source_target_pairs={{0,16},{16,0},{1,17},{17,1},{2,18},{18,2},{3,19},{19,3},{4,20},{20... | collective-permute-start | bytes 3637256 | tf_op jit(solution)/shard_map/ppermute | solution.py:496
  22.4 34.0 %collective-permute-start.1 = (bf16[1184,512]{1,0:T(8,128)(2,1)}, bf16[1184,512]{1,0:T(8,128)(2,1)}, u32[]{:S(2)}, u32[]{:S(2)}) collective-permute-start(bf16[1184,512]{1,0:T(8,128)(2,1)} %shard_map.79.refs_0_), channel_id=1, source_target_pairs={{0,32},{16,51},{32,1},{48,16},{1,33},{17,48},{33,2},{49,17},{2,34}... | collective-permute-start | bytes 3637256 | tf_op jit(solution)/shard_map/ppermute | solution.py:501
  24.3 32.1 %collective-permute-start.2 = (bf16[1184,512]{1,0:T(8,128)(2,1)}, bf16[1184,512]{1,0:T(8,128)(2,1)}, u32[]{:S(2)}, u32[]{:S(2)}) collective-permute-start(bf16[1184,512]{1,0:T(8,128)(2,1)} %shard_map.79.refs_0_), channel_id=1, source_target_pairs={{0,48},{16,35},{32,17},{48,0},{1,49},{17,32},{33,18},{49,1},{2,50}... | collective-permute-start | bytes 3637256 | tf_op jit(solution)/shard_map/ppermute | solution.py:502
  136.2 34.8 %all-to-all-start.1 = ((f32[64,1,64]{2,1,0:T(1,128)}), f32[64,1,64]{2,1,0:T(1,128)S(1)}, u32[]{:S(2)}, u32[]{:S(2)}) async-start(f32[64,1,64]{2,1,0:T(1,128)} %bitcast.9), calls=%async_computation.1 | async-start | bytes 65536 | tf_op jit(solution)/shard_map/all_to_all | solution.py:560
  161.8 9.9 %collective-permute-start.3 = (bf16[48,1024]{1,0:T(8,128)(2,1)S(1)}, bf16[48,1024]{1,0:T(8,128)(2,1)S(1)}, u32[]{:S(2)}, u32[]{:S(2)}) collective-permute-start(bf16[48,1024]{1,0:T(8,128)(2,1)S(1)} %get-tuple-element.32), channel_id=1, source_target_pairs={{0,16},{16,0},{32,48},{48,32},{1,17},{17,1},{33,49},{49,33},{2,18}... | collective-permute-start | bytes 294920 | tf_op jit(solution)/shard_map/ppermute | solution.py:550
  164.1 7.5 %collective-permute-start.4 = (bf16[48,1024]{1,0:T(8,128)(2,1)S(1)}, bf16[48,1024]{1,0:T(8,128)(2,1)S(1)}, u32[]{:S(2)}, u32[]{:S(2)}) collective-permute-start(bf16[48,1024]{1,0:T(8,128)(2,1)S(1)} %get-tuple-element.33), channel_id=1, source_target_pairs={{0,32},{16,48},{32,0},{48,16},{1,33},{17,49},{33,1},{49,17},{2,34}... | collective-permute-start | bytes 294920 | tf_op jit(solution)/shard_map/ppermute | solution.py:550
  167.4 6.9 %collective-permute-start.5 = (bf16[48,1024]{1,0:T(8,128)(2,1)S(1)}, bf16[48,1024]{1,0:T(8,128)(2,1)S(1)}, u32[]{:S(2)}, u32[]{:S(2)}) collective-permute-start(bf16[48,1024]{1,0:T(8,128)(2,1)S(1)} %get-tuple-element.34), channel_id=1, source_target_pairs={{0,48},{16,32},{32,16},{48,0},{1,49},{17,33},{33,17},{49,1},{2,50}... | collective-permute-start | bytes 294920 | tf_op jit(solution)/shard_map/ppermute | solution.py:550

commit v7 on v6

--- a/solution.py
+++ b/solution.py
@@ -106,13 +106,23 @@
     return slice(k * 8, (k + 1) * 8)
 
 
-def open_kernel(atom_ref, v_hbm, ham_hbm, proj_hbm, out_ref, v_ref, ham_ref, proj_ref, wide_ref, sems):
-    copies = run(
+def open_kernel(
+    atom_ref, v_hbm, ham_hbm, proj_hbm, out_ref, pack_ref, v_ref, ham_ref, proj_ref, wide_ref, sems
+):
+    proj_in, v_in, *edges = run(
         [
-            pltpu.make_async_copy(v_hbm, v_ref, sems.at[0]),
-            pltpu.make_async_copy(proj_hbm, proj_ref, sems.at[1]),
+            pltpu.make_async_copy(proj_hbm, proj_ref, sems.at[0]),
+            pltpu.make_async_copy(v_hbm, v_ref, sems.at[1]),
             pltpu.make_async_copy(ham_hbm.at[0, :LANES, :], ham_ref.at[0], sems.at[2]),
             pltpu.make_async_copy(ham_hbm.at[1, NODES - LANES :, :], ham_ref.at[1], sems.at[3]),
+        ]
+    )
+    hams = run(
+        [
+            pltpu.make_async_copy(
+                ham_hbm.at[k], pack_ref.at[pl.ds(k * NODES, NODES), :], sems.at[4 + k]
+            )
+            for k in range(2)
         ]
     )
     place0, place1 = placers()
@@ -123,13 +133,19 @@
         cell, slot = (0, block) if block < SLOTS else (1, block - SLOTS + 1)
         atoms = jnp.where(lane == block, atom_ref[cell, slot], atoms)
     atoms = atoms.astype(F32)
-    finish(copies)
     width = v_ref.shape[0]
+    proj_in.wait()
+    pad = jnp.zeros((PADDED - ROWS, NODES), BF16)
+    for k in range(2):
+        start = PART + k * PADDED
+        pack_ref[start : start + PADDED, :] = jnp.concatenate([proj_ref[k], pad], axis=0)
     p0 = dot(place0, proj_ref[0]).astype(BF16)
     p1 = dot(place1, proj_ref[1]).astype(BF16)
+    v_in.wait()
     v0 = v_ref[:, :NODES]
     v1 = v_ref[:, NODES:]
     coef = dot_nt(p0, v0) + dot_nt(p1, v1)
+    finish(edges)
     face = jnp.where(low_lanes(width), dot_nt(v0, ham_ref[0]), dot_nt(v1, ham_ref[1]))
     edge = jnp.where(
         low_lanes(ROWS),
@@ -149,20 +165,7 @@
         wide_ref[to, 24:32, :LANES] = edge[eight(8)]
         out_ref[to, :HEAD, :] = wide_ref[to].astype(BF16)
         out_ref[to, HEAD:, :] = v_ref[to * PIECE : (to + 1) * PIECE, :]
-
-
-def share_kernel(ham_hbm, proj_hbm, out_ref, proj_ref, sems):
-    copies = [
-        pltpu.make_async_copy(ham_hbm.at[k], out_ref.at[pl.ds(k * NODES, NODES), :], sems.at[k])
-        for k in range(2)
-    ]
-    copies = run([pltpu.make_async_copy(proj_hbm, proj_ref, sems.at[2])] + copies)
-    copies[0].wait()
-    pad = jnp.zeros((PADDED - ROWS, NODES), BF16)
-    for k in range(2):
-        start = PART + k * PADDED
-        out_ref[start : start + PADDED, :] = jnp.concatenate([proj_ref[k], pad], axis=0)
-    finish(copies[1:])
+    finish(hams)
 
 
 def place_face(face, wide_ref):
@@ -456,29 +459,21 @@
     place = jnp.stack([me, lax.axis_index("z")]).astype(jnp.int32)
     occ = jnp.pad(occupancy.reshape(GROUP, PIECE), ((0, 0), (0, LANES - PIECE)))
     v_t = states.T
-    opened = call(
+    opened, pack = call(
         open_kernel,
         megabytes=60,
-        out_shape=shape((GROUP, HEAD + PIECE, PART)),
+        out_shape=[shape((GROUP, HEAD + PIECE, PART)), shape((PACK, NODES))],
         in_specs=[smem()] + [hbm()] * 3,
-        out_specs=vmem(),
+        out_specs=[vmem()] * 2,
         scratch_shapes=[
             pltpu.VMEM((width, PART), BF16),
             pltpu.VMEM((2, LANES, NODES), BF16),
             pltpu.VMEM((2, ROWS, NODES), BF16),
             pltpu.VMEM((GROUP, HEAD, PART), F32),
-            dma((4,)),
+            dma((6,)),
         ],
     )(slot_atom, v_t, cell_ham, projectors)
     opened = lax.all_to_all(opened, near, 0, 0)
-    pack = call(
-        share_kernel,
-        megabytes=60,
-        out_shape=shape((PACK, NODES)),
-        in_specs=[hbm()] * 2,
-        out_specs=vmem(),
-        scratch_shapes=[pltpu.VMEM((2, ROWS, NODES), BF16), dma((3,))],
-    )(cell_ham, projectors)
     message = call(
         pack_kernel,
         out_shape=shape((BODY + 8, PART)),
@@ -546,9 +541,8 @@
         old, v, message = v, result[0], result[1]
 
     density, *pieces = result
-    pieces = [pieces[0]] + [
-        lax.ppermute(pieces[r], near, [(k, k ^ r) for k in range(GROUP)]) for r in (1, 2, 3)
-    ]
+    for r in (3, 2, 1):
+        pieces[r] = lax.ppermute(pieces[r], near, [(k, k ^ r) for k in range(GROUP)])
     filtered = call(
         join_kernel,
         out_shape=shape((width, PART)),

time: 176 us -> 176 us (level)
  starting transfers between devices: 56.6 us -> 59.5 us
    all_to_all x1, starting transfers between devices: 25.5 us -> 28.4 us  [shards(): lax.all_to_all(density.reshape(parts, GROUP * PART // parts), near + ('x'...]
    pallas_call x2 -> x1, Pallas kernels: 5.68 us -> 4 us  [shards(): call(open_kernel, megabytes=60, out_shape=[shape((GROUP, HEAD + PIECE, PA...]
  transfers between devices with their start and end apart: 8 -> 8, of which waited for: 2 -> 3; matrix products, arithmetic and copies ran while one was open for 0% -> 0% of each run, Pallas kernels for 1% -> 0%
where the time goes in v7:
time: 176 us
  blocking collectives  88.7 us (50%)
  starting transfers between devices  59.5 us (34%)
  Pallas kernels  21.8 us (12%)
  waiting for transfers between devices  4.22 us (2%)
    all_gather x4, blocking collectives, shards(): got = lax.all_gather(message, 'z')  88.7 us
    all_to_all x1, starting transfers between devices, shards(): lax.all_to_all(density.reshape(parts, GROUP * PART // parts), near + ('x'...  28.4 us
    all_to_all x1, starting transfers between devices, shards(): opened = lax.all_to_all(opened, near, 0, 0)  14.1 us
    pallas_call x3, Pallas kernels, shards(): call(functools.partial(step_kernel, degree, factors), out_shape=outs, in_...  10.6 us
    ppermute x3, starting transfers between devices, shards(): lax.ppermute(pieces[r], near, [(k, k ^ r) for k in range(GROUP)])  7.87 us
    pallas_call x1, Pallas kernels, shards(): call(functools.partial(first_kernel, factors), out_shape=[state_shape, me...  5.81 us
    ppermute x1, starting transfers between devices, shards(): lax.ppermute(pack, axes, across(1))  5.19 us
    pallas_call x1, Pallas kernels, shards(): call(open_kernel, megabytes=60, out_shape=[shape((GROUP, HEAD + PIECE, PA...  4 us
  transfers between devices with their start and end apart: 8, of which 3 were waited for; matrix products, arithmetic and copies ran while one was open for 0% of the time, Pallas kernels for 0%

profile of v7, /device:TPU:1, one launch (start us, length us, event | category | flops | bytes accessed | tf_op | source)
XLA Modules:
  0.0 175.9 jit_solution(910932369380183258)
XLA Ops:
  0.7 4.0 %shard_map.77 = (bf16[4,80,1024]{2,1,0:T(8,128)(2,1)}, bf16[1184,512]{1,0:T(8,128)(2,1)}) custom-call(s32[2,4]{1,0:T(2,128)} %atom_ref.1, bf16[192,1024]{1,0:T(8,128)(2,1)} %bitcast.15, bf16[2,512,512]{2,1,0:T(8,128)(2,1)} %ham_hbm.1, bf16[2,72,512]{2,1,0:T(8,128)(2,1)} %proj_hbm.1), custom_call_target="tpu_custom_call" | custom-call | tf_op jit(solution)/shard_map/pallas_call | solution.py:462
  4.7 14.1 %all-to-all-start = ((bf16[4,80,1024]{2,1,0:T(8,128)(2,1)}), bf16[4,80,1024]{2,1,0:T(8,128)(2,1)S(1)}, u32[]{:S(2)}, u32[]{:S(2)}) async-start(bf16[4,80,1024]{2,1,0:T(8,128)(2,1)} %get-tuple-element.21), calls=%async_computation | async-start | bytes 1310720 | tf_op jit(solution)/shard_map/all_to_all | solution.py:476
  18.8 2.0 %collective-permute-start = (bf16[1184,512]{1,0:T(8,128)(2,1)S(1)}, bf16[1184,512]{1,0:T(8,128)(2,1)S(1)}, u32[]{:S(2)}, u32[]{:S(2)}) collective-permute-start(bf16[1184,512]{1,0:T(8,128)(2,1)S(1)} %copy-done), channel_id=1, source_target_pairs={{0,16},{16,0},{1,17},{17,1},{2,18},{18,2},{3,19},{19,3},{4,20},{20... | collective-permute-start | bytes 3637256 | tf_op jit(solution)/shard_map/ppermute | solution.py:491
  20.8 1.9 %collective-permute-start.1 = (bf16[1184,512]{1,0:T(8,128)(2,1)S(1)}, bf16[1184,512]{1,0:T(8,128)(2,1)}, u32[]{:S(2)}, u32[]{:S(2)}) collective-permute-start(bf16[1184,512]{1,0:T(8,128)(2,1)S(1)} %copy-done), channel_id=1, source_target_pairs={{0,32},{16,51},{32,1},{48,16},{1,33},{17,48},{33,2},{49,17},{2,34}... | collective-permute-start | bytes 3637256 | tf_op jit(solution)/shard_map/ppermute | solution.py:496
  22.7 5.2 %collective-permute-start.2 = (bf16[1184,512]{1,0:T(8,128)(2,1)S(1)}, bf16[1184,512]{1,0:T(8,128)(2,1)}, u32[]{:S(2)}, u32[]{:S(2)}) collective-permute-start(bf16[1184,512]{1,0:T(8,128)(2,1)S(1)} %copy-done), channel_id=1, source_target_pairs={{0,48},{16,35},{32,17},{48,0},{1,49},{17,32},{33,18},{49,1},{2,50}... | collective-permute-start | bytes 3637256 | tf_op jit(solution)/shard_map/ppermute | solution.py:497
  27.9 0.1 copy.9.coupling_ref
  28.2 0.1 all-to-all-done.in_ref.open_hbm
  28.4 25.1 %all-gather = bf16[480,1024]{1,0:T(8,128)(2,1)S(1)} all-gather(bf16[40,1024]{1,0:T(8,128)(2,1)S(1)} %shard_map.78), channel_id=2, replica_groups=mesh['z'=12,'yl'=2,'c'=2,'x'=4,'yh'=4] {'z'}, dimensions={0}, use_global_device_ids=true | all-gather | bytes 1064960 | tf_op jit(solution)/shard_map/all_gather | solution.py:509
  53.5 5.8 %shard_map.79 = (bf16[4,48,1024]{2,1,0:T(8,128)(2,1)S(1)}, bf16[32,1024]{1,0:T(8,128)(2,1)S(1)}, bf16[4,48,1024]{2,1,0:T(8,128)(2,1)S(1)}, bf16[8,512,512]{2,1,0...) custom-call(s32[2]{0:T(128)S(1)} %pad_add_fusion.place_ref, ...), custom_call_target="tpu_custom_call" | custom-call | tf_op jit(solution)/shard_map/pallas_call | solution.py:510
  59.3 23.7 %all-gather.1 = bf16[384,1024]{1,0:T(8,128)(2,1)S(1)} all-gather(bf16[32,1024]{1,0:T(8,128)(2,1)S(1)} %get-tuple-element.23), channel_id=3, replica_groups=mesh['z'=12,'yl'=2,'c'=2,'x'=4,'yh'=4] {'z'}, dimensions={0}, use_global_device_ids=true | all-gather | bytes 851968 | tf_op jit(solution)/shard_map/all_gather | solution.py:528
  83.0 3.5 %shard_map.80 = (bf16[4,48,1024]{2,1,0:T(8,128)(2,1)S(1)}, bf16[32,1024]{1,0:T(8,128)(2,1)S(1)}) custom-call(s32[2]{0:T(128)S(1)} %pad_add_fusion.place_ref, bf16[12,32,1024]{2,1,0:T(8,128)(2,1)S(1)} %bitcast.12, bf16[4,48,1024]{2,1,0:T(8,128)(2,1)S(1)} %get-tuple-element.24.refs_0_.refs_1_, bf16[4,48,1024]{2,1,0:T(8,128)(2,1)S(1)} %get-tuple-element.25.refs_1_, ...), custom_call_target="tpu_custom_call" | custom-call | tf_op jit(solution)/shard_map/pallas_call | solution.py:534
  86.5 20.6 %all-gather.2 = bf16[384,1024]{1,0:T(8,128)(2,1)S(1)} all-gather(bf16[32,1024]{1,0:T(8,128)(2,1)S(1)} %get-tuple-element.31), channel_id=4, replica_groups=mesh['z'=12,'yl'=2,'c'=2,'x'=4,'yh'=4] {'z'}, dimensions={0}, use_global_device_ids=true | all-gather | bytes 851968 | tf_op jit(solution)/shard_map/all_gather | solution.py:528
  107.2 3.5 %shard_map.81 = (bf16[4,48,1024]{2,1,0:T(8,128)(2,1)S(1)}, bf16[32,1024]{1,0:T(8,128)(2,1)S(1)}) custom-call(s32[2]{0:T(128)S(1)} %pad_add_fusion.place_ref, bf16[12,32,1024]{2,1,0:T(8,128)(2,1)S(1)} %bitcast.13, bf16[4,48,1024]{2,1,0:T(8,128)(2,1)S(1)} %get-tuple-element.32.refs_0_.refs_1_, bf16[4,48,1024]{2,1,0:T(8,128)(2,1)S(1)} %get-tuple-element.24.refs_0_.refs_1_, ...), custom_call_target="tpu_custom_call" | custom-call | tf_op jit(solution)/shard_map/pallas_call | solution.py:534
  110.7 19.2 %all-gather.3 = bf16[384,1024]{1,0:T(8,128)(2,1)S(1)} all-gather(bf16[32,1024]{1,0:T(8,128)(2,1)S(1)} %get-tuple-element.33), channel_id=5, replica_groups=mesh['z'=12,'yl'=2,'c'=2,'x'=4,'yh'=4] {'z'}, dimensions={0}, use_global_device_ids=true | all-gather | bytes 851968 | tf_op jit(solution)/shard_map/all_gather | solution.py:528
  129.9 3.6 %shard_map.82 = (f32[4,16,64]{2,1,0:T(8,128)}, bf16[48,1024]{1,0:T(8,128)(2,1)S(1)}, bf16[48,1024]{1,0:T(8,128)(2,1)S(1)}, bf16[48,1024]{1,0:T(8,128)(2,1)S(1)}, bf16[48,1024]{1,0:T(8,128)(2,1)S(1)}) custom-call(s32[2]{0:T(128)S(1)} %pad_add_fusion.place_ref, bf16[12,32,1024]{2,1,0:T(8,128)(2,1)S(1)} %bitcast.14, ...), custom_call_target="tpu_custom_call" | custom-call | tf_op jit(solution)/shard_map/pallas_call | solution.py:534
  133.6 28.4 %all-to-all-start.1 = ((f32[64,1,64]{2,1,0:T(1,128)}), f32[64,1,64]{2,1,0:T(1,128)S(1)}, u32[]{:S(2)}, u32[]{:S(2)}) async-start(f32[64,1,64]{2,1,0:T(1,128)} %bitcast.9), calls=%async_computation.1 | async-start | bytes 65536 | tf_op jit(solution)/shard_map/all_to_all | solution.py:554
  162.0 2.4 %collective-permute-start.3 = (bf16[48,1024]{1,0:T(8,128)(2,1)S(1)}, bf16[48,1024]{1,0:T(8,128)(2,1)S(1)}, u32[]{:S(2)}, u32[]{:S(2)}) collective-permute-start(bf16[48,1024]{1,0:T(8,128)(2,1)S(1)} %get-tuple-element.36), channel_id=1, source_target_pairs={{0,16},{16,0},{32,48},{48,32},{1,17},{17,1},{33,49},{49,33},{2,18}... | collective-permute-start | bytes 294920 | tf_op jit(solution)/shard_map/ppermute | solution.py:545
  164.4 3.3 %collective-permute-start.4 = (bf16[48,1024]{1,0:T(8,128)(2,1)S(1)}, bf16[48,1024]{1,0:T(8,128)(2,1)S(1)}, u32[]{:S(2)}, u32[]{:S(2)}) collective-permute-start(bf16[48,1024]{1,0:T(8,128)(2,1)S(1)} %get-tuple-element.37), channel_id=1, source_target_pairs={{0,32},{16,48},{32,0},{48,16},{1,33},{17,49},{33,1},{49,17},{2,34}... | collective-permute-start | bytes 294920 | tf_op jit(solution)/shard_map/ppermute | solution.py:545
  167.7 2.2 %collective-permute-start.5 = (bf16[48,1024]{1,0:T(8,128)(2,1)S(1)}, bf16[48,1024]{1,0:T(8,128)(2,1)S(1)}, u32[]{:S(2)}, u32[]{:S(2)}) collective-permute-start(bf16[48,1024]{1,0:T(8,128)(2,1)S(1)} %get-tuple-element.38), channel_id=1, source_target_pairs={{0,48},{16,32},{32,16},{48,0},{1,49},{17,33},{33,17},{49,1},{2,50}... | collective-permute-start | bytes 294920 | tf_op jit(solution)/shard_map/ppermute | solution.py:545
  169.9 1.4 all-to-all-done.1
  171.2 0.1 reduce_sum.9
  171.3 0.5 broadcast_multiply_fusion
  171.9 2.7 %collective-permute-done.5.refs_3_ = bf16[48,1024]{1,0:T(8,128)(2,1)S(1)} collective-permute-done((bf16[48,1024]{1,0:T(8,128)(2,1)S(1)}, bf16[48,1024]{1,0:T(8,128)(2,1)S(1)}, u32[]{:S(2)}, u32[]{:S(2)}) %collective-permute-start.5) | collective-permute-done | bytes 98336 | tf_op jit(solution)/shard_map/ppermute | solution.py:545
  174.6 1.3 shard_map.83
  (15 shorter events, 0.3 us)
Async XLA Ops:
  0.6 27.3 %copy-start.1 = (f32[48,18]{0,1:T(8,128)S(1)}, f32[48,18]{0,1:T(8,128)}, u32[]{:S(2)}) copy-start(f32[48,18]{0,1:T(8,128)} %param.10) | copy-start | bytes 10372
  0.6 27.3 %copy-start.2 = (f32[192]{0:T(256)S(1)}, f32[192]{0:T(256)}, u32[]{:S(2)}) copy-start(f32[192]{0:T(256)} %param.11) | copy-start | bytes 2308
  4.7 14.1 %copy-start = (bf16[1184,512]{1,0:T(8,128)(2,1)S(1)}, bf16[1184,512]{1,0:T(8,128)(2,1)}, u32[]{:S(2)}) copy-start(bf16[1184,512]{1,0:T(8,128)(2,1)} %get-tuple-element.22.refs_0_) | copy-start | bytes 3637252
  4.7 23.6 %all-to-all-start = ((bf16[4,80,1024]{2,1,0:T(8,128)(2,1)}), bf16[4,80,1024]{2,1,0:T(8,128)(2,1)S(1)}, u32[]{:S(2)}, u32[]{:S(2)}) async-start(bf16[4,80,1024]{2,1,0:T(8,128)(2,1)} %get-tuple-element.21), calls=%async_computation | async-start | bytes 1310720 | tf_op jit(solution)/shard_map/all_to_all | solution.py:476
  18.8 34.7 %collective-permute-start = (bf16[1184,512]{1,0:T(8,128)(2,1)S(1)}, bf16[1184,512]{1,0:T(8,128)(2,1)S(1)}, u32[]{:S(2)}, u32[]{:S(2)}) collective-permute-start(bf16[1184,512]{1,0:T(8,128)(2,1)S(1)} %copy-done), channel_id=1, source_target_pairs={{0,16},{16,0},{1,17},{17,1},{2,18},{18,2},{3,19},{19,3},{4,20},{20... | collective-permute-start | bytes 3637256 | tf_op jit(solution)/shard_map/ppermute | solution.py:491
  20.8 32.7 %collective-permute-start.1 = (bf16[1184,512]{1,0:T(8,128)(2,1)S(1)}, bf16[1184,512]{1,0:T(8,128)(2,1)}, u32[]{:S(2)}, u32[]{:S(2)}) collective-permute-start(bf16[1184,512]{1,0:T(8,128)(2,1)S(1)} %copy-done), channel_id=1, source_target_pairs={{0,32},{16,51},{32,1},{48,16},{1,33},{17,48},{33,2},{49,17},{2,34}... | collective-permute-start | bytes 3637256 | tf_op jit(solution)/shard_map/ppermute | solution.py:496
  22.7 30.8 %collective-permute-start.2 = (bf16[1184,512]{1,0:T(8,128)(2,1)S(1)}, bf16[1184,512]{1,0:T(8,128)(2,1)}, u32[]{:S(2)}, u32[]{:S(2)}) collective-permute-start(bf16[1184,512]{1,0:T(8,128)(2,1)S(1)} %copy-done), channel_id=1, source_target_pairs={{0,48},{16,35},{32,17},{48,0},{1,49},{17,32},{33,18},{49,1},{2,50}... | collective-permute-start | bytes 3637256 | tf_op jit(solution)/shard_map/ppermute | solution.py:497
  133.6 37.7 %all-to-all-start.1 = ((f32[64,1,64]{2,1,0:T(1,128)}), f32[64,1,64]{2,1,0:T(1,128)S(1)}, u32[]{:S(2)}, u32[]{:S(2)}) async-start(f32[64,1,64]{2,1,0:T(1,128)} %bitcast.9), calls=%async_computation.1 | async-start | bytes 65536 | tf_op jit(solution)/shard_map/all_to_all | solution.py:554
  162.0 9.9 %collective-permute-start.3 = (bf16[48,1024]{1,0:T(8,128)(2,1)S(1)}, bf16[48,1024]{1,0:T(8,128)(2,1)S(1)}, u32[]{:S(2)}, u32[]{:S(2)}) collective-permute-start(bf16[48,1024]{1,0:T(8,128)(2,1)S(1)} %get-tuple-element.36), channel_id=1, source_target_pairs={{0,16},{16,0},{32,48},{48,32},{1,17},{17,1},{33,49},{49,33},{2,18}... | collective-permute-start | bytes 294920 | tf_op jit(solution)/shard_map/ppermute | solution.py:545
  164.4 7.5 %collective-permute-start.4 = (bf16[48,1024]{1,0:T(8,128)(2,1)S(1)}, bf16[48,1024]{1,0:T(8,128)(2,1)S(1)}, u32[]{:S(2)}, u32[]{:S(2)}) collective-permute-start(bf16[48,1024]{1,0:T(8,128)(2,1)S(1)} %get-tuple-element.37), channel_id=1, source_target_pairs={{0,32},{16,48},{32,0},{48,16},{1,33},{17,49},{33,1},{49,17},{2,34}... | collective-permute-start | bytes 294920 | tf_op jit(solution)/shard_map/ppermute | solution.py:545
  167.7 6.9 %collective-permute-start.5 = (bf16[48,1024]{1,0:T(8,128)(2,1)S(1)}, bf16[48,1024]{1,0:T(8,128)(2,1)S(1)}, u32[]{:S(2)}, u32[]{:S(2)}) collective-permute-start(bf16[48,1024]{1,0:T(8,128)(2,1)S(1)} %get-tuple-element.38), channel_id=1, source_target_pairs={{0,48},{16,32},{32,16},{48,0},{1,49},{17,33},{33,17},{49,1},{2,50}... | collective-permute-start | bytes 294920 | tf_op jit(solution)/shard_map/ppermute | solution.py:545

commit v8 on v7

--- a/solution.py
+++ b/solution.py
@@ -421,7 +421,7 @@
     for r in range(GROUP):
         start = pl.multiple_of(jnp.bitwise_xor(place_ref[0], r) * PIECE, 16)
         copies.append(
-            pltpu.make_async_copy(ins[r], out_ref.at[pl.ds(start, PIECE), :], sems.at[r])
+            pltpu.make_async_copy(ins[GROUP - 1 - r], out_ref.at[pl.ds(start, PIECE), :], sems.at[r])
         )
     run(copies)
     finish(copies)
@@ -549,7 +549,7 @@
         in_specs=[smem()] + [hbm()] * GROUP,
         out_specs=hbm(),
         scratch_shapes=[dma((GROUP,))],
-    )(place, *pieces)
+    )(place, *pieces[::-1])
     parts = GROUP * spread
     terms = lax.all_to_all(
         density.reshape(parts, GROUP * PART // parts), near + ("x", "yh"), 0, 0, tiled=True

time: 176 us -> 174 us (0.989)
  waiting for transfers between devices: 4.22 us -> 1.5 us
    ppermute x3, waiting for transfers between devices: 2.73 us -> 0.01 us  [shards(): lax.ppermute(pieces[r], near, [(k, k ^ r) for k in range(GROUP)])]
  transfers between devices with their start and end apart: 8 -> 8, of which waited for: 3 -> 2; matrix products, arithmetic and copies ran while one was open for 0% -> 0% of each run, Pallas kernels for 0% -> 0%
where the time goes in v8:
time: 174 us; the launch traced here: 173 us
  blocking collectives  88.7 us (51%)
  starting transfers between devices  59.5 us (34%)
  Pallas kernels  21.8 us (13%)
    all_gather x4, blocking collectives, shards(): got = lax.all_gather(message, 'z')  88.7 us
    all_to_all x1, starting transfers between devices, shards(): lax.all_to_all(density.reshape(parts, GROUP * PART // parts), near + ('x'...  28.4 us
    all_to_all x1, starting transfers between devices, shards(): opened = lax.all_to_all(opened, near, 0, 0)  14.1 us
    pallas_call x3, Pallas kernels, shards(): call(functools.partial(step_kernel, degree, factors), out_shape=outs, in_...  10.6 us
    ppermute x3, starting transfers between devices, shards(): lax.ppermute(pieces[r], near, [(k, k ^ r) for k in range(GROUP)])  7.87 us
    pallas_call x1, Pallas kernels, shards(): call(functools.partial(first_kernel, factors), out_shape=[state_shape, me...  5.81 us
    ppermute x1, starting transfers between devices, shards(): lax.ppermute(pack, axes, across(1))  5.19 us
    pallas_call x1, Pallas kernels, shards(): call(open_kernel, megabytes=60, out_shape=[shape((GROUP, HEAD + PIECE, PA...  4 us
  transfers between devices with their start and end apart: 8, of which 2 were waited for; matrix products, arithmetic and copies ran while one was open for 0% of the time, Pallas kernels for 0%

profile of v8, /device:TPU:1, one launch (start us, length us, event | category | flops | bytes accessed | tf_op | source)
XLA Modules:
  0.0 173.2 jit_solution(5038287138609733519)
XLA Ops:
  0.7 4.0 %shard_map.77 = (bf16[4,80,1024]{2,1,0:T(8,128)(2,1)}, bf16[1184,512]{1,0:T(8,128)(2,1)}) custom-call(s32[2,4]{1,0:T(2,128)} %atom_ref.1, bf16[192,1024]{1,0:T(8,128)(2,1)} %bitcast.15, bf16[2,512,512]{2,1,0:T(8,128)(2,1)} %ham_hbm.1, bf16[2,72,512]{2,1,0:T(8,128)(2,1)} %proj_hbm.1), custom_call_target="tpu_custom_call" | custom-call | tf_op jit(solution)/shard_map/pallas_call | solution.py:462
  4.7 14.1 %all-to-all-start = ((bf16[4,80,1024]{2,1,0:T(8,128)(2,1)}), bf16[4,80,1024]{2,1,0:T(8,128)(2,1)S(1)}, u32[]{:S(2)}, u32[]{:S(2)}) async-start(bf16[4,80,1024]{2,1,0:T(8,128)(2,1)} %get-tuple-element.21), calls=%async_computation | async-start | bytes 1310720 | tf_op jit(solution)/shard_map/all_to_all | solution.py:476
  18.8 2.0 %collective-permute-start = (bf16[1184,512]{1,0:T(8,128)(2,1)S(1)}, bf16[1184,512]{1,0:T(8,128)(2,1)S(1)}, u32[]{:S(2)}, u32[]{:S(2)}) collective-permute-start(bf16[1184,512]{1,0:T(8,128)(2,1)S(1)} %copy-done), channel_id=1, source_target_pairs={{0,16},{16,0},{1,17},{17,1},{2,18},{18,2},{3,19},{19,3},{4,20},{20... | collective-permute-start | bytes 3637256 | tf_op jit(solution)/shard_map/ppermute | solution.py:491
  20.8 1.9 %collective-permute-start.1 = (bf16[1184,512]{1,0:T(8,128)(2,1)S(1)}, bf16[1184,512]{1,0:T(8,128)(2,1)}, u32[]{:S(2)}, u32[]{:S(2)}) collective-permute-start(bf16[1184,512]{1,0:T(8,128)(2,1)S(1)} %copy-done), channel_id=1, source_target_pairs={{0,32},{16,51},{32,1},{48,16},{1,33},{17,48},{33,2},{49,17},{2,34}... | collective-permute-start | bytes 3637256 | tf_op jit(solution)/shard_map/ppermute | solution.py:496
  22.7 5.2 %collective-permute-start.2 = (bf16[1184,512]{1,0:T(8,128)(2,1)S(1)}, bf16[1184,512]{1,0:T(8,128)(2,1)}, u32[]{:S(2)}, u32[]{:S(2)}) collective-permute-start(bf16[1184,512]{1,0:T(8,128)(2,1)S(1)} %copy-done), channel_id=1, source_target_pairs={{0,48},{16,35},{32,17},{48,0},{1,49},{17,32},{33,18},{49,1},{2,50}... | collective-permute-start | bytes 3637256 | tf_op jit(solution)/shard_map/ppermute | solution.py:497
  27.9 0.1 copy.9.coupling_ref
  28.0 0.1 reshape.11
  28.2 0.1 all-to-all-done.in_ref.open_hbm
  28.4 25.1 %all-gather = bf16[480,1024]{1,0:T(8,128)(2,1)S(1)} all-gather(bf16[40,1024]{1,0:T(8,128)(2,1)S(1)} %shard_map.78), channel_id=2, replica_groups=mesh['z'=12,'yl'=2,'c'=2,'x'=4,'yh'=4] {'z'}, dimensions={0}, use_global_device_ids=true | all-gather | bytes 1064960 | tf_op jit(solution)/shard_map/all_gather | solution.py:509
  53.5 5.8 %shard_map.79 = (bf16[4,48,1024]{2,1,0:T(8,128)(2,1)S(1)}, bf16[32,1024]{1,0:T(8,128)(2,1)S(1)}, bf16[4,48,1024]{2,1,0:T(8,128)(2,1)S(1)}, bf16[8,512,512]{2,1,0...) custom-call(s32[2]{0:T(128)S(1)} %pad_add_fusion.place_ref, ...), custom_call_target="tpu_custom_call" | custom-call | tf_op jit(solution)/shard_map/pallas_call | solution.py:510
  59.3 23.7 %all-gather.1 = bf16[384,1024]{1,0:T(8,128)(2,1)S(1)} all-gather(bf16[32,1024]{1,0:T(8,128)(2,1)S(1)} %get-tuple-element.23), channel_id=3, replica_groups=mesh['z'=12,'yl'=2,'c'=2,'x'=4,'yh'=4] {'z'}, dimensions={0}, use_global_device_ids=true | all-gather | bytes 851968 | tf_op jit(solution)/shard_map/all_gather | solution.py:528
  83.0 3.5 %shard_map.80 = (bf16[4,48,1024]{2,1,0:T(8,128)(2,1)S(1)}, bf16[32,1024]{1,0:T(8,128)(2,1)S(1)}) custom-call(s32[2]{0:T(128)S(1)} %pad_add_fusion.place_ref, bf16[12,32,1024]{2,1,0:T(8,128)(2,1)S(1)} %bitcast.12, bf16[4,48,1024]{2,1,0:T(8,128)(2,1)S(1)} %get-tuple-element.24.refs_0_.refs_1_, bf16[4,48,1024]{2,1,0:T(8,128)(2,1)S(1)} %get-tuple-element.25.refs_1_, ...), custom_call_target="tpu_custom_call" | custom-call | tf_op jit(solution)/shard_map/pallas_call | solution.py:534
  86.5 20.6 %all-gather.2 = bf16[384,1024]{1,0:T(8,128)(2,1)S(1)} all-gather(bf16[32,1024]{1,0:T(8,128)(2,1)S(1)} %get-tuple-element.31), channel_id=4, replica_groups=mesh['z'=12,'yl'=2,'c'=2,'x'=4,'yh'=4] {'z'}, dimensions={0}, use_global_device_ids=true | all-gather | bytes 851968 | tf_op jit(solution)/shard_map/all_gather | solution.py:528
  107.2 3.5 %shard_map.81 = (bf16[4,48,1024]{2,1,0:T(8,128)(2,1)S(1)}, bf16[32,1024]{1,0:T(8,128)(2,1)S(1)}) custom-call(s32[2]{0:T(128)S(1)} %pad_add_fusion.place_ref, bf16[12,32,1024]{2,1,0:T(8,128)(2,1)S(1)} %bitcast.13, bf16[4,48,1024]{2,1,0:T(8,128)(2,1)S(1)} %get-tuple-element.32.refs_0_.refs_1_, bf16[4,48,1024]{2,1,0:T(8,128)(2,1)S(1)} %get-tuple-element.24.refs_0_.refs_1_, ...), custom_call_target="tpu_custom_call" | custom-call | tf_op jit(solution)/shard_map/pallas_call | solution.py:534
  110.7 19.2 %all-gather.3 = bf16[384,1024]{1,0:T(8,128)(2,1)S(1)} all-gather(bf16[32,1024]{1,0:T(8,128)(2,1)S(1)} %get-tuple-element.33), channel_id=5, replica_groups=mesh['z'=12,'yl'=2,'c'=2,'x'=4,'yh'=4] {'z'}, dimensions={0}, use_global_device_ids=true | all-gather | bytes 851968 | tf_op jit(solution)/shard_map/all_gather | solution.py:528
  129.9 3.6 %shard_map.82 = (f32[4,16,64]{2,1,0:T(8,128)}, bf16[48,1024]{1,0:T(8,128)(2,1)S(1)}, bf16[48,1024]{1,0:T(8,128)(2,1)S(1)}, bf16[48,1024]{1,0:T(8,128)(2,1)S(1)}, bf16[48,1024]{1,0:T(8,128)(2,1)S(1)}) custom-call(s32[2]{0:T(128)S(1)} %pad_add_fusion.place_ref, bf16[12,32,1024]{2,1,0:T(8,128)(2,1)S(1)} %bitcast.14, ...), custom_call_target="tpu_custom_call" | custom-call | tf_op jit(solution)/shard_map/pallas_call | solution.py:534
  133.6 28.4 %all-to-all-start.1 = ((f32[64,1,64]{2,1,0:T(1,128)}), f32[64,1,64]{2,1,0:T(1,128)S(1)}, u32[]{:S(2)}, u32[]{:S(2)}) async-start(f32[64,1,64]{2,1,0:T(1,128)} %bitcast.9), calls=%async_computation.1 | async-start | bytes 65536 | tf_op jit(solution)/shard_map/all_to_all | solution.py:554
  162.0 3.6 %collective-permute-start.3 = (bf16[48,1024]{1,0:T(8,128)(2,1)S(1)}, bf16[48,1024]{1,0:T(8,128)(2,1)S(1)}, u32[]{:S(2)}, u32[]{:S(2)}) collective-permute-start(bf16[48,1024]{1,0:T(8,128)(2,1)S(1)} %get-tuple-element.35), channel_id=1, source_target_pairs={{0,48},{16,32},{32,16},{48,0},{1,49},{17,33},{33,17},{49,1},{2,50}... | collective-permute-start | bytes 294920 | tf_op jit(solution)/shard_map/ppermute | solution.py:545
  165.6 2.0 %collective-permute-start.4 = (bf16[48,1024]{1,0:T(8,128)(2,1)S(1)}, bf16[48,1024]{1,0:T(8,128)(2,1)S(1)}, u32[]{:S(2)}, u32[]{:S(2)}) collective-permute-start(bf16[48,1024]{1,0:T(8,128)(2,1)S(1)} %get-tuple-element.36), channel_id=1, source_target_pairs={{0,32},{16,48},{32,0},{48,16},{1,33},{17,49},{33,1},{49,17},{2,34}... | collective-permute-start | bytes 294920 | tf_op jit(solution)/shard_map/ppermute | solution.py:545
  167.6 2.3 %collective-permute-start.5 = (bf16[48,1024]{1,0:T(8,128)(2,1)S(1)}, bf16[48,1024]{1,0:T(8,128)(2,1)S(1)}, u32[]{:S(2)}, u32[]{:S(2)}) collective-permute-start(bf16[48,1024]{1,0:T(8,128)(2,1)S(1)} %get-tuple-element.37), channel_id=1, source_target_pairs={{0,16},{16,0},{32,48},{48,32},{1,17},{17,1},{33,49},{49,33},{2,18}... | collective-permute-start | bytes 294920 | tf_op jit(solution)/shard_map/ppermute | solution.py:545
  169.9 1.4 all-to-all-done.1
  171.2 0.1 reduce_sum.9
  171.3 0.5 broadcast_multiply_fusion
  171.9 1.3 shard_map.83
  (15 shorter events, 0.2 us)
Async XLA Ops:
  0.6 27.3 %copy-start.1 = (f32[48,18]{0,1:T(8,128)S(1)}, f32[48,18]{0,1:T(8,128)}, u32[]{:S(2)}) copy-start(f32[48,18]{0,1:T(8,128)} %param.10) | copy-start | bytes 10372
  0.6 27.3 %copy-start.2 = (f32[192]{0:T(256)S(1)}, f32[192]{0:T(256)}, u32[]{:S(2)}) copy-start(f32[192]{0:T(256)} %param.11) | copy-start | bytes 2308
  4.7 14.1 %copy-start = (bf16[1184,512]{1,0:T(8,128)(2,1)S(1)}, bf16[1184,512]{1,0:T(8,128)(2,1)}, u32[]{:S(2)}) copy-start(bf16[1184,512]{1,0:T(8,128)(2,1)} %get-tuple-element.22.refs_0_) | copy-start | bytes 3637252
  4.7 23.6 %all-to-all-start = ((bf16[4,80,1024]{2,1,0:T(8,128)(2,1)}), bf16[4,80,1024]{2,1,0:T(8,128)(2,1)S(1)}, u32[]{:S(2)}, u32[]{:S(2)}) async-start(bf16[4,80,1024]{2,1,0:T(8,128)(2,1)} %get-tuple-element.21), calls=%async_computation | async-start | bytes 1310720 | tf_op jit(solution)/shard_map/all_to_all | solution.py:476
  18.8 34.7 %collective-permute-start = (bf16[1184,512]{1,0:T(8,128)(2,1)S(1)}, bf16[1184,512]{1,0:T(8,128)(2,1)S(1)}, u32[]{:S(2)}, u32[]{:S(2)}) collective-permute-start(bf16[1184,512]{1,0:T(8,128)(2,1)S(1)} %copy-done), channel_id=1, source_target_pairs={{0,16},{16,0},{1,17},{17,1},{2,18},{18,2},{3,19},{19,3},{4,20},{20... | collective-permute-start | bytes 3637256 | tf_op jit(solution)/shard_map/ppermute | solution.py:491
  20.8 32.7 %collective-permute-start.1 = (bf16[1184,512]{1,0:T(8,128)(2,1)S(1)}, bf16[1184,512]{1,0:T(8,128)(2,1)}, u32[]{:S(2)}, u32[]{:S(2)}) collective-permute-start(bf16[1184,512]{1,0:T(8,128)(2,1)S(1)} %copy-done), channel_id=1, source_target_pairs={{0,32},{16,51},{32,1},{48,16},{1,33},{17,48},{33,2},{49,17},{2,34}... | collective-permute-start | bytes 3637256 | tf_op jit(solution)/shard_map/ppermute | solution.py:496
  22.7 30.8 %collective-permute-start.2 = (bf16[1184,512]{1,0:T(8,128)(2,1)S(1)}, bf16[1184,512]{1,0:T(8,128)(2,1)}, u32[]{:S(2)}, u32[]{:S(2)}) collective-permute-start(bf16[1184,512]{1,0:T(8,128)(2,1)S(1)} %copy-done), channel_id=1, source_target_pairs={{0,48},{16,35},{32,17},{48,0},{1,49},{17,32},{33,18},{49,1},{2,50}... | collective-permute-start | bytes 3637256 | tf_op jit(solution)/shard_map/ppermute | solution.py:497
  133.6 37.7 %all-to-all-start.1 = ((f32[64,1,64]{2,1,0:T(1,128)}), f32[64,1,64]{2,1,0:T(1,128)S(1)}, u32[]{:S(2)}, u32[]{:S(2)}) async-start(f32[64,1,64]{2,1,0:T(1,128)} %bitcast.9), calls=%async_computation.1 | async-start | bytes 65536 | tf_op jit(solution)/shard_map/all_to_all | solution.py:554
  162.0 9.9 %collective-permute-start.3 = (bf16[48,1024]{1,0:T(8,128)(2,1)S(1)}, bf16[48,1024]{1,0:T(8,128)(2,1)S(1)}, u32[]{:S(2)}, u32[]{:S(2)}) collective-permute-start(bf16[48,1024]{1,0:T(8,128)(2,1)S(1)} %get-tuple-element.35), channel_id=1, source_target_pairs={{0,48},{16,32},{32,16},{48,0},{1,49},{17,33},{33,17},{49,1},{2,50}... | collective-permute-start | bytes 294920 | tf_op jit(solution)/shard_map/ppermute | solution.py:545
  165.6 6.2 %collective-permute-start.4 = (bf16[48,1024]{1,0:T(8,128)(2,1)S(1)}, bf16[48,1024]{1,0:T(8,128)(2,1)S(1)}, u32[]{:S(2)}, u32[]{:S(2)}) collective-permute-start(bf16[48,1024]{1,0:T(8,128)(2,1)S(1)} %get-tuple-element.36), channel_id=1, source_target_pairs={{0,32},{16,48},{32,0},{48,16},{1,33},{17,49},{33,1},{49,17},{2,34}... | collective-permute-start | bytes 294920 | tf_op jit(solution)/shard_map/ppermute | solution.py:545
  167.6 4.2 %collective-permute-start.5 = (bf16[48,1024]{1,0:T(8,128)(2,1)S(1)}, bf16[48,1024]{1,0:T(8,128)(2,1)S(1)}, u32[]{:S(2)}, u32[]{:S(2)}) collective-permute-start(bf16[48,1024]{1,0:T(8,128)(2,1)S(1)} %get-tuple-element.37), channel_id=1, source_target_pairs={{0,16},{16,0},{32,48},{48,32},{1,17},{17,1},{33,49},{49,33},{2,18}... | collective-permute-start | bytes 294920 | tf_op jit(solution)/shard_map/ppermute | solution.py:545

commit v9 on v8

--- a/solution.py
+++ b/solution.py
@@ -168,6 +168,13 @@
     finish(hams)
 
 
+def read(got_ref, group, rows, lane, width):
+    start = group * PART + lane
+    if not isinstance(group, int):
+        start = pl.multiple_of(start, LANES)
+    return got_ref[:rows, pl.ds(start, width)]
+
+
 def place_face(face, wide_ref):
     wide_ref[:BODY, WIDE:] = face[:BODY]
     for k in range(PIECE - BODY):
@@ -176,7 +183,7 @@
 
 
 def read_face(got_ref, group):
-    body = got_ref[group, :BODY, :].astype(F32)
+    body = read(got_ref, group, BODY, 0, PART).astype(F32)
     rows = [body[:, WIDE:]]
     for k in range(PIECE - BODY):
         row = (k % GROUP) * BLOCKS + BLOCKS - 1
@@ -215,11 +222,11 @@
 
 
 def choose(place_ref, coupling_ref, got_ref, pick_ref, factor_ref):
-    groups = got_ref.shape[0]
+    groups = got_ref.shape[1] // PART
     z, below, above = beside(place_ref, groups)
     lane = iota((8, LANES), 1)
     named = lambda group: jnp.broadcast_to(
-        got_ref[group, :16, tile(6)].astype(F32)[BLOCKS - 1 : BLOCKS], (8, LANES)
+        read(got_ref, group, 16, 6 * LANES, LANES).astype(F32)[BLOCKS - 1 : BLOCKS], (8, LANES)
     )
     shift = lambda x, by: pltpu.roll(x, by, 1) if by else x
     per = LANES // BODY
@@ -245,8 +252,8 @@
 
 
 def sum_coefs(got_ref, pick_ref, factor_ref, scaled_ref):
-    groups = got_ref.shape[0]
-    blocks = jnp.concatenate([got_ref[group, :BODY, :WIDE] for group in range(groups)], axis=0)
+    groups = got_ref.shape[1] // PART
+    blocks = jnp.concatenate([read(got_ref, g, BODY, 0, WIDE) for g in range(groups)], axis=0)
     total = dot(pick_ref[:, : groups * BODY], blocks) * factor_ref[...]
     for i in range(NPROJ):
         column = total[:, i * PIECE : (i + 1) * PIECE]
@@ -256,7 +263,7 @@
 
 
 def add_faces(place_ref, got_ref, near_ref, scaled, local_ref):
-    groups = got_ref.shape[0]
+    groups = got_ref.shape[1] // PART
     z, below, above = beside(place_ref, groups)
     low = low_lanes(PIECE)
     from_below = read_face(got_ref, below) + dot_tn(scaled[GROUP], near_ref[0])
@@ -325,7 +332,7 @@
     packs, refs = refs[:GROUP], refs[GROUP:]
     next_ref, message_ref, v_ref, held_ref, proj_ref, near_ref, pick_ref, factor_ref = refs[:8]
     local_ref, edge_ref, wide_ref, scaled_ref, raw_ref, sems = refs[8:]
-    groups = got_ref.shape[0]
+    groups = got_ref.shape[1] // PART
     me = place_ref[0]
     _, below, above = beside(place_ref, groups)
     copies = []
@@ -342,7 +349,7 @@
 
     place0, place1 = placers()
     for k, group, place in ((0, below, place1), (1, above, place0)):
-        rows = got_ref[group].astype(F32)
+        rows = read(got_ref, group, BODY + 8, 0, PART).astype(F32)
         raw = [rows[BODY:, tile(j)] for j in range(8)]
         for j in range(8):
             row = (j % GROUP) * BLOCKS + BLOCKS - 1
@@ -506,7 +513,7 @@
         pltpu.VMEM((BODY, PART), F32),
         pltpu.VMEM((GROUP + 2, PROJ, PIECE), F32),
     ]
-    got = lax.all_gather(message, "z")
+    got = lax.all_gather(message, "z", axis=1, tiled=True)
     v, message, old, *kept = call(
         functools.partial(first_kernel, factors),
         out_shape=[
@@ -525,7 +532,7 @@
         + [pltpu.VMEM((GROUP, 2 * PADDED, NODES), BF16), dma((4 * GROUP,))],
     )(place, coupling, got, opened, *packs)
     for degree in range(1, DEGREE):
-        got = lax.all_gather(message, "z")
+        got = lax.all_gather(message, "z", axis=1, tiled=True)
         last = degree == DEGREE - 1
         outs = [state_shape, message_shape]
         if last:

time: 174 us -> 174 us (level)
  no operation moved by 1% of the time
where the time goes in v9:
time: 174 us; the launch traced here: 173 us
  blocking collectives  88.7 us (51%)
  starting transfers between devices  59.5 us (34%)
  Pallas kernels  21.8 us (13%)
    all_gather x4, blocking collectives, shards(): got = lax.all_gather(message, 'z', axis=1, tiled=True)  88.7 us
    all_to_all x1, starting transfers between devices, shards(): lax.all_to_all(density.reshape(parts, GROUP * PART // parts), near + ('x'...  28.4 us
    all_to_all x1, starting transfers between devices, shards(): opened = lax.all_to_all(opened, near, 0, 0)  14.1 us
    pallas_call x3, Pallas kernels, shards(): call(functools.partial(step_kernel, degree, factors), out_shape=outs, in_...  10.6 us
    ppermute x3, starting transfers between devices, shards(): lax.ppermute(pieces[r], near, [(k, k ^ r) for k in range(GROUP)])  7.87 us
    pallas_call x1, Pallas kernels, shards(): call(functools.partial(first_kernel, factors), out_shape=[state_shape, me...  5.81 us
    ppermute x1, starting transfers between devices, shards(): lax.ppermute(pack, axes, across(1))  5.19 us
    pallas_call x1, Pallas kernels, shards(): call(open_kernel, megabytes=60, out_shape=[shape((GROUP, HEAD + PIECE, PA...  4 us
  transfers between devices with their start and end apart: 8, of which 2 were waited for; matrix products, arithmetic and copies ran while one was open for 0% of the time, Pallas kernels for 0%

profile of v9, /device:TPU:1, one launch (start us, length us, event | category | flops | bytes accessed | tf_op | source)
XLA Modules:
  0.0 173.2 jit_solution(1874034528342089838)
XLA Ops:
  0.7 4.0 %shard_map.77 = (bf16[4,80,1024]{2,1,0:T(8,128)(2,1)}, bf16[1184,512]{1,0:T(8,128)(2,1)}) custom-call(s32[2,4]{1,0:T(2,128)} %atom_ref.1, bf16[192,1024]{1,0:T(8,128)(2,1)} %bitcast.7, bf16[2,512,512]{2,1,0:T(8,128)(2,1)} %ham_hbm.1, bf16[2,72,512]{2,1,0:T(8,128)(2,1)} %proj_hbm.1), custom_call_target="tpu_custom_call" | custom-call | tf_op jit(solution)/shard_map/pallas_call | solution.py:469
  4.7 14.1 %all-to-all-start = ((bf16[4,80,1024]{2,1,0:T(8,128)(2,1)}), bf16[4,80,1024]{2,1,0:T(8,128)(2,1)S(1)}, u32[]{:S(2)}, u32[]{:S(2)}) async-start(bf16[4,80,1024]{2,1,0:T(8,128)(2,1)} %get-tuple-element.21), calls=%async_computation | async-start | bytes 1310720 | tf_op jit(solution)/shard_map/all_to_all | solution.py:483
  18.8 2.0 %collective-permute-start = (bf16[1184,512]{1,0:T(8,128)(2,1)S(1)}, bf16[1184,512]{1,0:T(8,128)(2,1)S(1)}, u32[]{:S(2)}, u32[]{:S(2)}) collective-permute-start(bf16[1184,512]{1,0:T(8,128)(2,1)S(1)} %copy-done), channel_id=1, source_target_pairs={{0,16},{16,0},{1,17},{17,1},{2,18},{18,2},{3,19},{19,3},{4,20},{20... | collective-permute-start | bytes 3637256 | tf_op jit(solution)/shard_map/ppermute | solution.py:498
  20.8 1.9 %collective-permute-start.1 = (bf16[1184,512]{1,0:T(8,128)(2,1)S(1)}, bf16[1184,512]{1,0:T(8,128)(2,1)}, u32[]{:S(2)}, u32[]{:S(2)}) collective-permute-start(bf16[1184,512]{1,0:T(8,128)(2,1)S(1)} %copy-done), channel_id=1, source_target_pairs={{0,32},{16,51},{32,1},{48,16},{1,33},{17,48},{33,2},{49,17},{2,34}... | collective-permute-start | bytes 3637256 | tf_op jit(solution)/shard_map/ppermute | solution.py:503
  22.7 5.2 %collective-permute-start.2 = (bf16[1184,512]{1,0:T(8,128)(2,1)S(1)}, bf16[1184,512]{1,0:T(8,128)(2,1)}, u32[]{:S(2)}, u32[]{:S(2)}) collective-permute-start(bf16[1184,512]{1,0:T(8,128)(2,1)S(1)} %copy-done), channel_id=1, source_target_pairs={{0,48},{16,35},{32,17},{48,0},{1,49},{17,32},{33,18},{49,1},{2,50}... | collective-permute-start | bytes 3637256 | tf_op jit(solution)/shard_map/ppermute | solution.py:504
  27.9 0.1 copy.9.coupling_ref
  28.0 0.1 reshape.11
  28.2 0.1 all-to-all-done.in_ref.open_hbm
  28.4 25.1 %all_gather.12.got_ref = bf16[40,12288]{1,0:T(8,128)(2,1)S(1)} all-gather(bf16[40,1024]{1,0:T(8,128)(2,1)S(1)} %shard_map.78), channel_id=1, replica_groups=mesh['z'=12,'yl'=2,'c'=2,'x'=4,'yh'=4] {'z'}, dimensions={1}, use_global_device_ids=true | all-gather | bytes 1064960 | tf_op jit(solution)/shard_map/all_gather | solution.py:516
  53.5 5.8 %shard_map.79 = (bf16[4,48,1024]{2,1,0:T(8,128)(2,1)S(1)}, bf16[32,1024]{1,0:T(8,128)(2,1)S(1)}, bf16[4,48,1024]{2,1,0:T(8,128)(2,1)S(1)}, bf16[8,512,512]{2,1,0...) custom-call(s32[2]{0:T(128)S(1)} %pad_add_fusion.place_ref, ...), custom_call_target="tpu_custom_call" | custom-call | tf_op jit(solution)/shard_map/pallas_call | solution.py:517
  59.3 23.7 %all_gather.13.got_ref = bf16[32,12288]{1,0:T(8,128)(2,1)S(1)} all-gather(bf16[32,1024]{1,0:T(8,128)(2,1)S(1)} %get-tuple-element.23), channel_id=1, replica_groups=mesh['z'=12,'yl'=2,'c'=2,'x'=4,'yh'=4] {'z'}, dimensions={1}, use_global_device_ids=true | all-gather | bytes 851968 | tf_op jit(solution)/shard_map/all_gather | solution.py:535
  83.0 3.5 %shard_map.80 = (bf16[4,48,1024]{2,1,0:T(8,128)(2,1)S(1)}, bf16[32,1024]{1,0:T(8,128)(2,1)S(1)}) custom-call(s32[2]{0:T(128)S(1)} %pad_add_fusion.place_ref, bf16[32,12288]{1,0:T(8,128)(2,1)S(1)} %all_gather.13.got_ref, bf16[4,48,1024]{2,1,0:T(8,128)(2,1)S(1)} %get-tuple-element.24.refs_0_.refs_1_, bf16[4,48,1024]{2,1,0:T(8,128)(2,1)S(1)} %get-tuple-element.25.refs_1_, ...), custom_call_target="tpu_custom_call" | custom-call | tf_op jit(solution)/shard_map/pallas_call | solution.py:541
  86.5 20.6 %all_gather.14.got_ref = bf16[32,12288]{1,0:T(8,128)(2,1)S(1)} all-gather(bf16[32,1024]{1,0:T(8,128)(2,1)S(1)} %get-tuple-element.31), channel_id=1, replica_groups=mesh['z'=12,'yl'=2,'c'=2,'x'=4,'yh'=4] {'z'}, dimensions={1}, use_global_device_ids=true | all-gather | bytes 851968 | tf_op jit(solution)/shard_map/all_gather | solution.py:535
  107.1 3.5 %shard_map.81 = (bf16[4,48,1024]{2,1,0:T(8,128)(2,1)S(1)}, bf16[32,1024]{1,0:T(8,128)(2,1)S(1)}) custom-call(s32[2]{0:T(128)S(1)} %pad_add_fusion.place_ref, bf16[32,12288]{1,0:T(8,128)(2,1)S(1)} %all_gather.14.got_ref, bf16[4,48,1024]{2,1,0:T(8,128)(2,1)S(1)} %get-tuple-element.32.refs_0_.refs_1_, ...), custom_call_target="tpu_custom_call" | custom-call | tf_op jit(solution)/shard_map/pallas_call | solution.py:541
  110.6 19.3 %all_gather.15.got_ref = bf16[32,12288]{1,0:T(8,128)(2,1)S(1)} all-gather(bf16[32,1024]{1,0:T(8,128)(2,1)S(1)} %get-tuple-element.33), channel_id=1, replica_groups=mesh['z'=12,'yl'=2,'c'=2,'x'=4,'yh'=4] {'z'}, dimensions={1}, use_global_device_ids=true | all-gather | bytes 851968 | tf_op jit(solution)/shard_map/all_gather | solution.py:535
  129.9 3.6 %shard_map.82 = (f32[4,16,64]{2,1,0:T(8,128)}, bf16[48,1024]{1,0:T(8,128)(2,1)S(1)}, bf16[48,1024]{1,0:T(8,128)(2,1)S(1)}, bf16[48,1024]{1,0:T(8,128)(2,1)S(1)}, bf16[48,1024]{1,0:T(8,128)(2,1)S(1)}) custom-call(s32[2]{0:T(128)S(1)} %pad_add_fusion.place_ref, bf16[32,12288]{1,0:T(8,128)(2,1)S(1)} %all_gather.15.got_ref, ...), custom_call_target="tpu_custom_call" | custom-call | tf_op jit(solution)/shard_map/pallas_call | solution.py:541
  133.6 28.4 %all-to-all-start.1 = ((f32[64,1,64]{2,1,0:T(1,128)}), f32[64,1,64]{2,1,0:T(1,128)S(1)}, u32[]{:S(2)}, u32[]{:S(2)}) async-start(f32[64,1,64]{2,1,0:T(1,128)} %bitcast.5), calls=%async_computation.1 | async-start | bytes 65536 | tf_op jit(solution)/shard_map/all_to_all | solution.py:561
  162.0 3.6 %collective-permute-start.3 = (bf16[48,1024]{1,0:T(8,128)(2,1)S(1)}, bf16[48,1024]{1,0:T(8,128)(2,1)S(1)}, u32[]{:S(2)}, u32[]{:S(2)}) collective-permute-start(bf16[48,1024]{1,0:T(8,128)(2,1)S(1)} %get-tuple-element.35), channel_id=1, source_target_pairs={{0,48},{16,32},{32,16},{48,0},{1,49},{17,33},{33,17},{49,1},{2,50}... | collective-permute-start | bytes 294920 | tf_op jit(solution)/shard_map/ppermute | solution.py:552
  165.6 2.0 %collective-permute-start.4 = (bf16[48,1024]{1,0:T(8,128)(2,1)S(1)}, bf16[48,1024]{1,0:T(8,128)(2,1)S(1)}, u32[]{:S(2)}, u32[]{:S(2)}) collective-permute-start(bf16[48,1024]{1,0:T(8,128)(2,1)S(1)} %get-tuple-element.36), channel_id=1, source_target_pairs={{0,32},{16,48},{32,0},{48,16},{1,33},{17,49},{33,1},{49,17},{2,34}... | collective-permute-start | bytes 294920 | tf_op jit(solution)/shard_map/ppermute | solution.py:552
  167.6 2.3 %collective-permute-start.5 = (bf16[48,1024]{1,0:T(8,128)(2,1)S(1)}, bf16[48,1024]{1,0:T(8,128)(2,1)S(1)}, u32[]{:S(2)}, u32[]{:S(2)}) collective-permute-start(bf16[48,1024]{1,0:T(8,128)(2,1)S(1)} %get-tuple-element.37), channel_id=1, source_target_pairs={{0,16},{16,0},{32,48},{48,32},{1,17},{17,1},{33,49},{49,33},{2,18}... | collective-permute-start | bytes 294920 | tf_op jit(solution)/shard_map/ppermute | solution.py:552
  169.9 1.4 all-to-all-done.1
  171.2 0.1 reduce_sum.9
  171.3 0.5 broadcast_multiply_fusion
  171.9 1.3 shard_map.83
  (15 shorter events, 0.2 us)
Async XLA Ops:
  0.6 27.3 %copy-start.1 = (f32[48,18]{0,1:T(8,128)S(1)}, f32[48,18]{0,1:T(8,128)}, u32[]{:S(2)}) copy-start(f32[48,18]{0,1:T(8,128)} %param.10) | copy-start | bytes 10372
  0.6 27.3 %copy-start.2 = (f32[192]{0:T(256)S(1)}, f32[192]{0:T(256)}, u32[]{:S(2)}) copy-start(f32[192]{0:T(256)} %param.11) | copy-start | bytes 2308
  4.7 14.1 %copy-start = (bf16[1184,512]{1,0:T(8,128)(2,1)S(1)}, bf16[1184,512]{1,0:T(8,128)(2,1)}, u32[]{:S(2)}) copy-start(bf16[1184,512]{1,0:T(8,128)(2,1)} %get-tuple-element.22.refs_0_) | copy-start | bytes 3637252
  4.7 23.6 %all-to-all-start = ((bf16[4,80,1024]{2,1,0:T(8,128)(2,1)}), bf16[4,80,1024]{2,1,0:T(8,128)(2,1)S(1)}, u32[]{:S(2)}, u32[]{:S(2)}) async-start(bf16[4,80,1024]{2,1,0:T(8,128)(2,1)} %get-tuple-element.21), calls=%async_computation | async-start | bytes 1310720 | tf_op jit(solution)/shard_map/all_to_all | solution.py:483
  18.8 34.7 %collective-permute-start = (bf16[1184,512]{1,0:T(8,128)(2,1)S(1)}, bf16[1184,512]{1,0:T(8,128)(2,1)S(1)}, u32[]{:S(2)}, u32[]{:S(2)}) collective-permute-start(bf16[1184,512]{1,0:T(8,128)(2,1)S(1)} %copy-done), channel_id=1, source_target_pairs={{0,16},{16,0},{1,17},{17,1},{2,18},{18,2},{3,19},{19,3},{4,20},{20... | collective-permute-start | bytes 3637256 | tf_op jit(solution)/shard_map/ppermute | solution.py:498
  20.8 32.7 %collective-permute-start.1 = (bf16[1184,512]{1,0:T(8,128)(2,1)S(1)}, bf16[1184,512]{1,0:T(8,128)(2,1)}, u32[]{:S(2)}, u32[]{:S(2)}) collective-permute-start(bf16[1184,512]{1,0:T(8,128)(2,1)S(1)} %copy-done), channel_id=1, source_target_pairs={{0,32},{16,51},{32,1},{48,16},{1,33},{17,48},{33,2},{49,17},{2,34}... | collective-permute-start | bytes 3637256 | tf_op jit(solution)/shard_map/ppermute | solution.py:503
  22.7 30.8 %collective-permute-start.2 = (bf16[1184,512]{1,0:T(8,128)(2,1)S(1)}, bf16[1184,512]{1,0:T(8,128)(2,1)}, u32[]{:S(2)}, u32[]{:S(2)}) collective-permute-start(bf16[1184,512]{1,0:T(8,128)(2,1)S(1)} %copy-done), channel_id=1, source_target_pairs={{0,48},{16,35},{32,17},{48,0},{1,49},{17,32},{33,18},{49,1},{2,50}... | collective-permute-start | bytes 3637256 | tf_op jit(solution)/shard_map/ppermute | solution.py:504
  133.6 37.7 %all-to-all-start.1 = ((f32[64,1,64]{2,1,0:T(1,128)}), f32[64,1,64]{2,1,0:T(1,128)S(1)}, u32[]{:S(2)}, u32[]{:S(2)}) async-start(f32[64,1,64]{2,1,0:T(1,128)} %bitcast.5), calls=%async_computation.1 | async-start | bytes 65536 | tf_op jit(solution)/shard_map/all_to_all | solution.py:561
  162.0 9.9 %collective-permute-start.3 = (bf16[48,1024]{1,0:T(8,128)(2,1)S(1)}, bf16[48,1024]{1,0:T(8,128)(2,1)S(1)}, u32[]{:S(2)}, u32[]{:S(2)}) collective-permute-start(bf16[48,1024]{1,0:T(8,128)(2,1)S(1)} %get-tuple-element.35), channel_id=1, source_target_pairs={{0,48},{16,32},{32,16},{48,0},{1,49},{17,33},{33,17},{49,1},{2,50}... | collective-permute-start | bytes 294920 | tf_op jit(solution)/shard_map/ppermute | solution.py:552
  165.6 6.2 %collective-permute-start.4 = (bf16[48,1024]{1,0:T(8,128)(2,1)S(1)}, bf16[48,1024]{1,0:T(8,128)(2,1)S(1)}, u32[]{:S(2)}, u32[]{:S(2)}) collective-permute-start(bf16[48,1024]{1,0:T(8,128)(2,1)S(1)} %get-tuple-element.36), channel_id=1, source_target_pairs={{0,32},{16,48},{32,0},{48,16},{1,33},{17,49},{33,1},{49,17},{2,34}... | collective-permute-start | bytes 294920 | tf_op jit(solution)/shard_map/ppermute | solution.py:552
  167.6 4.2 %collective-permute-start.5 = (bf16[48,1024]{1,0:T(8,128)(2,1)S(1)}, bf16[48,1024]{1,0:T(8,128)(2,1)S(1)}, u32[]{:S(2)}, u32[]{:S(2)}) collective-permute-start(bf16[48,1024]{1,0:T(8,128)(2,1)S(1)} %get-tuple-element.37), channel_id=1, source_target_pairs={{0,16},{16,0},{32,48},{48,32},{1,17},{17,1},{33,49},{49,33},{2,18}... | collective-permute-start | bytes 294920 | tf_op jit(solution)/shard_map/ppermute | solution.py:552

commit v10 on v9

--- a/solution.py
+++ b/solution.py
@@ -329,7 +329,7 @@
 
 
 def first_kernel(factors, place_ref, coupling_ref, got_ref, open_hbm, *refs):
-    packs, refs = refs[:GROUP], refs[GROUP:]
+    packs, refs = (refs[0], refs[3], refs[1], refs[2]), refs[GROUP:]
     next_ref, message_ref, v_ref, held_ref, proj_ref, near_ref, pick_ref, factor_ref = refs[:8]
     local_ref, edge_ref, wide_ref, scaled_ref, raw_ref, sems = refs[8:]
     groups = got_ref.shape[1] // PART
@@ -495,13 +495,12 @@
             (spot(y, c), spot((y + 1 - 2 * c) % ring, c ^ flip)) for y in range(ring) for c in (0, 1)
         ]
 
-    beside_core = lax.ppermute(pack, "c", [(0, 1), (1, 0)])
     axes = ("yl", "c", "yh")
     packs = [
         pack,
-        beside_core,
         lax.ppermute(pack, axes, across(0)),
         lax.ppermute(pack, axes, across(1)),
+        lax.ppermute(pack, "c", [(0, 1), (1, 0)]),
     ]
 
     factors = chebyshev_factors()

time: 174 us -> 172 us (0.989)
  no operation moved by 1% of the time
where the time goes in v10:
time: 172 us
  blocking collectives  87.3 us (51%)
  starting transfers between devices  59 us (34%)
  Pallas kernels  22 us (13%)
  waiting for transfers between devices  1.83 us (1%)
    all_gather x4, blocking collectives, shards(): got = lax.all_gather(message, 'z', axis=1, tiled=True)  87.3 us
    all_to_all x1, starting transfers between devices, shards(): lax.all_to_all(density.reshape(parts, GROUP * PART // parts), near + ('x'...  28.4 us
    all_to_all x1, starting transfers between devices, shards(): opened = lax.all_to_all(opened, near, 0, 0)  14.1 us
    pallas_call x3, Pallas kernels, shards(): call(functools.partial(step_kernel, degree, factors), out_shape=outs, in_...  10.6 us
    ppermute x3, starting transfers between devices, shards(): lax.ppermute(pieces[r], near, [(k, k ^ r) for k in range(GROUP)])  7.87 us
    pallas_call x1, Pallas kernels, shards(): call(functools.partial(first_kernel, factors), out_shape=[state_shape, me...  5.97 us
    ppermute x1, starting transfers between devices, shards(): lax.ppermute(pack, axes, across(1))  4.8 us
    pallas_call x1, Pallas kernels, shards(): call(open_kernel, megabytes=60, out_shape=[shape((GROUP, HEAD + PIECE, PA...  4 us
  transfers between devices with their start and end apart: 8, of which 2 were waited for; matrix products, arithmetic and copies ran while one was open for 0% of the time, Pallas kernels for 0%

profile of v10, /device:TPU:1, one launch (start us, length us, event | category | flops | bytes accessed | tf_op | source)
XLA Modules:
  0.0 171.8 jit_solution(2460467659111451348)
XLA Ops:
  0.7 4.0 %shard_map.77 = (bf16[4,80,1024]{2,1,0:T(8,128)(2,1)}, bf16[1184,512]{1,0:T(8,128)(2,1)}) custom-call(s32[2,4]{1,0:T(2,128)} %atom_ref.1, bf16[192,1024]{1,0:T(8,128)(2,1)} %bitcast.7, bf16[2,512,512]{2,1,0:T(8,128)(2,1)} %ham_hbm.1, bf16[2,72,512]{2,1,0:T(8,128)(2,1)} %proj_hbm.1), custom_call_target="tpu_custom_call" | custom-call | tf_op jit(solution)/shard_map/pallas_call | solution.py:469
  4.7 14.1 %all-to-all-start = ((bf16[4,80,1024]{2,1,0:T(8,128)(2,1)}), bf16[4,80,1024]{2,1,0:T(8,128)(2,1)S(1)}, u32[]{:S(2)}, u32[]{:S(2)}) async-start(bf16[4,80,1024]{2,1,0:T(8,128)(2,1)} %get-tuple-element.21), calls=%async_computation | async-start | bytes 1310720 | tf_op jit(solution)/shard_map/all_to_all | solution.py:483
  18.8 1.9 %collective-permute-start = (bf16[1184,512]{1,0:T(8,128)(2,1)S(1)}, bf16[1184,512]{1,0:T(8,128)(2,1)S(1)}, u32[]{:S(2)}, u32[]{:S(2)}) collective-permute-start(bf16[1184,512]{1,0:T(8,128)(2,1)S(1)} %copy-done), channel_id=1, source_target_pairs={{0,32},{16,51},{32,1},{48,16},{1,33},{17,48},{33,2},{49,17},{2,34}... | collective-permute-start | bytes 3637256 | tf_op jit(solution)/shard_map/ppermute | solution.py:501
  20.7 4.8 %collective-permute-start.1 = (bf16[1184,512]{1,0:T(8,128)(2,1)S(1)}, bf16[1184,512]{1,0:T(8,128)(2,1)}, u32[]{:S(2)}, u32[]{:S(2)}) collective-permute-start(bf16[1184,512]{1,0:T(8,128)(2,1)S(1)} %copy-done), channel_id=1, source_target_pairs={{0,48},{16,35},{32,17},{48,0},{1,49},{17,32},{33,18},{49,1},{2,50}... | collective-permute-start | bytes 3637256 | tf_op jit(solution)/shard_map/ppermute | solution.py:502
  25.5 1.9 %collective-permute-start.2 = (bf16[1184,512]{1,0:T(8,128)(2,1)S(1)}, bf16[1184,512]{1,0:T(8,128)(2,1)}, u32[]{:S(2)}, u32[]{:S(2)}) collective-permute-start(bf16[1184,512]{1,0:T(8,128)(2,1)S(1)} %copy-done), channel_id=1, source_target_pairs={{0,16},{16,0},{1,17},{17,1},{2,18},{18,2},{3,19},{19,3},{4,20},{20... | collective-permute-start | bytes 3637256 | tf_op jit(solution)/shard_map/ppermute | solution.py:503
  27.5 0.1 copy.9.coupling_ref
  27.6 0.1 reshape.11
  27.7 0.5 all-to-all-done.in_ref.open_hbm
  28.2 25.4 %all_gather.12.got_ref = bf16[40,12288]{1,0:T(8,128)(2,1)S(1)} all-gather(bf16[40,1024]{1,0:T(8,128)(2,1)S(1)} %shard_map.78), channel_id=1, replica_groups=mesh['z'=12,'yl'=2,'c'=2,'x'=4,'yh'=4] {'z'}, dimensions={1}, use_global_device_ids=true | all-gather | bytes 1064960 | tf_op jit(solution)/shard_map/all_gather | solution.py:515
  53.6 6.0 %shard_map.79 = (bf16[4,48,1024]{2,1,0:T(8,128)(2,1)S(1)}, bf16[32,1024]{1,0:T(8,128)(2,1)S(1)}, bf16[4,48,1024]{2,1,0:T(8,128)(2,1)S(1)}, bf16[8,512,512]{2,1,0...) custom-call(s32[2]{0:T(128)S(1)} %pad_add_fusion.place_ref, ...), custom_call_target="tpu_custom_call" | custom-call | tf_op jit(solution)/shard_map/pallas_call | solution.py:516
  59.6 21.8 %all_gather.13.got_ref = bf16[32,12288]{1,0:T(8,128)(2,1)S(1)} all-gather(bf16[32,1024]{1,0:T(8,128)(2,1)S(1)} %get-tuple-element.23), channel_id=1, replica_groups=mesh['z'=12,'yl'=2,'c'=2,'x'=4,'yh'=4] {'z'}, dimensions={1}, use_global_device_ids=true | all-gather | bytes 851968 | tf_op jit(solution)/shard_map/all_gather | solution.py:534
  81.4 3.5 %shard_map.80 = (bf16[4,48,1024]{2,1,0:T(8,128)(2,1)S(1)}, bf16[32,1024]{1,0:T(8,128)(2,1)S(1)}) custom-call(s32[2]{0:T(128)S(1)} %pad_add_fusion.place_ref, bf16[32,12288]{1,0:T(8,128)(2,1)S(1)} %all_gather.13.got_ref, bf16[4,48,1024]{2,1,0:T(8,128)(2,1)S(1)} %get-tuple-element.24.refs_0_.refs_1_, bf16[4,48,1024]{2,1,0:T(8,128)(2,1)S(1)} %get-tuple-element.25.refs_1_, ...), custom_call_target="tpu_custom_call" | custom-call | tf_op jit(solution)/shard_map/pallas_call | solution.py:540
  84.9 19.5 %all_gather.14.got_ref = bf16[32,12288]{1,0:T(8,128)(2,1)S(1)} all-gather(bf16[32,1024]{1,0:T(8,128)(2,1)S(1)} %get-tuple-element.31), channel_id=1, replica_groups=mesh['z'=12,'yl'=2,'c'=2,'x'=4,'yh'=4] {'z'}, dimensions={1}, use_global_device_ids=true | all-gather | bytes 851968 | tf_op jit(solution)/shard_map/all_gather | solution.py:534
  104.4 3.5 %shard_map.81 = (bf16[4,48,1024]{2,1,0:T(8,128)(2,1)S(1)}, bf16[32,1024]{1,0:T(8,128)(2,1)S(1)}) custom-call(s32[2]{0:T(128)S(1)} %pad_add_fusion.place_ref, bf16[32,12288]{1,0:T(8,128)(2,1)S(1)} %all_gather.14.got_ref, bf16[4,48,1024]{2,1,0:T(8,128)(2,1)S(1)} %get-tuple-element.32.refs_0_.refs_1_, ...), custom_call_target="tpu_custom_call" | custom-call | tf_op jit(solution)/shard_map/pallas_call | solution.py:540
  107.9 20.7 %all_gather.15.got_ref = bf16[32,12288]{1,0:T(8,128)(2,1)S(1)} all-gather(bf16[32,1024]{1,0:T(8,128)(2,1)S(1)} %get-tuple-element.33), channel_id=1, replica_groups=mesh['z'=12,'yl'=2,'c'=2,'x'=4,'yh'=4] {'z'}, dimensions={1}, use_global_device_ids=true | all-gather | bytes 851968 | tf_op jit(solution)/shard_map/all_gather | solution.py:534
  128.6 3.6 %shard_map.82 = (f32[4,16,64]{2,1,0:T(8,128)}, bf16[48,1024]{1,0:T(8,128)(2,1)S(1)}, bf16[48,1024]{1,0:T(8,128)(2,1)S(1)}, bf16[48,1024]{1,0:T(8,128)(2,1)S(1)}, bf16[48,1024]{1,0:T(8,128)(2,1)S(1)}) custom-call(s32[2]{0:T(128)S(1)} %pad_add_fusion.place_ref, bf16[32,12288]{1,0:T(8,128)(2,1)S(1)} %all_gather.15.got_ref, ...), custom_call_target="tpu_custom_call" | custom-call | tf_op jit(solution)/shard_map/pallas_call | solution.py:540
  132.2 28.4 %all-to-all-start.1 = ((f32[64,1,64]{2,1,0:T(1,128)}), f32[64,1,64]{2,1,0:T(1,128)S(1)}, u32[]{:S(2)}, u32[]{:S(2)}) async-start(f32[64,1,64]{2,1,0:T(1,128)} %bitcast.5), calls=%async_computation.1 | async-start | bytes 65536 | tf_op jit(solution)/shard_map/all_to_all | solution.py:560
  160.7 3.6 %collective-permute-start.3 = (bf16[48,1024]{1,0:T(8,128)(2,1)S(1)}, bf16[48,1024]{1,0:T(8,128)(2,1)S(1)}, u32[]{:S(2)}, u32[]{:S(2)}) collective-permute-start(bf16[48,1024]{1,0:T(8,128)(2,1)S(1)} %get-tuple-element.35), channel_id=1, source_target_pairs={{0,48},{16,32},{32,16},{48,0},{1,49},{17,33},{33,17},{49,1},{2,50}... | collective-permute-start | bytes 294920 | tf_op jit(solution)/shard_map/ppermute | solution.py:551
  164.3 2.0 %collective-permute-start.4 = (bf16[48,1024]{1,0:T(8,128)(2,1)S(1)}, bf16[48,1024]{1,0:T(8,128)(2,1)S(1)}, u32[]{:S(2)}, u32[]{:S(2)}) collective-permute-start(bf16[48,1024]{1,0:T(8,128)(2,1)S(1)} %get-tuple-element.36), channel_id=1, source_target_pairs={{0,32},{16,48},{32,0},{48,16},{1,33},{17,49},{33,1},{49,17},{2,34}... | collective-permute-start | bytes 294920 | tf_op jit(solution)/shard_map/ppermute | solution.py:551
  166.3 2.3 %collective-permute-start.5 = (bf16[48,1024]{1,0:T(8,128)(2,1)S(1)}, bf16[48,1024]{1,0:T(8,128)(2,1)S(1)}, u32[]{:S(2)}, u32[]{:S(2)}) collective-permute-start(bf16[48,1024]{1,0:T(8,128)(2,1)S(1)} %get-tuple-element.37), channel_id=1, source_target_pairs={{0,16},{16,0},{32,48},{48,32},{1,17},{17,1},{33,49},{49,33},{2,18}... | collective-permute-start | bytes 294920 | tf_op jit(solution)/shard_map/ppermute | solution.py:551
  168.5 1.4 all-to-all-done.1
  169.9 0.1 reduce_sum.9
  170.0 0.5 broadcast_multiply_fusion
  170.5 1.3 shard_map.83
  (15 shorter events, 0.2 us)
Async XLA Ops:
  0.6 26.8 %copy-start.1 = (f32[48,18]{0,1:T(8,128)S(1)}, f32[48,18]{0,1:T(8,128)}, u32[]{:S(2)}) copy-start(f32[48,18]{0,1:T(8,128)} %param.10) | copy-start | bytes 10372
  0.6 26.9 %copy-start.2 = (f32[192]{0:T(256)S(1)}, f32[192]{0:T(256)}, u32[]{:S(2)}) copy-start(f32[192]{0:T(256)} %param.11) | copy-start | bytes 2308
  4.7 14.1 %copy-start = (bf16[1184,512]{1,0:T(8,128)(2,1)S(1)}, bf16[1184,512]{1,0:T(8,128)(2,1)}, u32[]{:S(2)}) copy-start(bf16[1184,512]{1,0:T(8,128)(2,1)} %get-tuple-element.22.refs_0_) | copy-start | bytes 3637252
  4.7 23.5 %all-to-all-start = ((bf16[4,80,1024]{2,1,0:T(8,128)(2,1)}), bf16[4,80,1024]{2,1,0:T(8,128)(2,1)S(1)}, u32[]{:S(2)}, u32[]{:S(2)}) async-start(bf16[4,80,1024]{2,1,0:T(8,128)(2,1)} %get-tuple-element.21), calls=%async_computation | async-start | bytes 1310720 | tf_op jit(solution)/shard_map/all_to_all | solution.py:483
  18.8 34.8 %collective-permute-start = (bf16[1184,512]{1,0:T(8,128)(2,1)S(1)}, bf16[1184,512]{1,0:T(8,128)(2,1)S(1)}, u32[]{:S(2)}, u32[]{:S(2)}) collective-permute-start(bf16[1184,512]{1,0:T(8,128)(2,1)S(1)} %copy-done), channel_id=1, source_target_pairs={{0,32},{16,51},{32,1},{48,16},{1,33},{17,48},{33,2},{49,17},{2,34}... | collective-permute-start | bytes 3637256 | tf_op jit(solution)/shard_map/ppermute | solution.py:501
  20.7 32.9 %collective-permute-start.1 = (bf16[1184,512]{1,0:T(8,128)(2,1)S(1)}, bf16[1184,512]{1,0:T(8,128)(2,1)}, u32[]{:S(2)}, u32[]{:S(2)}) collective-permute-start(bf16[1184,512]{1,0:T(8,128)(2,1)S(1)} %copy-done), channel_id=1, source_target_pairs={{0,48},{16,35},{32,17},{48,0},{1,49},{17,32},{33,18},{49,1},{2,50}... | collective-permute-start | bytes 3637256 | tf_op jit(solution)/shard_map/ppermute | solution.py:502
  25.5 28.1 %collective-permute-start.2 = (bf16[1184,512]{1,0:T(8,128)(2,1)S(1)}, bf16[1184,512]{1,0:T(8,128)(2,1)}, u32[]{:S(2)}, u32[]{:S(2)}) collective-permute-start(bf16[1184,512]{1,0:T(8,128)(2,1)S(1)} %copy-done), channel_id=1, source_target_pairs={{0,16},{16,0},{1,17},{17,1},{2,18},{18,2},{3,19},{19,3},{4,20},{20... | collective-permute-start | bytes 3637256 | tf_op jit(solution)/shard_map/ppermute | solution.py:503
  132.2 37.7 %all-to-all-start.1 = ((f32[64,1,64]{2,1,0:T(1,128)}), f32[64,1,64]{2,1,0:T(1,128)S(1)}, u32[]{:S(2)}, u32[]{:S(2)}) async-start(f32[64,1,64]{2,1,0:T(1,128)} %bitcast.5), calls=%async_computation.1 | async-start | bytes 65536 | tf_op jit(solution)/shard_map/all_to_all | solution.py:560
  160.7 9.9 %collective-permute-start.3 = (bf16[48,1024]{1,0:T(8,128)(2,1)S(1)}, bf16[48,1024]{1,0:T(8,128)(2,1)S(1)}, u32[]{:S(2)}, u32[]{:S(2)}) collective-permute-start(bf16[48,1024]{1,0:T(8,128)(2,1)S(1)} %get-tuple-element.35), channel_id=1, source_target_pairs={{0,48},{16,32},{32,16},{48,0},{1,49},{17,33},{33,17},{49,1},{2,50}... | collective-permute-start | bytes 294920 | tf_op jit(solution)/shard_map/ppermute | solution.py:551
  164.3 6.2 %collective-permute-start.4 = (bf16[48,1024]{1,0:T(8,128)(2,1)S(1)}, bf16[48,1024]{1,0:T(8,128)(2,1)S(1)}, u32[]{:S(2)}, u32[]{:S(2)}) collective-permute-start(bf16[48,1024]{1,0:T(8,128)(2,1)S(1)} %get-tuple-element.36), channel_id=1, source_target_pairs={{0,32},{16,48},{32,0},{48,16},{1,33},{17,49},{33,1},{49,17},{2,34}... | collective-permute-start | bytes 294920 | tf_op jit(solution)/shard_map/ppermute | solution.py:551
  166.3 4.2 %collective-permute-start.5 = (bf16[48,1024]{1,0:T(8,128)(2,1)S(1)}, bf16[48,1024]{1,0:T(8,128)(2,1)S(1)}, u32[]{:S(2)}, u32[]{:S(2)}) collective-permute-start(bf16[48,1024]{1,0:T(8,128)(2,1)S(1)} %get-tuple-element.37), channel_id=1, source_target_pairs={{0,16},{16,0},{32,48},{48,32},{1,17},{17,1},{33,49},{49,33},{2,18}... | collective-permute-start | bytes 294920 | tf_op jit(solution)/shard_map/ppermute | solution.py:551

commit v11 on v10

--- a/solution.py
+++ b/solution.py
@@ -295,8 +295,9 @@
     )
 
 
-def add_local(me, v_ref, held_ref, local_ref):
+def add_local(me, v_ref, held_ref, local_ref, hams=()):
     for r in range(GROUP):
+        finish(hams[2 * r : 2 * r + 2])
         part = jnp.bitwise_xor(me, r)
         for cell in range(2):
             lanes = slice(cell * NODES, (cell + 1) * NODES)
@@ -367,8 +368,7 @@
             proj_ref[part, :, lanes] = dot(place, raw).astype(BF16)
     for part in range(GROUP):
         local_ref[part] = dot_tn(scaled[part], proj_ref[part])
-    finish(hams)
-    add_local(me, v_ref, held_ref, local_ref)
+    add_local(me, v_ref, held_ref, local_ref, hams)
     add_faces(place_ref, got_ref, near_ref, scaled, local_ref)
     gain, _ = factors[0]
     new = []

time: 172 us -> 173 us (level)
  no operation moved by 1% of the time
where the time goes in v11:
time: 173 us; the launch traced here: 172 us
  blocking collectives  87.4 us (51%)
  starting transfers between devices  59 us (34%)
  Pallas kernels  22.2 us (13%)
  waiting for transfers between devices  1.83 us (1%)
    all_gather x4, blocking collectives, shards(): got = lax.all_gather(message, 'z', axis=1, tiled=True)  87.4 us
    all_to_all x1, starting transfers between devices, shards(): lax.all_to_all(density.reshape(parts, GROUP * PART // parts), near + ('x'...  28.4 us
    all_to_all x1, starting transfers between devices, shards(): opened = lax.all_to_all(opened, near, 0, 0)  14.1 us
    pallas_call x3, Pallas kernels, shards(): call(functools.partial(step_kernel, degree, factors), out_shape=outs, in_...  10.6 us
    ppermute x3, starting transfers between devices, shards(): lax.ppermute(pieces[r], near, [(k, k ^ r) for k in range(GROUP)])  7.87 us
    pallas_call x1, Pallas kernels, shards(): call(functools.partial(first_kernel, factors), out_shape=[state_shape, me...  6.15 us
    ppermute x1, starting transfers between devices, shards(): lax.ppermute(pack, axes, across(1))  4.8 us
    pallas_call x1, Pallas kernels, shards(): call(open_kernel, megabytes=60, out_shape=[shape((GROUP, HEAD + PIECE, PA...  4 us
  transfers between devices with their start and end apart: 8, of which 2 were waited for; matrix products, arithmetic and copies ran while one was open for 0% of the time, Pallas kernels for 0%

profile of v11, /device:TPU:1, one launch (start us, length us, event | category | flops | bytes accessed | tf_op | source)
XLA Modules:
  0.0 172.0 jit_solution(5361786981104204962)
XLA Ops:
  0.7 4.0 %shard_map.77 = (bf16[4,80,1024]{2,1,0:T(8,128)(2,1)}, bf16[1184,512]{1,0:T(8,128)(2,1)}) custom-call(s32[2,4]{1,0:T(2,128)} %atom_ref.1, bf16[192,1024]{1,0:T(8,128)(2,1)} %bitcast.7, bf16[2,512,512]{2,1,0:T(8,128)(2,1)} %ham_hbm.1, bf16[2,72,512]{2,1,0:T(8,128)(2,1)} %proj_hbm.1), custom_call_target="tpu_custom_call" | custom-call | tf_op jit(solution)/shard_map/pallas_call | solution.py:469
  4.7 14.1 %all-to-all-start = ((bf16[4,80,1024]{2,1,0:T(8,128)(2,1)}), bf16[4,80,1024]{2,1,0:T(8,128)(2,1)S(1)}, u32[]{:S(2)}, u32[]{:S(2)}) async-start(bf16[4,80,1024]{2,1,0:T(8,128)(2,1)} %get-tuple-element.21), calls=%async_computation | async-start | bytes 1310720 | tf_op jit(solution)/shard_map/all_to_all | solution.py:483
  18.8 1.9 %collective-permute-start = (bf16[1184,512]{1,0:T(8,128)(2,1)S(1)}, bf16[1184,512]{1,0:T(8,128)(2,1)S(1)}, u32[]{:S(2)}, u32[]{:S(2)}) collective-permute-start(bf16[1184,512]{1,0:T(8,128)(2,1)S(1)} %copy-done), channel_id=1, source_target_pairs={{0,32},{16,51},{32,1},{48,16},{1,33},{17,48},{33,2},{49,17},{2,34}... | collective-permute-start | bytes 3637256 | tf_op jit(solution)/shard_map/ppermute | solution.py:501
  20.7 4.8 %collective-permute-start.1 = (bf16[1184,512]{1,0:T(8,128)(2,1)S(1)}, bf16[1184,512]{1,0:T(8,128)(2,1)}, u32[]{:S(2)}, u32[]{:S(2)}) collective-permute-start(bf16[1184,512]{1,0:T(8,128)(2,1)S(1)} %copy-done), channel_id=1, source_target_pairs={{0,48},{16,35},{32,17},{48,0},{1,49},{17,32},{33,18},{49,1},{2,50}... | collective-permute-start | bytes 3637256 | tf_op jit(solution)/shard_map/ppermute | solution.py:502
  25.5 1.9 %collective-permute-start.2 = (bf16[1184,512]{1,0:T(8,128)(2,1)S(1)}, bf16[1184,512]{1,0:T(8,128)(2,1)}, u32[]{:S(2)}, u32[]{:S(2)}) collective-permute-start(bf16[1184,512]{1,0:T(8,128)(2,1)S(1)} %copy-done), channel_id=1, source_target_pairs={{0,16},{16,0},{1,17},{17,1},{2,18},{18,2},{3,19},{19,3},{4,20},{20... | collective-permute-start | bytes 3637256 | tf_op jit(solution)/shard_map/ppermute | solution.py:503
  27.5 0.1 copy.9.coupling_ref
  27.6 0.1 reshape.11
  27.7 0.5 all-to-all-done.in_ref.open_hbm
  28.2 25.4 %all_gather.12.got_ref = bf16[40,12288]{1,0:T(8,128)(2,1)S(1)} all-gather(bf16[40,1024]{1,0:T(8,128)(2,1)S(1)} %shard_map.78), channel_id=1, replica_groups=mesh['z'=12,'yl'=2,'c'=2,'x'=4,'yh'=4] {'z'}, dimensions={1}, use_global_device_ids=true | all-gather | bytes 1064960 | tf_op jit(solution)/shard_map/all_gather | solution.py:515
  53.6 6.1 %shard_map.79 = (bf16[4,48,1024]{2,1,0:T(8,128)(2,1)S(1)}, bf16[32,1024]{1,0:T(8,128)(2,1)S(1)}, bf16[4,48,1024]{2,1,0:T(8,128)(2,1)S(1)}, bf16[8,512,512]{2,1,0...) custom-call(s32[2]{0:T(128)S(1)} %pad_add_fusion.place_ref, ...), custom_call_target="tpu_custom_call" | custom-call | tf_op jit(solution)/shard_map/pallas_call | solution.py:516
  59.8 21.8 %all_gather.13.got_ref = bf16[32,12288]{1,0:T(8,128)(2,1)S(1)} all-gather(bf16[32,1024]{1,0:T(8,128)(2,1)S(1)} %get-tuple-element.23), channel_id=1, replica_groups=mesh['z'=12,'yl'=2,'c'=2,'x'=4,'yh'=4] {'z'}, dimensions={1}, use_global_device_ids=true | all-gather | bytes 851968 | tf_op jit(solution)/shard_map/all_gather | solution.py:534
  81.6 3.5 %shard_map.80 = (bf16[4,48,1024]{2,1,0:T(8,128)(2,1)S(1)}, bf16[32,1024]{1,0:T(8,128)(2,1)S(1)}) custom-call(s32[2]{0:T(128)S(1)} %pad_add_fusion.place_ref, bf16[32,12288]{1,0:T(8,128)(2,1)S(1)} %all_gather.13.got_ref, bf16[4,48,1024]{2,1,0:T(8,128)(2,1)S(1)} %get-tuple-element.24.refs_0_.refs_1_, bf16[4,48,1024]{2,1,0:T(8,128)(2,1)S(1)} %get-tuple-element.25.refs_1_, ...), custom_call_target="tpu_custom_call" | custom-call | tf_op jit(solution)/shard_map/pallas_call | solution.py:540
  85.1 19.5 %all_gather.14.got_ref = bf16[32,12288]{1,0:T(8,128)(2,1)S(1)} all-gather(bf16[32,1024]{1,0:T(8,128)(2,1)S(1)} %get-tuple-element.31), channel_id=1, replica_groups=mesh['z'=12,'yl'=2,'c'=2,'x'=4,'yh'=4] {'z'}, dimensions={1}, use_global_device_ids=true | all-gather | bytes 851968 | tf_op jit(solution)/shard_map/all_gather | solution.py:534
  104.6 3.5 %shard_map.81 = (bf16[4,48,1024]{2,1,0:T(8,128)(2,1)S(1)}, bf16[32,1024]{1,0:T(8,128)(2,1)S(1)}) custom-call(s32[2]{0:T(128)S(1)} %pad_add_fusion.place_ref, bf16[32,12288]{1,0:T(8,128)(2,1)S(1)} %all_gather.14.got_ref, bf16[4,48,1024]{2,1,0:T(8,128)(2,1)S(1)} %get-tuple-element.32.refs_0_.refs_1_, ...), custom_call_target="tpu_custom_call" | custom-call | tf_op jit(solution)/shard_map/pallas_call | solution.py:540
  108.1 20.7 %all_gather.15.got_ref = bf16[32,12288]{1,0:T(8,128)(2,1)S(1)} all-gather(bf16[32,1024]{1,0:T(8,128)(2,1)S(1)} %get-tuple-element.33), channel_id=1, replica_groups=mesh['z'=12,'yl'=2,'c'=2,'x'=4,'yh'=4] {'z'}, dimensions={1}, use_global_device_ids=true | all-gather | bytes 851968 | tf_op jit(solution)/shard_map/all_gather | solution.py:534
  128.8 3.6 %shard_map.82 = (f32[4,16,64]{2,1,0:T(8,128)}, bf16[48,1024]{1,0:T(8,128)(2,1)S(1)}, bf16[48,1024]{1,0:T(8,128)(2,1)S(1)}, bf16[48,1024]{1,0:T(8,128)(2,1)S(1)}, bf16[48,1024]{1,0:T(8,128)(2,1)S(1)}) custom-call(s32[2]{0:T(128)S(1)} %pad_add_fusion.place_ref, bf16[32,12288]{1,0:T(8,128)(2,1)S(1)} %all_gather.15.got_ref, ...), custom_call_target="tpu_custom_call" | custom-call | tf_op jit(solution)/shard_map/pallas_call | solution.py:540
  132.4 28.4 %all-to-all-start.1 = ((f32[64,1,64]{2,1,0:T(1,128)}), f32[64,1,64]{2,1,0:T(1,128)S(1)}, u32[]{:S(2)}, u32[]{:S(2)}) async-start(f32[64,1,64]{2,1,0:T(1,128)} %bitcast.5), calls=%async_computation.1 | async-start | bytes 65536 | tf_op jit(solution)/shard_map/all_to_all | solution.py:560
  160.9 3.6 %collective-permute-start.3 = (bf16[48,1024]{1,0:T(8,128)(2,1)S(1)}, bf16[48,1024]{1,0:T(8,128)(2,1)S(1)}, u32[]{:S(2)}, u32[]{:S(2)}) collective-permute-start(bf16[48,1024]{1,0:T(8,128)(2,1)S(1)} %get-tuple-element.35), channel_id=1, source_target_pairs={{0,48},{16,32},{32,16},{48,0},{1,49},{17,33},{33,17},{49,1},{2,50}... | collective-permute-start | bytes 294920 | tf_op jit(solution)/shard_map/ppermute | solution.py:551
  164.5 2.0 %collective-permute-start.4 = (bf16[48,1024]{1,0:T(8,128)(2,1)S(1)}, bf16[48,1024]{1,0:T(8,128)(2,1)S(1)}, u32[]{:S(2)}, u32[]{:S(2)}) collective-permute-start(bf16[48,1024]{1,0:T(8,128)(2,1)S(1)} %get-tuple-element.36), channel_id=1, source_target_pairs={{0,32},{16,48},{32,0},{48,16},{1,33},{17,49},{33,1},{49,17},{2,34}... | collective-permute-start | bytes 294920 | tf_op jit(solution)/shard_map/ppermute | solution.py:551
  166.5 2.3 %collective-permute-start.5 = (bf16[48,1024]{1,0:T(8,128)(2,1)S(1)}, bf16[48,1024]{1,0:T(8,128)(2,1)S(1)}, u32[]{:S(2)}, u32[]{:S(2)}) collective-permute-start(bf16[48,1024]{1,0:T(8,128)(2,1)S(1)} %get-tuple-element.37), channel_id=1, source_target_pairs={{0,16},{16,0},{32,48},{48,32},{1,17},{17,1},{33,49},{49,33},{2,18}... | collective-permute-start | bytes 294920 | tf_op jit(solution)/shard_map/ppermute | solution.py:551
  168.8 1.4 all-to-all-done.1
  170.1 0.1 reduce_sum.9
  170.2 0.5 broadcast_multiply_fusion
  170.7 1.3 shard_map.83
  (15 shorter events, 0.2 us)
Async XLA Ops:
  0.6 26.8 %copy-start.1 = (f32[48,18]{0,1:T(8,128)S(1)}, f32[48,18]{0,1:T(8,128)}, u32[]{:S(2)}) copy-start(f32[48,18]{0,1:T(8,128)} %param.10) | copy-start | bytes 10372
  0.6 26.9 %copy-start.2 = (f32[192]{0:T(256)S(1)}, f32[192]{0:T(256)}, u32[]{:S(2)}) copy-start(f32[192]{0:T(256)} %param.11) | copy-start | bytes 2308
  4.7 14.1 %copy-start = (bf16[1184,512]{1,0:T(8,128)(2,1)S(1)}, bf16[1184,512]{1,0:T(8,128)(2,1)}, u32[]{:S(2)}) copy-start(bf16[1184,512]{1,0:T(8,128)(2,1)} %get-tuple-element.22.refs_0_) | copy-start | bytes 3637252
  4.7 23.5 %all-to-all-start = ((bf16[4,80,1024]{2,1,0:T(8,128)(2,1)}), bf16[4,80,1024]{2,1,0:T(8,128)(2,1)S(1)}, u32[]{:S(2)}, u32[]{:S(2)}) async-start(bf16[4,80,1024]{2,1,0:T(8,128)(2,1)} %get-tuple-element.21), calls=%async_computation | async-start | bytes 1310720 | tf_op jit(solution)/shard_map/all_to_all | solution.py:483
  18.8 34.8 %collective-permute-start = (bf16[1184,512]{1,0:T(8,128)(2,1)S(1)}, bf16[1184,512]{1,0:T(8,128)(2,1)S(1)}, u32[]{:S(2)}, u32[]{:S(2)}) collective-permute-start(bf16[1184,512]{1,0:T(8,128)(2,1)S(1)} %copy-done), channel_id=1, source_target_pairs={{0,32},{16,51},{32,1},{48,16},{1,33},{17,48},{33,2},{49,17},{2,34}... | collective-permute-start | bytes 3637256 | tf_op jit(solution)/shard_map/ppermute | solution.py:501
  20.7 32.9 %collective-permute-start.1 = (bf16[1184,512]{1,0:T(8,128)(2,1)S(1)}, bf16[1184,512]{1,0:T(8,128)(2,1)}, u32[]{:S(2)}, u32[]{:S(2)}) collective-permute-start(bf16[1184,512]{1,0:T(8,128)(2,1)S(1)} %copy-done), channel_id=1, source_target_pairs={{0,48},{16,35},{32,17},{48,0},{1,49},{17,32},{33,18},{49,1},{2,50}... | collective-permute-start | bytes 3637256 | tf_op jit(solution)/shard_map/ppermute | solution.py:502
  25.5 28.1 %collective-permute-start.2 = (bf16[1184,512]{1,0:T(8,128)(2,1)S(1)}, bf16[1184,512]{1,0:T(8,128)(2,1)}, u32[]{:S(2)}, u32[]{:S(2)}) collective-permute-start(bf16[1184,512]{1,0:T(8,128)(2,1)S(1)} %copy-done), channel_id=1, source_target_pairs={{0,16},{16,0},{1,17},{17,1},{2,18},{18,2},{3,19},{19,3},{4,20},{20... | collective-permute-start | bytes 3637256 | tf_op jit(solution)/shard_map/ppermute | solution.py:503
  132.4 37.7 %all-to-all-start.1 = ((f32[64,1,64]{2,1,0:T(1,128)}), f32[64,1,64]{2,1,0:T(1,128)S(1)}, u32[]{:S(2)}, u32[]{:S(2)}) async-start(f32[64,1,64]{2,1,0:T(1,128)} %bitcast.5), calls=%async_computation.1 | async-start | bytes 65536 | tf_op jit(solution)/shard_map/all_to_all | solution.py:560
  160.9 9.9 %collective-permute-start.3 = (bf16[48,1024]{1,0:T(8,128)(2,1)S(1)}, bf16[48,1024]{1,0:T(8,128)(2,1)S(1)}, u32[]{:S(2)}, u32[]{:S(2)}) collective-permute-start(bf16[48,1024]{1,0:T(8,128)(2,1)S(1)} %get-tuple-element.35), channel_id=1, source_target_pairs={{0,48},{16,32},{32,16},{48,0},{1,49},{17,33},{33,17},{49,1},{2,50}... | collective-permute-start | bytes 294920 | tf_op jit(solution)/shard_map/ppermute | solution.py:551
  164.5 6.2 %collective-permute-start.4 = (bf16[48,1024]{1,0:T(8,128)(2,1)S(1)}, bf16[48,1024]{1,0:T(8,128)(2,1)S(1)}, u32[]{:S(2)}, u32[]{:S(2)}) collective-permute-start(bf16[48,1024]{1,0:T(8,128)(2,1)S(1)} %get-tuple-element.36), channel_id=1, source_target_pairs={{0,32},{16,48},{32,0},{48,16},{1,33},{17,49},{33,1},{49,17},{2,34}... | collective-permute-start | bytes 294920 | tf_op jit(solution)/shard_map/ppermute | solution.py:551
  166.5 4.2 %collective-permute-start.5 = (bf16[48,1024]{1,0:T(8,128)(2,1)S(1)}, bf16[48,1024]{1,0:T(8,128)(2,1)S(1)}, u32[]{:S(2)}, u32[]{:S(2)}) collective-permute-start(bf16[48,1024]{1,0:T(8,128)(2,1)S(1)} %get-tuple-element.37), channel_id=1, source_target_pairs={{0,16},{16,0},{32,48},{48,32},{1,17},{17,1},{33,49},{49,33},{2,18}... | collective-permute-start | bytes 294920 | tf_op jit(solution)/shard_map/ppermute | solution.py:551
